TPU v7x, 128 devices: a whole 4x4x4 slice. The times are simulated.
128 devices in a mesh: row: 64 (over z, y, x_hi, core), blk: 2 (over x_lo).
Axes of the slice: x: 4 (x_hi: 2, x_lo: 2; x = x_hi * 2 + x_lo), y: 4, z: 4, core: 2. Of those that a mesh axis runs over, the one named last changes fastest.
Arguments:
- field: bfloat16 [2, 256, 1024, 1024], P(None, 'blk', 'row'), may hold values from -400 to 400
- gain: float32 [256], P('blk'), may hold values from 0.1 to 1.9
- w_first: bfloat16 [2, 8, 32, 32], replicated, may hold values from -1 to 1
- b_first: float32 [2, 256], replicated, may hold values from -4 to 4
- w_second: bfloat16 [2, 8, 32, 32], replicated, may hold values from -1 to 1
- b_second: float32 [2, 256], replicated, may hold values from -4 to 4
Outputs:
- mixed: bfloat16 [2, 256, 1024, 1024], P(None, 'blk', 'row')
All inputs are finite; a program needn't handle non-finite values.
Results may differ from a plain program's by a relative error of at most 0.02.
Values may be sent and summed in bfloat16 or wider, within the bound.
No kernel may reach another device: no remote copies, remote signals or barrier semaphores. Data moves between devices by JAX's collectives and lax.ppermute only.
A program may use at most 128 MiB of HBM per device.

v0:
```python
import functools
import math

import jax
import jax.numpy as jnp
import ml_dtypes
import numpy as np
from jax import lax
from jax.experimental import pallas as pl
from jax.experimental.pallas import tpu as pltpu
from jax.sharding import PartitionSpec as P

BLOCK_CH = 32
EPS = 1e-05
SHRINK = 0.01
LANES = 128
BF16 = jnp.bfloat16
F32 = jnp.float32
MIB = 1 << 20


def _angles(first, second, count):
    phase = np.mod(np.outer(first, second), count)
    return phase.astype(np.float32) * np.float32(2.0 * math.pi / count)


def _bf16(values):
    return np.asarray(values, np.float32).astype(ml_dtypes.bfloat16)


def forward_table(count, modes):
    t = _angles(np.arange(count), np.arange(modes), count)
    scale = np.float32(1.0 / math.sqrt(count))
    return _bf16(np.concatenate([np.cos(t) * scale, -np.sin(t) * scale], axis=1))


def inverse_table(count, modes):
    t = _angles(np.arange(modes), np.arange(count), count)
    weight = np.where(np.arange(modes) == 0, 1.0, 2.0)[:, None].astype(np.float32)
    weight = weight * np.float32(1.0 / math.sqrt(count))
    return _bf16(np.concatenate([np.cos(t) * weight, -np.sin(t) * weight], axis=0))


def height_tables(height):
    modes = height // 2
    s = _angles(np.arange(modes) - modes // 2, np.arange(height), height)
    scale = np.float32(1.0 / math.sqrt(height))
    cosine, sine = np.cos(s) * scale, np.sin(s) * scale
    return _bf16(np.concatenate([cosine, sine], axis=0)), _bf16(
        np.concatenate([cosine.T, sine.T], axis=1)
    )


def stats_kernel(x_ref, out_ref):
    channels = x_ref.shape[1]
    zero = jnp.zeros(x_ref.shape[2:], F32)

    def add(c, total):
        return total + x_ref[0, c].astype(F32)

    mean = lax.fori_loop(0, channels, add, zero, unroll=16) * (1.0 / channels)

    def add_square(c, total):
        centered = x_ref[0, c].astype(F32) - mean
        return total + centered * centered

    moment = lax.fori_loop(0, channels, add_square, zero, unroll=16)
    high = mean.astype(BF16)
    out_ref[0] = high
    out_ref[1] = (mean - high.astype(F32)).astype(BF16)
    out_ref[2] = moment.astype(BF16)


def channel_stats(field, which):
    _, channels, rows, width = field.shape
    wide = min(256, width)
    return pl.pallas_call(
        stats_kernel,
        grid=(width // wide,),
        in_specs=[pl.BlockSpec((1, channels, rows, wide), lambda j: (which, 0, 0, j))],
        out_specs=pl.BlockSpec((3, rows, wide), lambda j: (0, 0, j)),
        out_shape=jax.ShapeDtypeStruct((3, rows, width), BF16),
        compiler_params=pltpu.CompilerParams(vmem_limit_bytes=16 * MIB),
        cost_estimate=pl.CostEstimate(
            flops=5 * channels * rows * width, bytes_accessed=2 * channels * rows * width, transcendentals=0
        ),
        name="channel_stats",
    )(field)


def forward_kernel(chan_block, gain_ref, x_ref, own_ref, other_ref, table_ref, eye_ref, *rest):
    send_ref, mean_s, scale_s, spec_s, turn_s = rest[-5:]
    step = pl.program_id(0)
    rows = x_ref.shape[2]
    channels = spec_s.shape[1] // rows
    two_k = table_ref.shape[1]
    half = spec_s.shape[2]
    parts = spec_s.shape[0]

    @pl.when(step == 0)
    def _():
        own_mean = own_ref[0].astype(F32) + own_ref[1].astype(F32)
        other_mean = other_ref[0].astype(F32) + other_ref[1].astype(F32)
        delta = own_mean - other_mean
        total = 2.0 * channels
        moment = own_ref[2].astype(F32) + other_ref[2].astype(F32) + delta * delta * (channels * 0.5)
        mean_s[...] = (own_mean + other_mean) * 0.5
        scale_s[...] = lax.rsqrt(moment * (1.0 / total) + EPS)

    mean = mean_s[...][None]
    scale = scale_s[...][None]
    normed = ((x_ref[0].astype(F32) - mean) * scale).astype(BF16)
    spec = jnp.dot(normed.reshape(chan_block * rows, -1), table_ref[...], preferred_element_type=F32)
    for c in range(chan_block):
        scaled = spec[c * rows : (c + 1) * rows] * gain_ref[step * chan_block + c]
        start = pl.multiple_of(step * (chan_block * rows), chan_block * rows) + c * rows
        for p in range(parts):
            spec_s[p, pl.ds(start, rows), :] = scaled[:, p * half : (p + 1) * half]

    @pl.when(step == pl.num_programs(0) - 1)
    def _():
        per_part = half
        for h in range(rows):
            for p in range(parts):
                picked = spec_s[p, pl.ds(h, channels, stride=rows), :].astype(BF16)
                turned = lax.dot_general(
                    eye_ref[...], picked, (((1,), (1,)), ((), ())), preferred_element_type=F32
                )
                turn_s[pl.ds(p * per_part * rows + h, per_part, stride=rows), :] = turned
        owners = send_ref.shape[1]
        lanes = turn_s.shape[1]
        for r in range(2):
            chunk = turn_s[r * (two_k // 2) * rows : (r + 1) * (two_k // 2) * rows, :]
            chunk = chunk.astype(BF16).reshape(owners, 2, rows, lanes)
            for kk in range(2):
                send_ref[0, :, r * rows : (r + 1) * rows, kk * lanes : (kk + 1) * lanes] = chunk[:, kk]


def forward_slice(field, which, gain, own, other, table, eye, owners, send):
    slices, channels, rows, width = field.shape
    two_k = table.shape[1]
    half = eye.shape[0]
    chan_block = min(32, channels)
    aliased = [] if send is None else [send]
    return pl.pallas_call(
        functools.partial(forward_kernel, chan_block),
        grid=(channels // chan_block,),
        in_specs=[
            pl.BlockSpec(memory_space=pltpu.SMEM),
            pl.BlockSpec((1, chan_block, rows, width), lambda i: (which, i, 0, 0)),
            pl.BlockSpec((3, rows, width), lambda i: (0, 0, 0)),
            pl.BlockSpec((3, rows, width), lambda i: (0, 0, 0)),
            pl.BlockSpec((width, two_k), lambda i: (0, 0)),
            pl.BlockSpec((half, half), lambda i: (0, 0)),
        ]
        + [pl.BlockSpec(memory_space=pl.ANY) for _ in aliased],
        out_specs=pl.BlockSpec((1, owners, 2 * rows, 2 * channels), lambda i: (which, 0, 0, 0)),
        out_shape=jax.ShapeDtypeStruct((slices, owners, 2 * rows, 2 * channels), BF16),
        scratch_shapes=[
            pltpu.VMEM((rows, width), F32),
            pltpu.VMEM((rows, width), F32),
            pltpu.VMEM((two_k // half, channels * rows, half), F32),
            pltpu.VMEM((two_k * rows, channels), F32),
        ],
        input_output_aliases={6: 0} if aliased else {},
        compiler_params=pltpu.CompilerParams(vmem_limit_bytes=24 * MIB),
        cost_estimate=pl.CostEstimate(
            flops=2 * channels * rows * width * two_k,
            bytes_accessed=2 * channels * rows * width,
            transcendentals=0,
        ),
        name="norm_and_row_dft",
    )(gain, field, own, other, table, eye, *aliased)


def block_diagonal(weights, spread, lanes):
    tiled = jnp.dot(weights, spread, preferred_element_type=F32)
    row = lax.broadcasted_iota(jnp.int32, (lanes, lanes), 0) // BLOCK_CH
    col = lax.broadcasted_iota(jnp.int32, (lanes, lanes), 1) // BLOCK_CH
    return jnp.where(row == col, tiled, 0.0)


def fill_weights(w_ref, spread, big, lanes):
    big[...] = jnp.zeros(big.shape, big.dtype)
    real = block_diagonal(w_ref[0], spread, lanes)
    imag = block_diagonal(w_ref[1], spread, lanes)
    for kk in range(2):
        for part_in in range(2):
            for part_out in range(2):
                if part_in == part_out:
                    block = real
                else:
                    block = imag if part_in == 0 else -imag
                row = (part_in * 2 + kk) * lanes
                col = (part_out * 2 + kk) * lanes
                big[row : row + lanes, col : col + lanes] = block.astype(big.dtype)


def bias_row(b_ref):
    parts = [b_ref[0, 0:1], b_ref[0, 0:1], b_ref[0, 1:2], b_ref[0, 1:2]]
    return jnp.concatenate(parts, axis=1)


def filter_kernel(x_ref, fwd_ref, inv_ref, spread_ref, w1_ref, b1_ref, w2_ref, b2_ref, out_ref, big1, big2, turned):
    owners, two_rows, wide = x_ref.shape[1:]
    rows = two_rows // 2
    lanes = wide // 2
    height = owners * rows
    modes = height // 2
    fill_weights(w1_ref, spread_ref[...], big1, lanes)
    fill_weights(w2_ref, spread_ref[...], big2, lanes)

    real_in = x_ref[0, :, :rows, :].reshape(height, wide)
    imag_in = x_ref[0, :, rows:, :].reshape(height, wide)
    from_real = jnp.dot(fwd_ref[...], real_in, preferred_element_type=F32)
    from_imag = jnp.dot(fwd_ref[...], imag_in, preferred_element_type=F32)
    real = (from_real[:modes] + from_imag[modes:]).astype(BF16)
    imag = (from_imag[:modes] - from_real[modes:]).astype(BF16)
    spectrum = jnp.concatenate([real, imag], axis=1)
    hidden = jnp.dot(spectrum, big1[...], preferred_element_type=F32) + bias_row(b1_ref)
    hidden = jnp.maximum(hidden, 0.0).astype(BF16)
    mixed = jnp.dot(hidden, big2[...], preferred_element_type=F32) + bias_row(b2_ref)
    kept = (mixed - jnp.clip(mixed, -SHRINK, SHRINK)).astype(BF16)
    turned[:modes, :] = kept
    turned[modes:, :wide] = -kept[:, wide:]
    turned[modes:, wide:] = kept[:, :wide]
    column = jnp.dot(inv_ref[...], turned[...], preferred_element_type=F32).astype(BF16)
    out_ref[0, :, :rows, :] = column[:, :wide].reshape(owners, rows, wide)
    out_ref[0, :, rows:, :] = column[:, wide:].reshape(owners, rows, wide)


def filter_columns(received, fwd, inv, spread, w_first, b_first, w_second, b_second):
    groups, owners, two_rows, wide = received.shape
    lanes = wide // 2
    height = owners * two_rows // 2
    whole = lambda a: (0, 0)
    weights = pl.BlockSpec((2, lanes, BLOCK_CH), lambda a: (0, a, 0))
    bias = pl.BlockSpec((1, 2, lanes), lambda a: (a, 0, 0))
    block = pl.BlockSpec((1, owners, two_rows, wide), lambda a: (a, 0, 0, 0))

    def flat(w):
        return w.reshape(2, -1, BLOCK_CH)

    def grouped(b):
        return jnp.swapaxes(b.reshape(2, groups, lanes), 0, 1)

    return pl.pallas_call(
        filter_kernel,
        grid=(groups,),
        in_specs=[
            block,
            pl.BlockSpec(fwd.shape, whole),
            pl.BlockSpec(inv.shape, whole),
            pl.BlockSpec(spread.shape, whole),
            weights,
            bias,
            weights,
            bias,
        ],
        out_specs=block,
        out_shape=jax.ShapeDtypeStruct(received.shape, BF16),
        scratch_shapes=[
            pltpu.VMEM((2 * wide, 2 * wide), BF16),
            pltpu.VMEM((2 * wide, 2 * wide), BF16),
            pltpu.VMEM((height, 2 * wide), BF16),
        ],
        compiler_params=pltpu.CompilerParams(vmem_limit_bytes=40 * MIB),
        cost_estimate=pl.CostEstimate(
            flops=2 * groups * height * wide * 5 * height, bytes_accessed=8 * MIB, transcendentals=0
        ),
        name="column_filter",
    )(received, fwd, inv, spread, flat(w_first), grouped(b_first), flat(w_second), grouped(b_second))


def inverse_kernel(chan_block, x_ref, table_ref, eye_ref, out_ref, turn_s, spec_s):
    owners, two_rows, wide = x_ref.shape[1:]
    rows = two_rows // 2
    lanes = wide // 2
    channels = spec_s.shape[1] // rows
    parts, _, half = spec_s.shape
    step = pl.program_id(1)

    @pl.when(step == 0)
    def _():
        for r in range(2):
            pair = [
                x_ref[0, :, r * rows : (r + 1) * rows, kk * lanes : (kk + 1) * lanes][:, None]
                for kk in range(2)
            ]
            block = jnp.concatenate(pair, axis=1).astype(F32)
            size = owners * 2 * rows
            turn_s[r * size : (r + 1) * size, :] = block.reshape(size, lanes)
        for h in range(rows):
            for p in range(parts):
                picked = turn_s[pl.ds(p * half * rows + h, half, stride=rows), :].astype(BF16)
                turned = lax.dot_general(
                    eye_ref[...], picked, (((1,), (1,)), ((), ())), preferred_element_type=F32
                )
                spec_s[p, pl.ds(h, channels, stride=rows), :] = turned

    size = chan_block * rows
    start = pl.multiple_of(step * size, size)
    spec = jnp.concatenate([spec_s[p, pl.ds(start, size), :].astype(BF16) for p in range(parts)], axis=1)
    mixed = jnp.dot(spec, table_ref[...], preferred_element_type=F32)
    out_ref[0] = mixed.astype(BF16).reshape(chan_block, rows, -1)


def inverse_rows(received, table, eye):
    slices, owners, two_rows, wide = received.shape
    rows = two_rows // 2
    channels = wide // 2
    two_k, width = table.shape
    half = two_k // 2
    chan_block = min(32, channels)
    return pl.pallas_call(
        functools.partial(inverse_kernel, chan_block),
        grid=(slices, channels // chan_block),
        in_specs=[
            pl.BlockSpec((1, owners, two_rows, wide), lambda b, i: (b, 0, 0, 0)),
            pl.BlockSpec(table.shape, lambda b, i: (0, 0)),
            pl.BlockSpec(eye.shape, lambda b, i: (0, 0)),
        ],
        out_specs=pl.BlockSpec((1, chan_block, rows, width), lambda b, i: (b, i, 0, 0)),
        out_shape=jax.ShapeDtypeStruct((slices, channels, rows, width), BF16),
        scratch_shapes=[
            pltpu.VMEM((two_k * rows, channels), F32),
            pltpu.VMEM((2, channels * rows, half), F32),
        ],
        compiler_params=pltpu.CompilerParams(vmem_limit_bytes=24 * MIB),
        cost_estimate=pl.CostEstimate(
            flops=2 * slices * channels * rows * width * two_k,
            bytes_accessed=2 * slices * channels * rows * width,
            transcendentals=0,
        ),
        name="inverse_row_dft",
    )(received, table, eye)


def exchange(blocks):
    shape = blocks.shape
    flat = blocks.reshape((shape[0] * shape[1],) + shape[2:])
    flat = lax.all_to_all(flat, ("blk", "row"), split_axis=0, concat_axis=0, tiled=True)
    return flat.reshape(shape)


def local(field, gain, w_first, b_first, w_second, b_second):
    slices, channels, rows, width = field.shape
    owners = lax.axis_size("row")
    modes_x = 2 * owners
    height = owners * rows
    fwd, inv = height_tables(height)
    eye_k = jnp.asarray(np.eye(modes_x), BF16)
    eye_c = jnp.asarray(np.eye(channels), BF16)
    spread = jnp.asarray(np.tile(np.eye(BLOCK_CH), (1, channels // BLOCK_CH)), BF16)
    table = jnp.asarray(forward_table(width, modes_x))

    swap = [(0, 1), (1, 0)]
    own = [channel_stats(field, b) for b in range(slices)]
    other = [lax.ppermute(s, "blk", swap) for s in own]
    send = None
    for b in range(slices):
        send = forward_slice(field, b, gain, own[b], other[b], table, eye_k, owners, send)
    columns = exchange(send)
    filtered = filter_columns(
        columns, jnp.asarray(fwd), jnp.asarray(inv), spread, w_first, b_first, w_second, b_second
    )
    colfield = exchange(filtered)
    return inverse_rows(colfield, jnp.asarray(inverse_table(width, modes_x)), eye_c)


def solution(mesh):
    return jax.shard_map(
        local,
        mesh=mesh,
        in_specs=(P(None, "blk", "row", None), P("blk"), P(), P(), P(), P()),
        out_specs=P(None, "blk", "row", None),
        check_vma=False,
    )
```

profile of v0, /device:TPU:1, one launch (start us, length us, event | category | flops | bytes accessed | tf_op | source)
XLA Modules:
  0.0 113.6 jit_solution(18117788565984555323)
XLA Ops:
  0.0 3.4 %copy-done = bf16[2,128,16,1024]{3,2,1,0:T(8,128)(2,1)S(1)} copy-done((bf16[2,128,16,1024]{3,2,1,0:T(8,128)(2,1)S(1)}, bf16[2,128,16,1024]{3,2,1,0:T(8,128)(2,1)}, u32[]{:S(2)}) %copy-start) | copy-done | bytes 8388632
  3.4 2.5 %channel_stats.3.own_ref = bf16[3,16,1024]{2,1,0:T(8,128)(2,1)S(1)} custom-call(bf16[2,128,16,1024]{3,2,1,0:T(8,128)(2,1)S(1)} %copy-done), custom_call_target="tpu_custom_call" | custom-call | flops 10485760 | bytes 4194304 | tf_op jit(solution)/shard_map/channel_stats/pallas_call | solution.py:77
  5.9 0.0 slice-start.1
  5.9 0.0 copy-start.1
  5.9 0.0 copy-start.3
  6.0 0.0 copy-start.4
  6.0 2.1 %collective-permute-start.1 = (bf16[3,16,1024]{2,1,0:T(8,128)(2,1)S(1)}, bf16[3,16,1024]{2,1,0:T(8,128)(2,1)S(1)}, u32[]{:S(2)}, u32[]{:S(2)}) collective-permute-start(bf16[3,16,1024]{2,1,0:T(8,128)(2,1)S(1)} %channel_stats.3.own_ref), channel_id=1, source_target_pairs={{0,1},{1,0},{2,3},{3,2},{4,5},{5,4},{6,7},{7,6},{8,9},{9,8},{10,11... | collective-permute-start | bytes 294920 | tf_op jit(solution)/shard_map/ppermute | solution.py:359
  8.1 2.5 %channel_stats.2.own_ref = bf16[3,16,1024]{2,1,0:T(8,128)(2,1)S(1)} custom-call(bf16[2,128,16,1024]{3,2,1,0:T(8,128)(2,1)S(1)} %copy-done), custom_call_target="tpu_custom_call" | custom-call | flops 10485760 | bytes 4194304 | tf_op jit(solution)/shard_map/channel_stats/pallas_call | solution.py:77
  10.6 0.1 collective-permute-start
  10.7 0.0 collective-permute-done.1.other_ref
  10.8 4.4 %norm_and_row_dft.2.rest_0_ = bf16[2,64,32,256]{3,2,1,0:T(8,128)(2,1)S(1)} custom-call(f32[128]{0:T(128)S(1)} %copy-done.4, bf16[2,128,16,1024]{3,2,1,0:T(8,128)(2,1)S(1)} %bitcast.13, bf16[3,16,1024]{2,1,0:T(8,128)(2,1)S(1)} %channel_stats.3.own_ref, bf16[3,16,1024]{2,1,0:T(8,128)(2,1)S(1)} %collective-permute-done.1.other_ref, ...), custom_call_target="tpu_custom_call" | custom-call | flops 1073741824 | bytes 4194304 | tf_op jit(solution)/shard_map/norm_and_row_dft/pallas_call | solution.py:145
  15.2 0.0 copy-start.10
  15.2 4.4 %norm_and_row_dft.3 = bf16[2,64,32,256]{3,2,1,0:T(8,128)(2,1)S(1)} custom-call(f32[128]{0:T(128)S(1)} %copy-done.4, bf16[2,128,16,1024]{3,2,1,0:T(8,128)(2,1)S(1)} %bitcast.13, bf16[3,16,1024]{2,1,0:T(8,128)(2,1)S(1)} %channel_stats.2.own_ref, bf16[3,16,1024]{2,1,0:T(8,128)(2,1)S(1)} %collective-permute-done.other_ref, ...), custom_call_target="tpu_custom_call", output_to_operand_aliasing={{}: (6, {})} | custom-call | flops 1073741824 | bytes 4194304 | tf_op jit(solution)/shard_map/norm_and_row_dft/pallas_call | solution.py:145
  19.6 0.0 copy-start.5
  19.6 0.0 copy-start.6
  19.6 0.0 copy-start.7
  19.6 0.0 copy-start.8
  19.7 0.0 copy-start.9
  19.7 0.0 copy-start.11
  19.7 41.5 %all_to_all.10 = bf16[128,32,256]{2,1,0:T(8,128)(2,1)S(1)} all-to-all(bf16[128,32,256]{2,1,0:T(8,128)(2,1)S(1)} %bitcast.14), channel_id=1, replica_groups=mesh['row'=64,'blk'=2] {'blk','row'}, dimensions={0} | all-to-all | bytes 4194304 | tf_op jit(solution)/shard_map/all_to_all | solution.py:342
  61.2 8.2 %column_filter.1 = bf16[2,64,32,256]{3,2,1,0:T(8,128)(2,1)S(1)} custom-call(bf16[2,64,32,256]{3,2,1,0:T(8,128)(2,1)S(1)} %bitcast.16, bf16[1024,1024]{1,0:T(8,128)(2,1)S(1)} %copy-done.10, bf16[1024,1024]{1,0:T(8,128)(2,1)S(1)} %copy-done.9, bf16[32,128]{1,0:T(8,128)(2,1)S(1)} %copy-done.11, bf16[2,256,32]{2,1,0:T(8,128)(2,1)S(1)} %bitcast.18, ...), custom_call_target="tpu_custom_call" | custom-call | flops 5368709120 | bytes 8388608 | tf_op jit(solution)/shard_map/column_filter/pallas_call | solution.py:247
  69.4 0.0 copy-start.2
  69.4 34.4 %all_to_all.11 = bf16[128,32,256]{2,1,0:T(8,128)(2,1)S(1)} all-to-all(bf16[128,32,256]{2,1,0:T(8,128)(2,1)S(1)} %bitcast.17), channel_id=1, replica_groups=mesh['row'=64,'blk'=2] {'blk','row'}, dimensions={0} | all-to-all | bytes 4194304 | tf_op jit(solution)/shard_map/all_to_all | solution.py:342
  103.8 9.8 %inverse_row_dft.1 = bf16[2,128,16,1024]{3,2,1,0:T(8,128)(2,1)} custom-call(bf16[2,64,32,256]{3,2,1,0:T(8,128)(2,1)S(1)} %bitcast.15, bf16[256,1024]{1,0:T(8,128)(2,1)S(1)} %copy-done.2, bf16[128,128]{1,0:T(8,128)(2,1)S(1)} %copy-done.3), custom_call_target="tpu_custom_call" | custom-call | flops 2147483648 | bytes 8388608 | tf_op jit(solution)/shard_map/inverse_row_dft/pallas_call | solution.py:315
  (17 shorter events, 0.0 us)
Async XLA Ops:
  0.0 3.4 %copy-start = (bf16[2,128,16,1024]{3,2,1,0:T(8,128)(2,1)S(1)}, bf16[2,128,16,1024]{3,2,1,0:T(8,128)(2,1)}, u32[]{:S(2)}) copy-start(bf16[2,128,16,1024]{3,2,1,0:T(8,128)(2,1)} %x_ref.7) | copy-start | bytes 25165828
  3.4 7.3 %slice-start = ((s8[8388608]{0:T(1024)(128)(4,1)}), s8[4194304]{0:T(1024)(128)(4,1)S(1)}, s32[]{:S(2)}) async-start(s8[8388608]{0:T(1024)(128)(4,1)} %bitcast.12), calls=%async_computation.2 | async-start | bytes 8388608
  5.9 4.8 %slice-start.1 = ((s8[8388608]{0:T(1024)(128)(4,1)}), s8[4194304]{0:T(1024)(128)(4,1)S(1)}, s32[]{:S(2)}) async-start(s8[8388608]{0:T(1024)(128)(4,1)} %bitcast.12), calls=%async_computation.3 | async-start | bytes 8388608
  5.9 4.8 %copy-start.1 = (bf16[1024,256]{1,0:T(8,128)(2,1)S(1)}, bf16[1024,256]{1,0:T(8,128)(2,1)}, u32[]{:S(2)}) copy-start(bf16[1024,256]{1,0:T(8,128)(2,1)} %constant.14.clone.table_ref) | copy-start | bytes 1572868
  5.9 4.8 %copy-start.3 = (bf16[128,128]{1,0:T(8,128)(2,1)S(1)}, bf16[128,128]{1,0:T(8,128)(2,1)}, u32[]{:S(2)}) copy-start(bf16[128,128]{1,0:T(8,128)(2,1)} %constant.12.clone.eye_ref) | copy-start | bytes 98308
  6.0 4.8 %copy-start.4 = (f32[128]{0:T(128)S(1)}, f32[128]{0:T(128)}, u32[]{:S(2)}) copy-start(f32[128]{0:T(128)} %gain_ref.3) | copy-start | bytes 1540
  6.0 4.8 %collective-permute-start.1 = (bf16[3,16,1024]{2,1,0:T(8,128)(2,1)S(1)}, bf16[3,16,1024]{2,1,0:T(8,128)(2,1)S(1)}, u32[]{:S(2)}, u32[]{:S(2)}) collective-permute-start(bf16[3,16,1024]{2,1,0:T(8,128)(2,1)S(1)} %channel_stats.3.own_ref), channel_id=1, source_target_pairs={{0,1},{1,0},{2,3},{3,2},{4,5},{5,4},{6,7},{7,6},{8,9},{9,8},{10,11... | collective-permute-start | bytes 294920 | tf_op jit(solution)/shard_map/ppermute | solution.py:359
  10.6 4.6 %collective-permute-start = (bf16[3,16,1024]{2,1,0:T(8,128)(2,1)S(1)}, bf16[3,16,1024]{2,1,0:T(8,128)(2,1)S(1)}, u32[]{:S(2)}, u32[]{:S(2)}) collective-permute-start(bf16[3,16,1024]{2,1,0:T(8,128)(2,1)S(1)} %channel_stats.2.own_ref), channel_id=1, source_target_pairs={{0,1},{1,0},{2,3},{3,2},{4,5},{5,4},{6,7},{7,6},{8,9},{9,8},{10,11... | collective-permute-start | bytes 294920 | tf_op jit(solution)/shard_map/ppermute | solution.py:359
  15.2 46.0 %copy-start.10 = (bf16[1024,1024]{1,0:T(8,128)(2,1)S(1)}, bf16[1024,1024]{1,0:T(8,128)(2,1)}, u32[]{:S(2)}) copy-start(bf16[1024,1024]{1,0:T(8,128)(2,1)} %constant.15.clone.fwd_ref) | copy-start | bytes 6291460
  19.6 41.5 %copy-start.5 = (bf16[2,8,32,32]{3,2,1,0:T(8,128)(2,1)S(1)}, bf16[2,8,32,32]{3,2,1,0:T(8,128)(2,1)}, u32[]{:S(2)}) copy-start(bf16[2,8,32,32]{3,2,1,0:T(8,128)(2,1)} %param.15) | copy-start | bytes 98308
  19.6 41.5 %copy-start.6 = (bf16[2,8,32,32]{3,2,1,0:T(8,128)(2,1)S(1)}, bf16[2,8,32,32]{3,2,1,0:T(8,128)(2,1)}, u32[]{:S(2)}) copy-start(bf16[2,8,32,32]{3,2,1,0:T(8,128)(2,1)} %param.17) | copy-start | bytes 98308
  19.6 41.5 %copy-start.7 = (f32[2,256]{1,0:T(2,128)S(1)}, f32[2,256]{1,0:T(2,128)}, u32[]{:S(2)}) copy-start(f32[2,256]{1,0:T(2,128)} %param.16) | copy-start | bytes 6148
  19.6 41.5 %copy-start.8 = (f32[2,256]{1,0:T(2,128)S(1)}, f32[2,256]{1,0:T(2,128)}, u32[]{:S(2)}) copy-start(f32[2,256]{1,0:T(2,128)} %param.18) | copy-start | bytes 6148
  19.7 41.5 %copy-start.9 = (bf16[1024,1024]{1,0:T(8,128)(2,1)S(1)}, bf16[1024,1024]{1,0:T(8,128)(2,1)}, u32[]{:S(2)}) copy-start(bf16[1024,1024]{1,0:T(8,128)(2,1)} %constant.16.clone.inv_ref) | copy-start | bytes 6291460
  19.7 41.5 %copy-start.11 = (bf16[32,128]{1,0:T(8,128)(2,1)S(1)}, bf16[32,128]{1,0:T(8,128)(2,1)}, u32[]{:S(2)}) copy-start(bf16[32,128]{1,0:T(8,128)(2,1)} %constant.13.clone.spread_ref) | copy-start | bytes 24580
  69.4 34.4 %copy-start.2 = (bf16[256,1024]{1,0:T(8,128)(2,1)S(1)}, bf16[256,1024]{1,0:T(8,128)(2,1)}, u32[]{:S(2)}) copy-start(bf16[256,1024]{1,0:T(8,128)(2,1)} %constant.17.clone.table_ref) | copy-start | bytes 1572868
where the time goes:
time: 114 us
  blocking collectives  75.9 us (67%)
  Pallas kernels  31.8 us (28%)
  local copies, waits for them, and re-layouts  3.47 us (3%)
  starting transfers between devices  2.23 us (2%)
    all_to_all x2, blocking collectives, exchange(): lax.all_to_all(flat, ('blk', 'row'), split_axis=0, concat_axis=0, tiled=T...  75.9 us
    pallas_call x1, Pallas kernels, inverse_rows(): pl.pallas_call(functools.partial(inverse_kernel, chan_block), grid=(slice...  9.84 us
    pallas_call x2, Pallas kernels, forward_slice(): pl.pallas_call(functools.partial(forward_kernel, chan_block), grid=(chann...  8.8 us
    pallas_call x1, Pallas kernels, filter_columns(): pl.pallas_call(filter_kernel, grid=(groups,), in_specs=[block, pl.BlockSp...  8.17 us
    pallas_call x2, Pallas kernels, channel_stats(): pl.pallas_call(stats_kernel, grid=(width // wide,), in_specs=[pl.BlockSpe...  5.04 us
    unnamed x28, local copies, waits for them, and re-layouts  3.47 us
  transfers between devices with their start and end apart: 2, of which 0 were waited for; matrix products, arithmetic and copies ran while one was open for 0% of the time, Pallas kernels for 6%

commit v1 on v0

v1 whole, which is shorter than its diff:
```python
import functools
import math

import jax
import jax.numpy as jnp
import ml_dtypes
import numpy as np
from jax import lax
from jax.experimental import pallas as pl
from jax.experimental.pallas import tpu as pltpu
from jax.sharding import PartitionSpec as P

BLOCK_CH = 32
EPS = 1e-05
SHRINK = 0.01
LANES = 128
BF16 = jnp.bfloat16
F32 = jnp.float32
MIB = 1 << 20


def _angles(first, second, count):
    phase = np.mod(np.outer(first, second), count)
    return phase.astype(np.float32) * np.float32(2.0 * math.pi / count)


def _bf16(values):
    return np.asarray(values, np.float32).astype(ml_dtypes.bfloat16)


def mode_order(modes):
    return np.arange(modes).reshape(-1, 2).T.reshape(-1)


def forward_table(count, modes):
    t = _angles(np.arange(count), mode_order(modes), count)
    scale = np.float32(1.0 / math.sqrt(count))
    return _bf16(np.concatenate([np.cos(t) * scale, -np.sin(t) * scale], axis=1))


def inverse_table(count, modes):
    order = mode_order(modes)
    t = _angles(order, np.arange(count), count)
    weight = np.where(order == 0, 1.0, 2.0)[:, None].astype(np.float32)
    weight = weight * np.float32(1.0 / math.sqrt(count))
    return _bf16(np.concatenate([np.cos(t) * weight, -np.sin(t) * weight], axis=0))


def height_tables(height):
    quarter = height // 4
    s = _angles(np.arange(quarter + 1), np.arange(height), height)
    scale = np.float32(1.0 / math.sqrt(height))
    cosine, sine = np.cos(s) * scale, np.sin(s) * scale
    last = np.zeros((16, height), np.float32)
    last[0], last[1] = cosine[quarter], sine[quarter]
    forward = np.concatenate([cosine[:quarter], sine[:quarter], last], axis=0)
    inverse = np.concatenate([cosine[:quarter].T, sine[:quarter].T], axis=1)
    return _bf16(forward), _bf16(inverse)


def stats_kernel(x_ref, out_ref):
    channels = x_ref.shape[1]
    zero = jnp.zeros(x_ref.shape[2:], F32)

    def add(c, total):
        return total + x_ref[0, c].astype(F32)

    mean = lax.fori_loop(0, channels, add, zero, unroll=16) * (1.0 / channels)

    def add_square(c, total):
        centered = x_ref[0, c].astype(F32) - mean
        return total + centered * centered

    moment = lax.fori_loop(0, channels, add_square, zero, unroll=16)
    high = mean.astype(BF16)
    out_ref[0] = high
    out_ref[1] = (mean - high.astype(F32)).astype(BF16)
    out_ref[2] = moment.astype(BF16)


def channel_stats(field, which):
    _, channels, rows, width = field.shape
    wide = min(256, width)
    return pl.pallas_call(
        stats_kernel,
        grid=(width // wide,),
        in_specs=[pl.BlockSpec((1, channels, rows, wide), lambda j: (which, 0, 0, j))],
        out_specs=pl.BlockSpec((3, rows, wide), lambda j: (0, 0, j)),
        out_shape=jax.ShapeDtypeStruct((3, rows, width), BF16),
        compiler_params=pltpu.CompilerParams(vmem_limit_bytes=16 * MIB),
        cost_estimate=pl.CostEstimate(
            flops=5 * channels * rows * width, bytes_accessed=2 * channels * rows * width, transcendentals=0
        ),
        name="channel_stats",
    )(pltpu.with_memory_space_constraint(field, pltpu.HBM))


def forward_kernel(which, pitch, x_ref, gain_ref, own_ref, other_ref, table_ref, *rest):
    send_ref, mean_s, scale_s, spec_s, turn_s = rest[-5:]
    step = pl.program_id(0)
    chan_block, rows, width = x_ref.shape[1:]
    parts, _, half = spec_s.shape
    channels = turn_s.shape[-1]
    owners = send_ref.shape[1]

    @pl.when(step == 0)
    def _():
        own_mean = own_ref[0].astype(F32) + own_ref[1].astype(F32)
        other_mean = other_ref[0].astype(F32) + other_ref[1].astype(F32)
        delta = own_mean - other_mean
        total = 2.0 * channels
        moment = own_ref[2].astype(F32) + other_ref[2].astype(F32) + delta * delta * (channels * 0.5)
        mean_s[...] = (own_mean + other_mean) * 0.5
        scale_s[...] = lax.rsqrt(moment * (1.0 / total) + EPS)

    normed = ((x_ref[0].astype(F32) - mean_s[...][None]) * scale_s[...][None]).astype(BF16)
    spec = jnp.dot(normed.reshape(chan_block * rows, width), table_ref[...], preferred_element_type=F32)
    for c in range(chan_block):
        start = pl.multiple_of(step * (chan_block * pitch), chan_block * pitch) + c * pitch
        for p in range(parts):
            spec_s[p, pl.ds(start, rows), :] = spec[c * rows : (c + 1) * rows, p * half : (p + 1) * half]

    @pl.when(step == pl.num_programs(0) - 1)
    def _():
        for h in range(rows):
            for p in range(parts):
                turned = spec_s[p, pl.ds(h, channels, stride=pitch), :].T * gain_ref[...]
                turn_s[pl.ds(p * half * pitch + h, half, stride=pitch), :] = turned
        for r in range(2):
            for kk in range(2):
                for d in range(owners):
                    start = ((r * 2 + kk) * owners + d) * pitch
                    send_ref[which, d, r * rows : (r + 1) * rows, kk * channels : (kk + 1) * channels] = turn_s[
                        start : start + rows, :
                    ].astype(BF16)


def forward_slice(field, which, gain, own, other, table, owners, send):
    slices, channels, rows, width = field.shape
    two_k = table.shape[1]
    chan_block = min(32, channels)
    pitch = rows + 8
    aliased = [] if send is None else [send]
    vmem = pl.BlockSpec(memory_space=pltpu.VMEM)
    return pl.pallas_call(
        functools.partial(forward_kernel, which, pitch),
        grid=(channels // chan_block,),
        in_specs=[pl.BlockSpec((1, chan_block, rows, width), lambda i: (which, i, 0, 0))]
        + [vmem] * (4 + len(aliased)),
        out_specs=vmem,
        out_shape=jax.ShapeDtypeStruct((slices, owners, 2 * rows, 2 * channels), BF16),
        scratch_shapes=[
            pltpu.VMEM((rows, width), F32),
            pltpu.VMEM((rows, width), F32),
            pltpu.VMEM((2, channels * pitch, two_k // 2), F32),
            pltpu.VMEM((two_k * pitch, channels), F32),
        ],
        input_output_aliases={5: 0} if aliased else {},
        compiler_params=pltpu.CompilerParams(vmem_limit_bytes=24 * MIB),
        cost_estimate=pl.CostEstimate(
            flops=2 * channels * rows * width * two_k,
            bytes_accessed=2 * channels * rows * width,
            transcendentals=0,
        ),
        name="norm_and_row_dft",
    )(pltpu.with_memory_space_constraint(field, pltpu.HBM), gain.reshape(1, channels), own, other, table, *aliased)


def block_diagonal(weights, spread, lanes):
    tiled = jnp.dot(weights, spread, preferred_element_type=F32)
    row = lax.broadcasted_iota(jnp.int32, (lanes, lanes), 0) // BLOCK_CH
    col = lax.broadcasted_iota(jnp.int32, (lanes, lanes), 1) // BLOCK_CH
    return jnp.where(row == col, tiled, 0.0)


def fill_weights(w_ref, group, spread, big, lanes):
    mine = slice(group * lanes, (group + 1) * lanes)
    real = block_diagonal(w_ref[0, mine, :], spread, lanes)
    imag = block_diagonal(w_ref[1, mine, :], spread, lanes)
    big[:lanes, :lanes] = real.astype(BF16)
    big[:lanes, lanes:] = imag.astype(BF16)
    big[lanes:, :lanes] = (-imag).astype(BF16)
    big[lanes:, lanes:] = real.astype(BF16)


def bias_row(b_ref, group, lanes):
    mine = slice(group * lanes, (group + 1) * lanes)
    return jnp.concatenate([b_ref[0:1, mine], b_ref[1:2, mine]], axis=1)


def filter_kernel(x_ref, fwd_ref, inv_ref, spread_ref, w1_ref, b1_ref, w2_ref, b2_ref, out_ref, big1, big2, packed):
    groups, owners, two_rows, wide = x_ref.shape
    rows = two_rows // 2
    lanes = wide // 2
    height = owners * rows
    quarter = height // 4
    top = lax.broadcasted_iota(jnp.int32, (quarter, lanes), 0) == 0
    turn = lax.broadcasted_iota(jnp.int32, (8, 1), 0) % 4
    norm = 1.0 / math.sqrt(height)
    last_cos = jnp.where(turn == 0, norm, jnp.where(turn == 2, -norm, 0.0))
    last_sin = jnp.where(turn == 1, norm, jnp.where(turn == 3, -norm, 0.0))
    for group in range(groups):
        fill_weights(w1_ref, group, spread_ref[...], big1, lanes)
        fill_weights(w2_ref, group, spread_ref[...], big2, lanes)
        bias1 = bias_row(b1_ref, group, lanes)
        bias2 = bias_row(b2_ref, group, lanes)
        real_in = x_ref[group, :, :rows, :].reshape(height, wide)
        imag_in = x_ref[group, :, rows:, :].reshape(height, wide)
        from_real = jnp.dot(fwd_ref[...], real_in, preferred_element_type=F32)
        from_imag = jnp.dot(fwd_ref[...], imag_in, preferred_element_type=F32)
        extra = []
        for kk in range(2):
            part = slice(kk * lanes, (kk + 1) * lanes)
            cos_re, sin_re = from_real[:quarter, part], from_real[quarter : 2 * quarter, part]
            cos_im, sin_im = from_imag[:quarter, part], from_imag[quarter : 2 * quarter, part]
            last_re = from_real[2 * quarter : 2 * quarter + 1, part] - from_imag[2 * quarter + 1 : 2 * quarter + 2, part]
            last_im = from_imag[2 * quarter : 2 * quarter + 1, part] + from_real[2 * quarter + 1 : 2 * quarter + 2, part]
            plus = jnp.concatenate([cos_re + sin_im, cos_im - sin_re], axis=1)
            minus = jnp.concatenate(
                [jnp.where(top, last_re, cos_re - sin_im), jnp.where(top, last_im, cos_im + sin_re)], axis=1
            )
            spectrum = jnp.concatenate([plus, minus], axis=0).astype(BF16)
            hidden = jnp.dot(spectrum, big1[...], preferred_element_type=F32) + bias1
            hidden = jnp.maximum(hidden, 0.0).astype(BF16)
            mixed = jnp.dot(hidden, big2[...], preferred_element_type=F32) + bias2
            kept = mixed - jnp.clip(mixed, -SHRINK, SHRINK)
            plus_re, plus_im = kept[:quarter, :lanes], kept[:quarter, lanes:]
            minus_re, minus_im = kept[quarter:, :lanes], kept[quarter:, lanes:]
            last_re, last_im = minus_re[0:1], minus_im[0:1]
            minus_re = jnp.where(top, 0.0, minus_re)
            minus_im = jnp.where(top, 0.0, minus_im)
            packed[:quarter, part] = (plus_re + minus_re).astype(BF16)
            packed[:quarter, wide + kk * lanes : wide + (kk + 1) * lanes] = (plus_im + minus_im).astype(BF16)
            packed[quarter:, part] = (minus_im - plus_im).astype(BF16)
            packed[quarter:, wide + kk * lanes : wide + (kk + 1) * lanes] = (plus_re - minus_re).astype(BF16)
            extra.append((last_cos * last_re + last_sin * last_im, last_cos * last_im - last_sin * last_re))
        column = jnp.dot(inv_ref[...], packed[...], preferred_element_type=F32)
        extra = jnp.concatenate([extra[0][0], extra[1][0], extra[0][1], extra[1][1]], axis=1)
        column = (column.reshape(height // 8, 8, 2 * wide) + extra[None]).astype(BF16)
        column = column.reshape(height, 2 * wide)
        out_ref[group, :, :rows, :] = column[:, :wide].reshape(owners, rows, wide)
        out_ref[group, :, rows:, :] = column[:, wide:].reshape(owners, rows, wide)


def filter_columns(received, fwd, inv, spread, w_first, b_first, w_second, b_second):
    groups, owners, two_rows, wide = received.shape
    height = owners * two_rows // 2
    vmem = pl.BlockSpec(memory_space=pltpu.VMEM)

    def flat(w):
        return w.reshape(2, -1, BLOCK_CH)

    return pl.pallas_call(
        filter_kernel,
        in_specs=[vmem] * 8,
        out_specs=vmem,
        out_shape=jax.ShapeDtypeStruct(received.shape, BF16),
        scratch_shapes=[
            pltpu.VMEM((wide, wide), BF16),
            pltpu.VMEM((wide, wide), BF16),
            pltpu.VMEM((height // 2, 2 * wide), BF16),
        ],
        compiler_params=pltpu.CompilerParams(vmem_limit_bytes=40 * MIB),
        cost_estimate=pl.CostEstimate(
            flops=2 * groups * height * wide * 3 * height, bytes_accessed=8 * MIB, transcendentals=0
        ),
        name="column_filter",
    )(received, fwd, inv, spread, flat(w_first), b_first, flat(w_second), b_second)


def inverse_kernel(pitch, x_ref, table_ref, out_ref, turn_s, spec_s):
    owners, two_rows, wide = x_ref.shape[1:]
    rows = two_rows // 2
    channels = wide // 2
    parts, _, half = spec_s.shape
    chan_block = out_ref.shape[1]
    which = pl.program_id(0)
    step = pl.program_id(1)

    @pl.when(step == 0)
    def _():
        for r in range(2):
            for kk in range(2):
                for d in range(owners):
                    start = ((r * 2 + kk) * owners + d) * pitch
                    turn_s[start : start + rows, :] = x_ref[
                        which, d, r * rows : (r + 1) * rows, kk * channels : (kk + 1) * channels
                    ].astype(F32)
        for h in range(rows):
            for p in range(parts):
                turned = turn_s[pl.ds(p * half * pitch + h, half, stride=pitch), :].T
                spec_s[p, pl.ds(h, channels, stride=pitch), :] = turned

    spec = []
    for c in range(chan_block):
        start = pl.multiple_of(step * (chan_block * pitch), chan_block * pitch) + c * pitch
        spec.append(jnp.concatenate([spec_s[p, pl.ds(start, rows), :].astype(BF16) for p in range(parts)], axis=1))
    mixed = jnp.dot(jnp.concatenate(spec, axis=0), table_ref[...], preferred_element_type=F32)
    out_ref[0] = mixed.astype(BF16).reshape(chan_block, rows, -1)


def inverse_rows(received, table):
    slices, owners, two_rows, wide = received.shape
    rows = two_rows // 2
    channels = wide // 2
    two_k, width = table.shape
    chan_block = min(32, channels)
    pitch = rows + 8
    vmem = pl.BlockSpec(memory_space=pltpu.VMEM)
    return pl.pallas_call(
        functools.partial(inverse_kernel, pitch),
        grid=(slices, channels // chan_block),
        in_specs=[vmem, vmem],
        out_specs=pl.BlockSpec((1, chan_block, rows, width), lambda b, i: (b, i, 0, 0)),
        out_shape=jax.ShapeDtypeStruct((slices, channels, rows, width), BF16),
        scratch_shapes=[
            pltpu.VMEM((two_k * pitch, channels), F32),
            pltpu.VMEM((2, channels * pitch, two_k // 2), F32),
        ],
        compiler_params=pltpu.CompilerParams(vmem_limit_bytes=24 * MIB),
        cost_estimate=pl.CostEstimate(
            flops=2 * slices * channels * rows * width * two_k,
            bytes_accessed=2 * slices * channels * rows * width,
            transcendentals=0,
        ),
        name="inverse_row_dft",
    )(received, table)


def exchange(blocks):
    shape = blocks.shape
    flat = blocks.reshape((shape[0] * shape[1],) + shape[2:])
    flat = lax.all_to_all(flat, ("blk", "row"), split_axis=0, concat_axis=0, tiled=True)
    return flat.reshape(shape)


def local(field, gain, w_first, b_first, w_second, b_second):
    slices, channels, rows, width = field.shape
    owners = lax.axis_size("row")
    modes_x = 2 * owners
    height = owners * rows
    fwd, inv = height_tables(height)
    spread = jnp.asarray(np.tile(np.eye(BLOCK_CH), (1, channels // BLOCK_CH)), BF16)
    table = jnp.asarray(forward_table(width, modes_x))

    swap = [(0, 1), (1, 0)]
    own = [channel_stats(field, b) for b in range(slices)]
    other = [lax.ppermute(s, "blk", swap) for s in own]
    send = None
    for b in range(slices):
        send = forward_slice(field, b, gain, own[b], other[b], table, owners, send)
    columns = exchange(send)
    filtered = filter_columns(
        columns, jnp.asarray(fwd), jnp.asarray(inv), spread, w_first, b_first, w_second, b_second
    )
    colfield = exchange(filtered)
    return inverse_rows(colfield, jnp.asarray(inverse_table(width, modes_x)))


def solution(mesh):
    return jax.shard_map(
        local,
        mesh=mesh,
        in_specs=(P(None, "blk", "row", None), P("blk"), P(), P(), P(), P()),
        out_specs=P(None, "blk", "row", None),
        check_vma=False,
    )
```

time: 114 us -> 108 us (0.947)
  local copies, waits for them, and re-layouts: 3.47 us -> 0.07 us
  Pallas kernels: 31.8 us -> 28.8 us
    pallas_call x4, Pallas kernels: 26.8 us -> 20.9 us  [the longest x2 9.52 us: forward_slice(): pl.pallas_call(functools.partial(forward_kernel, which, pitch), grid=(cha...]
    unnamed x28 -> x20, local copies, waits for them, and re-layouts: 3.47 us -> 0.07 us
    pallas_call x2, Pallas kernels: 5.04 us -> 7.96 us  [channel_stats(): pl.pallas_call(stats_kernel, grid=(width // wide,), in_specs=[pl.BlockSpe...]
  transfers between devices with their start and end apart: 2 -> 2, of which waited for: 0 -> 0; matrix products, arithmetic and copies ran while one was open for 0% -> 0% of each run, Pallas kernels for 6% -> 8%
where the time goes in v1:
time: 108 us; the launch traced here: 107 us
  blocking collectives  75.8 us (70%)
  Pallas kernels  28.8 us (27%)
  starting transfers between devices  2.27 us (2%)
    all_to_all x2, blocking collectives, exchange(): lax.all_to_all(flat, ('blk', 'row'), split_axis=0, concat_axis=0, tiled=T...  75.8 us
    pallas_call x2, Pallas kernels, forward_slice(): pl.pallas_call(functools.partial(forward_kernel, which, pitch), grid=(cha...  9.52 us
    pallas_call x2, Pallas kernels, channel_stats(): pl.pallas_call(stats_kernel, grid=(width // wide,), in_specs=[pl.BlockSpe...  7.96 us
    pallas_call x1, Pallas kernels, inverse_rows(): pl.pallas_call(functools.partial(inverse_kernel, pitch), grid=(slices, ch...  7.61 us
    pallas_call x1, Pallas kernels, filter_columns(): pl.pallas_call(filter_kernel, in_specs=[vmem] * 8, out_specs=vmem, out_sh...  3.76 us
    ppermute x2, starting transfers between devices, local(): other = [lax.ppermute(s, 'blk', swap) for s in own]  2.27 us
  transfers between devices with their start and end apart: 2, of which 0 were waited for; matrix products, arithmetic and copies ran while one was open for 0% of the time, Pallas kernels for 8%

profile of v1, /device:TPU:1, one launch (start us, length us, event | category | flops | bytes accessed | tf_op | source)
XLA Modules:
  0.0 107.2 jit_solution(12753134256375667531)
XLA Ops:
  0.0 4.0 %channel_stats.3.own_ref = bf16[3,16,1024]{2,1,0:T(8,128)(2,1)S(1)} custom-call(bf16[2,128,16,1024]{3,2,1,0:T(8,128)(2,1)} %x_ref.7), custom_call_target="tpu_custom_call" | custom-call | flops 10485760 | bytes 4194304 | tf_op jit(solution)/shard_map/channel_stats/pallas_call | solution.py:84
  4.0 0.0 copy-start
  4.0 0.0 copy-start.2
  4.0 2.1 %collective-permute-start.1 = (bf16[3,16,1024]{2,1,0:T(8,128)(2,1)S(1)}, bf16[3,16,1024]{2,1,0:T(8,128)(2,1)S(1)}, u32[]{:S(2)}, u32[]{:S(2)}) collective-permute-start(bf16[3,16,1024]{2,1,0:T(8,128)(2,1)S(1)} %channel_stats.3.own_ref), channel_id=1, source_target_pairs={{0,1},{1,0},{2,3},{3,2},{4,5},{5,4},{6,7},{7,6},{8,9},{9,8},{10,11... | collective-permute-start | bytes 294920 | tf_op jit(solution)/shard_map/ppermute | solution.py:348
  6.1 4.0 %channel_stats.2.own_ref = bf16[3,16,1024]{2,1,0:T(8,128)(2,1)S(1)} custom-call(bf16[2,128,16,1024]{3,2,1,0:T(8,128)(2,1)} %x_ref.7), custom_call_target="tpu_custom_call" | custom-call | flops 10485760 | bytes 4194304 | tf_op jit(solution)/shard_map/channel_stats/pallas_call | solution.py:84
  10.1 0.2 collective-permute-start
  10.3 0.0 collective-permute-done.1.other_ref
  10.3 0.0 copy-done
  10.3 4.8 %norm_and_row_dft.2.rest_0_ = bf16[2,64,32,256]{3,2,1,0:T(8,128)(2,1)S(1)} custom-call(bf16[2,128,16,1024]{3,2,1,0:T(8,128)(2,1)} %x_ref.7, f32[1,128]{1,0:T(1,128)S(1)} %bitcast.11, bf16[3,16,1024]{2,1,0:T(8,128)(2,1)S(1)} %channel_stats.3.own_ref, bf16[3,16,1024]{2,1,0:T(8,128)(2,1)S(1)} %collective-permute-done.1.other_ref, bf16[1024,256]{1,0:T(8,128)(2,1)S(1)} %copy-done), custom_call_target="tpu_custom_call" | custom-call | flops 1073741824 | bytes 4194304 | tf_op jit(solution)/shard_map/norm_and_row_dft/pallas_call | solution.py:145
  15.1 0.0 collective-permute-done.other_ref
  15.1 4.8 %norm_and_row_dft.3 = bf16[2,64,32,256]{3,2,1,0:T(8,128)(2,1)S(1)} custom-call(bf16[2,128,16,1024]{3,2,1,0:T(8,128)(2,1)} %x_ref.7, f32[1,128]{1,0:T(1,128)S(1)} %bitcast.12, bf16[3,16,1024]{2,1,0:T(8,128)(2,1)S(1)} %channel_stats.2.own_ref, bf16[3,16,1024]{2,1,0:T(8,128)(2,1)S(1)} %collective-permute-done.other_ref, ...), custom_call_target="tpu_custom_call", output_to_operand_aliasing={{}: (5, {})} | custom-call | flops 1073741824 | bytes 4194304 | tf_op jit(solution)/shard_map/norm_and_row_dft/pallas_call | solution.py:145
  19.8 0.0 copy-start.3
  19.8 0.0 copy-start.4
  19.9 0.0 copy-start.5
  19.9 0.0 copy-start.6
  19.9 0.0 copy-start.7
  19.9 0.0 copy-start.8
  19.9 0.0 copy-start.9
  19.9 41.4 %all_to_all.10 = bf16[128,32,256]{2,1,0:T(8,128)(2,1)S(1)} all-to-all(bf16[128,32,256]{2,1,0:T(8,128)(2,1)S(1)} %bitcast.7), channel_id=1, replica_groups=mesh['row'=64,'blk'=2] {'blk','row'}, dimensions={0} | all-to-all | bytes 4194304 | tf_op jit(solution)/shard_map/all_to_all | solution.py:333
  61.3 0.0 copy-done.4
  61.4 3.8 %column_filter.1 = bf16[2,64,32,256]{3,2,1,0:T(8,128)(2,1)S(1)} custom-call(bf16[2,64,32,256]{3,2,1,0:T(8,128)(2,1)S(1)} %bitcast.9, bf16[528,1024]{1,0:T(8,128)(2,1)S(1)} %copy-done.7, bf16[1024,512]{1,0:T(8,128)(2,1)S(1)} %copy-done.8, bf16[32,128]{1,0:T(8,128)(2,1)S(1)} %copy-done.9, bf16[2,256,32]{2,1,0:T(8,128)(2,1)S(1)} %bitcast.13, ...), custom_call_target="tpu_custom_call" | custom-call | flops 3221225472 | bytes 8388608 | tf_op jit(solution)/shard_map/column_filter/pallas_call | solution.py:253
  65.1 0.0 copy-start.1
  65.1 34.4 %all_to_all.11 = bf16[128,32,256]{2,1,0:T(8,128)(2,1)S(1)} all-to-all(bf16[128,32,256]{2,1,0:T(8,128)(2,1)S(1)} %bitcast.10), channel_id=1, replica_groups=mesh['row'=64,'blk'=2] {'blk','row'}, dimensions={0} | all-to-all | bytes 4194304 | tf_op jit(solution)/shard_map/all_to_all | solution.py:333
  99.6 7.6 %inverse_row_dft.1 = bf16[2,128,16,1024]{3,2,1,0:T(8,128)(2,1)} custom-call(bf16[2,64,32,256]{3,2,1,0:T(8,128)(2,1)S(1)} %bitcast.8, bf16[256,1024]{1,0:T(8,128)(2,1)S(1)} %copy-done.1), custom_call_target="tpu_custom_call" | custom-call | flops 2147483648 | bytes 8388608 | tf_op jit(solution)/shard_map/inverse_row_dft/pallas_call | solution.py:310
  (8 shorter events, 0.0 us)
Async XLA Ops:
  4.0 6.3 %copy-start = (bf16[1024,256]{1,0:T(8,128)(2,1)S(1)}, bf16[1024,256]{1,0:T(8,128)(2,1)}, u32[]{:S(2)}) copy-start(bf16[1024,256]{1,0:T(8,128)(2,1)} %constant.11.clone.table_ref) | copy-start | bytes 1572868
  4.0 6.3 %copy-start.2 = (f32[128]{0:T(128)S(1)}, f32[128]{0:T(128)}, u32[]{:S(2)}) copy-start(f32[128]{0:T(128)} %param.12) | copy-start | bytes 1540
  4.0 6.3 %collective-permute-start.1 = (bf16[3,16,1024]{2,1,0:T(8,128)(2,1)S(1)}, bf16[3,16,1024]{2,1,0:T(8,128)(2,1)S(1)}, u32[]{:S(2)}, u32[]{:S(2)}) collective-permute-start(bf16[3,16,1024]{2,1,0:T(8,128)(2,1)S(1)} %channel_stats.3.own_ref), channel_id=1, source_target_pairs={{0,1},{1,0},{2,3},{3,2},{4,5},{5,4},{6,7},{7,6},{8,9},{9,8},{10,11... | collective-permute-start | bytes 294920 | tf_op jit(solution)/shard_map/ppermute | solution.py:348
  10.1 4.9 %collective-permute-start = (bf16[3,16,1024]{2,1,0:T(8,128)(2,1)S(1)}, bf16[3,16,1024]{2,1,0:T(8,128)(2,1)S(1)}, u32[]{:S(2)}, u32[]{:S(2)}) collective-permute-start(bf16[3,16,1024]{2,1,0:T(8,128)(2,1)S(1)} %channel_stats.2.own_ref), channel_id=1, source_target_pairs={{0,1},{1,0},{2,3},{3,2},{4,5},{5,4},{6,7},{7,6},{8,9},{9,8},{10,11... | collective-permute-start | bytes 294920 | tf_op jit(solution)/shard_map/ppermute | solution.py:348
  19.8 41.5 %copy-start.3 = (bf16[2,8,32,32]{3,2,1,0:T(8,128)(2,1)S(1)}, bf16[2,8,32,32]{3,2,1,0:T(8,128)(2,1)}, u32[]{:S(2)}) copy-start(bf16[2,8,32,32]{3,2,1,0:T(8,128)(2,1)} %param.13) | copy-start | bytes 98308
  19.8 41.5 %copy-start.4 = (bf16[2,8,32,32]{3,2,1,0:T(8,128)(2,1)S(1)}, bf16[2,8,32,32]{3,2,1,0:T(8,128)(2,1)}, u32[]{:S(2)}) copy-start(bf16[2,8,32,32]{3,2,1,0:T(8,128)(2,1)} %param.15) | copy-start | bytes 98308
  19.9 41.5 %copy-start.5 = (f32[2,256]{1,0:T(2,128)S(1)}, f32[2,256]{1,0:T(2,128)}, u32[]{:S(2)}) copy-start(f32[2,256]{1,0:T(2,128)} %b1_ref.1) | copy-start | bytes 6148
  19.9 41.5 %copy-start.6 = (f32[2,256]{1,0:T(2,128)S(1)}, f32[2,256]{1,0:T(2,128)}, u32[]{:S(2)}) copy-start(f32[2,256]{1,0:T(2,128)} %b2_ref.1) | copy-start | bytes 6148
  19.9 41.5 %copy-start.7 = (bf16[528,1024]{1,0:T(8,128)(2,1)S(1)}, bf16[528,1024]{1,0:T(8,128)(2,1)}, u32[]{:S(2)}) copy-start(bf16[528,1024]{1,0:T(8,128)(2,1)} %constant.12.clone.fwd_ref) | copy-start | bytes 3244036
  19.9 41.5 %copy-start.8 = (bf16[1024,512]{1,0:T(8,128)(2,1)S(1)}, bf16[1024,512]{1,0:T(8,128)(2,1)}, u32[]{:S(2)}) copy-start(bf16[1024,512]{1,0:T(8,128)(2,1)} %constant.13.clone.inv_ref) | copy-start | bytes 3145732
  19.9 41.5 %copy-start.9 = (bf16[32,128]{1,0:T(8,128)(2,1)S(1)}, bf16[32,128]{1,0:T(8,128)(2,1)}, u32[]{:S(2)}) copy-start(bf16[32,128]{1,0:T(8,128)(2,1)} %constant.10.clone.spread_ref) | copy-start | bytes 24580
  65.1 34.4 %copy-start.1 = (bf16[256,1024]{1,0:T(8,128)(2,1)S(1)}, bf16[256,1024]{1,0:T(8,128)(2,1)}, u32[]{:S(2)}) copy-start(bf16[256,1024]{1,0:T(8,128)(2,1)} %constant.14.clone.table_ref) | copy-start | bytes 1572868

commit v2 on v1

--- a/solution.py
+++ b/solution.py
@@ -58,35 +58,62 @@
     return _bf16(forward), _bf16(inverse)
 
 
-def stats_kernel(x_ref, out_ref):
-    channels = x_ref.shape[1]
-    zero = jnp.zeros(x_ref.shape[2:], F32)
-
-    def add(c, total):
-        return total + x_ref[0, c].astype(F32)
-
-    mean = lax.fori_loop(0, channels, add, zero, unroll=16) * (1.0 / channels)
-
-    def add_square(c, total):
-        centered = x_ref[0, c].astype(F32) - mean
-        return total + centered * centered
-
-    moment = lax.fori_loop(0, channels, add_square, zero, unroll=16)
-    high = mean.astype(BF16)
-    out_ref[0] = high
-    out_ref[1] = (mean - high.astype(F32)).astype(BF16)
-    out_ref[2] = moment.astype(BF16)
+def stats_kernel(which, x_ref, slice_ref, stat_ref, pivot_s, first_s, second_s, sems):
+    channels, rows, width = slice_ref.shape
+    chunks = sems.shape[0]
+    chunk = channels // chunks
+    wide = min(512, width)
+    copies = []
+    for i in range(chunks):
+        part = pl.ds(i * chunk, chunk)
+        copies.append(pltpu.make_async_copy(x_ref.at[which, part], slice_ref.at[part], sems.at[i]))
+        copies[-1].start()
+    for i in range(chunks):
+        copies[i].wait()
+        for lane in range(0, width, wide):
+            here = slice(lane, lane + wide)
+            if i == 0:
+                pivot = jnp.zeros((rows, wide), F32)
+                for c in range(chunk):
+                    pivot = pivot + slice_ref[c, :, here].astype(F32)
+                pivot = pivot * (1.0 / chunk)
+                pivot_s[:, here] = pivot
+                first = jnp.zeros((rows, wide), F32)
+                second = jnp.zeros((rows, wide), F32)
+            else:
+                pivot, first, second = pivot_s[:, here], first_s[:, here], second_s[:, here]
+            for c in range(i * chunk, (i + 1) * chunk):
+                shifted = slice_ref[c, :, here].astype(F32) - pivot
+                first = first + shifted
+                second = second + shifted * shifted
+            if i < chunks - 1:
+                first_s[:, here], second_s[:, here] = first, second
+            else:
+                offset = first * (1.0 / channels)
+                mean = pivot + offset
+                high = mean.astype(BF16)
+                stat_ref[0, :, here] = high
+                stat_ref[1, :, here] = (mean - high.astype(F32)).astype(BF16)
+                stat_ref[2, :, here] = jnp.maximum(second - first * offset, 0.0).astype(BF16)
 
 
 def channel_stats(field, which):
     _, channels, rows, width = field.shape
-    wide = min(256, width)
+    vmem = pl.BlockSpec(memory_space=pltpu.VMEM)
     return pl.pallas_call(
-        stats_kernel,
-        grid=(width // wide,),
-        in_specs=[pl.BlockSpec((1, channels, rows, wide), lambda j: (which, 0, 0, j))],
-        out_specs=pl.BlockSpec((3, rows, wide), lambda j: (0, 0, j)),
-        out_shape=jax.ShapeDtypeStruct((3, rows, width), BF16),
+        functools.partial(stats_kernel, which),
+        in_specs=[pl.BlockSpec(memory_space=pltpu.HBM)],
+        out_specs=[vmem, vmem],
+        out_shape=[
+            jax.ShapeDtypeStruct((channels, rows, width), BF16),
+            jax.ShapeDtypeStruct((3, rows, width), BF16),
+        ],
+        scratch_shapes=[
+            pltpu.VMEM((rows, width), F32),
+            pltpu.VMEM((rows, width), F32),
+            pltpu.VMEM((rows, width), F32),
+            pltpu.SemaphoreType.DMA((8,)),
+        ],
         compiler_params=pltpu.CompilerParams(vmem_limit_bytes=16 * MIB),
         cost_estimate=pl.CostEstimate(
             flops=5 * channels * rows * width, bytes_accessed=2 * channels * rows * width, transcendentals=0
@@ -95,63 +122,55 @@
     )(pltpu.with_memory_space_constraint(field, pltpu.HBM))
 
 
-def forward_kernel(which, pitch, x_ref, gain_ref, own_ref, other_ref, table_ref, *rest):
-    send_ref, mean_s, scale_s, spec_s, turn_s = rest[-5:]
-    step = pl.program_id(0)
-    chan_block, rows, width = x_ref.shape[1:]
+def forward_kernel(which, chan_block, pitch, x_ref, gain_ref, own_ref, other_ref, table_ref, *rest):
+    send_ref, spec_s, turn_s = rest[-3:]
+    channels, rows, width = x_ref.shape
     parts, _, half = spec_s.shape
-    channels = turn_s.shape[-1]
     owners = send_ref.shape[1]
 
-    @pl.when(step == 0)
-    def _():
-        own_mean = own_ref[0].astype(F32) + own_ref[1].astype(F32)
-        other_mean = other_ref[0].astype(F32) + other_ref[1].astype(F32)
-        delta = own_mean - other_mean
-        total = 2.0 * channels
-        moment = own_ref[2].astype(F32) + other_ref[2].astype(F32) + delta * delta * (channels * 0.5)
-        mean_s[...] = (own_mean + other_mean) * 0.5
-        scale_s[...] = lax.rsqrt(moment * (1.0 / total) + EPS)
-
-    normed = ((x_ref[0].astype(F32) - mean_s[...][None]) * scale_s[...][None]).astype(BF16)
-    spec = jnp.dot(normed.reshape(chan_block * rows, width), table_ref[...], preferred_element_type=F32)
-    for c in range(chan_block):
-        start = pl.multiple_of(step * (chan_block * pitch), chan_block * pitch) + c * pitch
+    own_mean = own_ref[0].astype(F32) + own_ref[1].astype(F32)
+    other_mean = other_ref[0].astype(F32) + other_ref[1].astype(F32)
+    delta = own_mean - other_mean
+    total = 2.0 * channels
+    moment = own_ref[2].astype(F32) + other_ref[2].astype(F32) + delta * delta * (channels * 0.5)
+    mean = (own_mean + other_mean) * 0.5
+    scale = lax.rsqrt(moment * (1.0 / total) + EPS)
+
+    for first in range(0, channels, chan_block):
+        field = x_ref[first : first + chan_block].astype(F32)
+        normed = ((field - mean[None]) * scale[None]).astype(BF16)
+        spec = jnp.dot(normed.reshape(chan_block * rows, width), table_ref[...], preferred_element_type=F32)
+        for c in range(chan_block):
+            start = (first + c) * pitch
+            for p in range(parts):
+                spec_s[p, start : start + rows, :] = spec[c * rows : (c + 1) * rows, p * half : (p + 1) * half]
+
+    for h in range(rows):
         for p in range(parts):
-            spec_s[p, pl.ds(start, rows), :] = spec[c * rows : (c + 1) * rows, p * half : (p + 1) * half]
-
-    @pl.when(step == pl.num_programs(0) - 1)
-    def _():
-        for h in range(rows):
-            for p in range(parts):
-                turned = spec_s[p, pl.ds(h, channels, stride=pitch), :].T * gain_ref[...]
-                turn_s[pl.ds(p * half * pitch + h, half, stride=pitch), :] = turned
-        for r in range(2):
-            for kk in range(2):
-                for d in range(owners):
-                    start = ((r * 2 + kk) * owners + d) * pitch
-                    send_ref[which, d, r * rows : (r + 1) * rows, kk * channels : (kk + 1) * channels] = turn_s[
-                        start : start + rows, :
-                    ].astype(BF16)
-
-
-def forward_slice(field, which, gain, own, other, table, owners, send):
-    slices, channels, rows, width = field.shape
+            turned = spec_s[p, pl.ds(h, channels, stride=pitch), :].T * gain_ref[...]
+            turn_s[pl.ds(p * half * pitch + h, half, stride=pitch), :] = turned
+    for r in range(2):
+        for kk in range(2):
+            for d in range(owners):
+                start = ((r * 2 + kk) * owners + d) * pitch
+                send_ref[which, d, r * rows : (r + 1) * rows, kk * channels : (kk + 1) * channels] = turn_s[
+                    start : start + rows, :
+                ].astype(BF16)
+
+
+def forward_slice(field, which, slices, gain, own, other, table, owners, send):
+    channels, rows, width = field.shape
     two_k = table.shape[1]
     chan_block = min(32, channels)
     pitch = rows + 8
     aliased = [] if send is None else [send]
     vmem = pl.BlockSpec(memory_space=pltpu.VMEM)
     return pl.pallas_call(
-        functools.partial(forward_kernel, which, pitch),
-        grid=(channels // chan_block,),
-        in_specs=[pl.BlockSpec((1, chan_block, rows, width), lambda i: (which, i, 0, 0))]
-        + [vmem] * (4 + len(aliased)),
+        functools.partial(forward_kernel, which, chan_block, pitch),
+        in_specs=[vmem] * (5 + len(aliased)),
         out_specs=vmem,
         out_shape=jax.ShapeDtypeStruct((slices, owners, 2 * rows, 2 * channels), BF16),
         scratch_shapes=[
-            pltpu.VMEM((rows, width), F32),
-            pltpu.VMEM((rows, width), F32),
             pltpu.VMEM((2, channels * pitch, two_k // 2), F32),
             pltpu.VMEM((two_k * pitch, channels), F32),
         ],
@@ -163,7 +182,7 @@
             transcendentals=0,
         ),
         name="norm_and_row_dft",
-    )(pltpu.with_memory_space_constraint(field, pltpu.HBM), gain.reshape(1, channels), own, other, table, *aliased)
+    )(field, gain.reshape(1, channels), own, other, table, *aliased)
 
 
 def block_diagonal(weights, spread, lanes):
@@ -268,17 +287,13 @@
     )(received, fwd, inv, spread, flat(w_first), b_first, flat(w_second), b_second)
 
 
-def inverse_kernel(pitch, x_ref, table_ref, out_ref, turn_s, spec_s):
-    owners, two_rows, wide = x_ref.shape[1:]
+def inverse_kernel(chan_block, pitch, x_ref, table_ref, out_ref, turn_s, spec_s, done_s, sems):
+    slices, owners, two_rows, wide = x_ref.shape
     rows = two_rows // 2
     channels = wide // 2
     parts, _, half = spec_s.shape
-    chan_block = out_ref.shape[1]
-    which = pl.program_id(0)
-    step = pl.program_id(1)
-
-    @pl.when(step == 0)
-    def _():
+    copies = []
+    for which in range(slices):
         for r in range(2):
             for kk in range(2):
                 for d in range(owners):
@@ -290,13 +305,21 @@
             for p in range(parts):
                 turned = turn_s[pl.ds(p * half * pitch + h, half, stride=pitch), :].T
                 spec_s[p, pl.ds(h, channels, stride=pitch), :] = turned
-
-    spec = []
-    for c in range(chan_block):
-        start = pl.multiple_of(step * (chan_block * pitch), chan_block * pitch) + c * pitch
-        spec.append(jnp.concatenate([spec_s[p, pl.ds(start, rows), :].astype(BF16) for p in range(parts)], axis=1))
-    mixed = jnp.dot(jnp.concatenate(spec, axis=0), table_ref[...], preferred_element_type=F32)
-    out_ref[0] = mixed.astype(BF16).reshape(chan_block, rows, -1)
+        for first in range(0, channels, chan_block):
+            spec = []
+            for c in range(first, first + chan_block):
+                start = c * pitch
+                both = [spec_s[p, start : start + rows, :].astype(BF16) for p in range(parts)]
+                spec.append(jnp.concatenate(both, axis=1))
+            mixed = jnp.dot(jnp.concatenate(spec, axis=0), table_ref[...], preferred_element_type=F32)
+            block = pl.ds(first, chan_block)
+            done_s[which, block] = mixed.astype(BF16).reshape(chan_block, rows, -1)
+            copies.append(
+                pltpu.make_async_copy(done_s.at[which, block], out_ref.at[which, block], sems.at[len(copies)])
+            )
+            copies[-1].start()
+    for copy in copies:
+        copy.wait()
 
 
 def inverse_rows(received, table):
@@ -304,20 +327,21 @@
     rows = two_rows // 2
     channels = wide // 2
     two_k, width = table.shape
-    chan_block = min(32, channels)
+    chan_block = min(16, channels)
     pitch = rows + 8
     vmem = pl.BlockSpec(memory_space=pltpu.VMEM)
     return pl.pallas_call(
-        functools.partial(inverse_kernel, pitch),
-        grid=(slices, channels // chan_block),
+        functools.partial(inverse_kernel, chan_block, pitch),
         in_specs=[vmem, vmem],
-        out_specs=pl.BlockSpec((1, chan_block, rows, width), lambda b, i: (b, i, 0, 0)),
+        out_specs=pl.BlockSpec(memory_space=pltpu.HBM),
         out_shape=jax.ShapeDtypeStruct((slices, channels, rows, width), BF16),
         scratch_shapes=[
             pltpu.VMEM((two_k * pitch, channels), F32),
             pltpu.VMEM((2, channels * pitch, two_k // 2), F32),
-        ],
-        compiler_params=pltpu.CompilerParams(vmem_limit_bytes=24 * MIB),
+            pltpu.VMEM((slices, channels, rows, width), BF16),
+            pltpu.SemaphoreType.DMA((slices * channels // chan_block,)),
+        ],
+        compiler_params=pltpu.CompilerParams(vmem_limit_bytes=40 * MIB),
         cost_estimate=pl.CostEstimate(
             flops=2 * slices * channels * rows * width * two_k,
             bytes_accessed=2 * slices * channels * rows * width,
@@ -344,11 +368,11 @@
     table = jnp.asarray(forward_table(width, modes_x))
 
     swap = [(0, 1), (1, 0)]
-    own = [channel_stats(field, b) for b in range(slices)]
+    held, own = zip(*[channel_stats(field, b) for b in range(slices)])
     other = [lax.ppermute(s, "blk", swap) for s in own]
     send = None
     for b in range(slices):
-        send = forward_slice(field, b, gain, own[b], other[b], table, owners, send)
+        send = forward_slice(held[b], b, slices, gain, own[b], other[b], table, owners, send)
     columns = exchange(send)
     filtered = filter_columns(
         columns, jnp.asarray(fwd), jnp.asarray(inv), spread, w_first, b_first, w_second, b_second

time: 108 us -> 98.7 us (0.914)
  Pallas kernels: 28.8 us -> 18.4 us
  waiting for transfers between devices: 0.01 us -> 1.28 us
    pallas_call x5, Pallas kernels: 25.1 us -> 14.6 us  [the longest x2 5.69 us: channel_stats(): pl.pallas_call(functools.partial(stats_kernel, which), in_specs=[pl.Block...]
    ppermute x2, waiting for transfers between devices: 0.01 us -> 1.28 us  [local(): other = [lax.ppermute(s, 'blk', swap) for s in own]]
  transfers between devices with their start and end apart: 2 -> 2, of which waited for: 0 -> 1; matrix products, arithmetic and copies ran while one was open for 0% -> 0% of each run, Pallas kernels for 8% -> 5%
where the time goes in v2:
time: 98.7 us; the launch traced here: 98.5 us
  blocking collectives  76.2 us (77%)
  Pallas kernels  18.4 us (19%)
  starting transfers between devices  2.27 us (2%)
  waiting for transfers between devices  1.28 us (1%)
    all_to_all x2, blocking collectives, exchange(): lax.all_to_all(flat, ('blk', 'row'), split_axis=0, concat_axis=0, tiled=T...  76.2 us
    pallas_call x2, Pallas kernels, channel_stats(): pl.pallas_call(functools.partial(stats_kernel, which), in_specs=[pl.Block...  5.69 us
    pallas_call x1, Pallas kernels, inverse_rows(): pl.pallas_call(functools.partial(inverse_kernel, chan_block, pitch), in_s...  4.73 us
    pallas_call x2, Pallas kernels, forward_slice(): pl.pallas_call(functools.partial(forward_kernel, which, chan_block, pitch...  4.2 us
    pallas_call x1, Pallas kernels, filter_columns(): pl.pallas_call(filter_kernel, in_specs=[vmem] * 8, out_specs=vmem, out_sh...  3.77 us
    ppermute x2, starting transfers between devices, local(): other = [lax.ppermute(s, 'blk', swap) for s in own]  2.27 us
  transfers between devices with their start and end apart: 2, of which 1 were waited for; matrix products, arithmetic and copies ran while one was open for 0% of the time, Pallas kernels for 5%

profile of v2, /device:TPU:1, one launch (start us, length us, event | category | flops | bytes accessed | tf_op | source)
XLA Modules:
  0.0 98.5 jit_solution(7175787624805843406)
XLA Ops:
  0.0 2.8 %channel_stats.3 = (bf16[128,16,1024]{2,1,0:T(8,128)(2,1)S(1)}, bf16[3,16,1024]{2,1,0:T(8,128)(2,1)S(1)}) custom-call(bf16[2,128,16,1024]{3,2,1,0:T(8,128)(2,1)} %x_ref.3), custom_call_target="tpu_custom_call" | custom-call | flops 10485760 | bytes 4194304 | tf_op jit(solution)/shard_map/channel_stats/pallas_call | solution.py:103
  2.8 0.0 copy-start
  2.9 0.0 copy-start.2
  2.9 2.1 %collective-permute-start.1 = (bf16[3,16,1024]{2,1,0:T(8,128)(2,1)S(1)}, bf16[3,16,1024]{2,1,0:T(8,128)(2,1)S(1)}, u32[]{:S(2)}, u32[]{:S(2)}) collective-permute-start(bf16[3,16,1024]{2,1,0:T(8,128)(2,1)S(1)} %get-tuple-element.12.own_ref), channel_id=1, source_target_pairs={{0,1},{1,0},{2,3},{3,2},{4,5},{5,4},{6,7},{7,6},{8,9},{9,8},{10,11... | collective-permute-start | bytes 294920 | tf_op jit(solution)/shard_map/ppermute | solution.py:372
  5.0 2.9 %channel_stats.2 = (bf16[128,16,1024]{2,1,0:T(8,128)(2,1)S(1)}, bf16[3,16,1024]{2,1,0:T(8,128)(2,1)S(1)}) custom-call(bf16[2,128,16,1024]{3,2,1,0:T(8,128)(2,1)} %x_ref.3), custom_call_target="tpu_custom_call" | custom-call | flops 10485760 | bytes 4194304 | tf_op jit(solution)/shard_map/channel_stats/pallas_call | solution.py:103
  7.9 0.2 collective-permute-start
  8.0 0.0 collective-permute-done.1.other_ref
  8.0 0.0 copy-done
  8.0 2.1 %norm_and_row_dft.2.rest_0_ = bf16[2,64,32,256]{3,2,1,0:T(8,128)(2,1)S(1)} custom-call(bf16[128,16,1024]{2,1,0:T(8,128)(2,1)S(1)} %get-tuple-element.11.x_ref, f32[1,128]{1,0:T(1,128)S(1)} %bitcast.11, bf16[3,16,1024]{2,1,0:T(8,128)(2,1)S(1)} %get-tuple-element.12.own_ref, bf16[3,16,1024]{2,1,0:T(8,128)(2,1)S(1)} %collective-permute-done.1.other_ref, ...), custom_call_target="tpu_custom_call" | custom-call | flops 1073741824 | bytes 4194304 | tf_op jit(solution)/shard_map/norm_and_row_dft/pallas_call | solution.py:168
  10.1 1.3 %collective-permute-done.other_ref = bf16[3,16,1024]{2,1,0:T(8,128)(2,1)S(1)} collective-permute-done((bf16[3,16,1024]{2,1,0:T(8,128)(2,1)S(1)}, bf16[3,16,1024]{2,1,0:T(8,128)(2,1)S(1)}, u32[]{:S(2)}, u32[]{:S(2)}) %collective-permute-start) | collective-permute-done | bytes 98336 | tf_op jit(solution)/shard_map/ppermute | solution.py:372
  11.4 2.1 %norm_and_row_dft.3 = bf16[2,64,32,256]{3,2,1,0:T(8,128)(2,1)S(1)} custom-call(bf16[128,16,1024]{2,1,0:T(8,128)(2,1)S(1)} %get-tuple-element.9.x_ref, f32[1,128]{1,0:T(1,128)S(1)} %bitcast.12, bf16[3,16,1024]{2,1,0:T(8,128)(2,1)S(1)} %get-tuple-element.10.own_ref, ...), custom_call_target="tpu_custom_call", output_to_operand_aliasing={{}: (5, {})} | custom-call | flops 1073741824 | bytes 4194304 | tf_op jit(solution)/shard_map/norm_and_row_dft/pallas_call | solution.py:168
  13.5 0.0 copy-start.3
  13.5 0.0 copy-start.4
  13.5 0.0 copy-start.5
  13.5 0.0 copy-start.6
  13.6 0.0 copy-start.7
  13.6 0.0 copy-start.8
  13.6 0.0 copy-start.9
  13.6 41.8 %all_to_all.10 = bf16[128,32,256]{2,1,0:T(8,128)(2,1)S(1)} all-to-all(bf16[128,32,256]{2,1,0:T(8,128)(2,1)S(1)} %bitcast.7), channel_id=1, replica_groups=mesh['row'=64,'blk'=2] {'blk','row'}, dimensions={0} | all-to-all | bytes 4194304 | tf_op jit(solution)/shard_map/all_to_all | solution.py:357
  55.4 0.0 copy-done.3
  55.4 3.8 %column_filter.1 = bf16[2,64,32,256]{3,2,1,0:T(8,128)(2,1)S(1)} custom-call(bf16[2,64,32,256]{3,2,1,0:T(8,128)(2,1)S(1)} %bitcast.9, bf16[528,1024]{1,0:T(8,128)(2,1)S(1)} %copy-done.7, bf16[1024,512]{1,0:T(8,128)(2,1)S(1)} %copy-done.8, bf16[32,128]{1,0:T(8,128)(2,1)S(1)} %copy-done.9, bf16[2,256,32]{2,1,0:T(8,128)(2,1)S(1)} %bitcast.13, ...), custom_call_target="tpu_custom_call" | custom-call | flops 3221225472 | bytes 8388608 | tf_op jit(solution)/shard_map/column_filter/pallas_call | solution.py:272
  59.2 0.0 copy-start.1
  59.2 34.4 %all_to_all.11 = bf16[128,32,256]{2,1,0:T(8,128)(2,1)S(1)} all-to-all(bf16[128,32,256]{2,1,0:T(8,128)(2,1)S(1)} %bitcast.10), channel_id=1, replica_groups=mesh['row'=64,'blk'=2] {'blk','row'}, dimensions={0} | all-to-all | bytes 4194304 | tf_op jit(solution)/shard_map/all_to_all | solution.py:357
  93.6 4.7 %inverse_row_dft.1 = bf16[2,128,16,1024]{3,2,1,0:T(8,128)(2,1)} custom-call(bf16[2,64,32,256]{3,2,1,0:T(8,128)(2,1)S(1)} %bitcast.8, bf16[256,1024]{1,0:T(8,128)(2,1)S(1)} %copy-done.1), custom_call_target="tpu_custom_call" | custom-call | flops 2147483648 | bytes 8388608 | tf_op jit(solution)/shard_map/inverse_row_dft/pallas_call | solution.py:333
  (8 shorter events, 0.0 us)
Async XLA Ops:
  2.8 5.2 %copy-start = (bf16[1024,256]{1,0:T(8,128)(2,1)S(1)}, bf16[1024,256]{1,0:T(8,128)(2,1)}, u32[]{:S(2)}) copy-start(bf16[1024,256]{1,0:T(8,128)(2,1)} %constant.11.clone.table_ref) | copy-start | bytes 1572868
  2.9 5.2 %copy-start.2 = (f32[128]{0:T(128)S(1)}, f32[128]{0:T(128)}, u32[]{:S(2)}) copy-start(f32[128]{0:T(128)} %param.12) | copy-start | bytes 1540
  2.9 5.1 %collective-permute-start.1 = (bf16[3,16,1024]{2,1,0:T(8,128)(2,1)S(1)}, bf16[3,16,1024]{2,1,0:T(8,128)(2,1)S(1)}, u32[]{:S(2)}, u32[]{:S(2)}) collective-permute-start(bf16[3,16,1024]{2,1,0:T(8,128)(2,1)S(1)} %get-tuple-element.12.own_ref), channel_id=1, source_target_pairs={{0,1},{1,0},{2,3},{3,2},{4,5},{5,4},{6,7},{7,6},{8,9},{9,8},{10,11... | collective-permute-start | bytes 294920 | tf_op jit(solution)/shard_map/ppermute | solution.py:372
  7.9 3.5 %collective-permute-start = (bf16[3,16,1024]{2,1,0:T(8,128)(2,1)S(1)}, bf16[3,16,1024]{2,1,0:T(8,128)(2,1)S(1)}, u32[]{:S(2)}, u32[]{:S(2)}) collective-permute-start(bf16[3,16,1024]{2,1,0:T(8,128)(2,1)S(1)} %get-tuple-element.10.own_ref), channel_id=1, source_target_pairs={{0,1},{1,0},{2,3},{3,2},{4,5},{5,4},{6,7},{7,6},{8,9},{9,8},{10,11... | collective-permute-start | bytes 294920 | tf_op jit(solution)/shard_map/ppermute | solution.py:372
  13.5 41.9 %copy-start.3 = (bf16[2,8,32,32]{3,2,1,0:T(8,128)(2,1)S(1)}, bf16[2,8,32,32]{3,2,1,0:T(8,128)(2,1)}, u32[]{:S(2)}) copy-start(bf16[2,8,32,32]{3,2,1,0:T(8,128)(2,1)} %param.13) | copy-start | bytes 98308
  13.5 41.9 %copy-start.4 = (bf16[2,8,32,32]{3,2,1,0:T(8,128)(2,1)S(1)}, bf16[2,8,32,32]{3,2,1,0:T(8,128)(2,1)}, u32[]{:S(2)}) copy-start(bf16[2,8,32,32]{3,2,1,0:T(8,128)(2,1)} %param.15) | copy-start | bytes 98308
  13.5 41.9 %copy-start.5 = (f32[2,256]{1,0:T(2,128)S(1)}, f32[2,256]{1,0:T(2,128)}, u32[]{:S(2)}) copy-start(f32[2,256]{1,0:T(2,128)} %b1_ref.1) | copy-start | bytes 6148
  13.5 41.9 %copy-start.6 = (f32[2,256]{1,0:T(2,128)S(1)}, f32[2,256]{1,0:T(2,128)}, u32[]{:S(2)}) copy-start(f32[2,256]{1,0:T(2,128)} %b2_ref.1) | copy-start | bytes 6148
  13.6 41.9 %copy-start.7 = (bf16[528,1024]{1,0:T(8,128)(2,1)S(1)}, bf16[528,1024]{1,0:T(8,128)(2,1)}, u32[]{:S(2)}) copy-start(bf16[528,1024]{1,0:T(8,128)(2,1)} %constant.12.clone.fwd_ref) | copy-start | bytes 3244036
  13.6 41.9 %copy-start.8 = (bf16[1024,512]{1,0:T(8,128)(2,1)S(1)}, bf16[1024,512]{1,0:T(8,128)(2,1)}, u32[]{:S(2)}) copy-start(bf16[1024,512]{1,0:T(8,128)(2,1)} %constant.13.clone.inv_ref) | copy-start | bytes 3145732
  13.6 41.9 %copy-start.9 = (bf16[32,128]{1,0:T(8,128)(2,1)S(1)}, bf16[32,128]{1,0:T(8,128)(2,1)}, u32[]{:S(2)}) copy-start(bf16[32,128]{1,0:T(8,128)(2,1)} %constant.10.clone.spread_ref) | copy-start | bytes 24580
  59.2 34.4 %copy-start.1 = (bf16[256,1024]{1,0:T(8,128)(2,1)S(1)}, bf16[256,1024]{1,0:T(8,128)(2,1)}, u32[]{:S(2)}) copy-start(bf16[256,1024]{1,0:T(8,128)(2,1)} %constant.14.clone.table_ref) | copy-start | bytes 1572868

commit v3 on v2

--- a/solution.py
+++ b/solution.py
@@ -76,21 +76,22 @@
                 pivot = jnp.zeros((rows, wide), F32)
                 for c in range(chunk):
                     pivot = pivot + slice_ref[c, :, here].astype(F32)
-                pivot = pivot * (1.0 / chunk)
+                pivot = (pivot * (1.0 / chunk)).astype(BF16)
                 pivot_s[:, here] = pivot
                 first = jnp.zeros((rows, wide), F32)
                 second = jnp.zeros((rows, wide), F32)
             else:
                 pivot, first, second = pivot_s[:, here], first_s[:, here], second_s[:, here]
-            for c in range(i * chunk, (i + 1) * chunk):
-                shifted = slice_ref[c, :, here].astype(F32) - pivot
-                first = first + shifted
-                second = second + shifted * shifted
+            for c in range(i * chunk, (i + 1) * chunk, 2):
+                one = slice_ref[c, :, here] - pivot
+                two = slice_ref[c + 1, :, here] - pivot
+                first = first + (one + two).astype(F32)
+                second = second + (one * one + two * two).astype(F32)
             if i < chunks - 1:
                 first_s[:, here], second_s[:, here] = first, second
             else:
                 offset = first * (1.0 / channels)
-                mean = pivot + offset
+                mean = pivot.astype(F32) + offset
                 high = mean.astype(BF16)
                 stat_ref[0, :, here] = high
                 stat_ref[1, :, here] = (mean - high.astype(F32)).astype(BF16)
@@ -109,7 +110,7 @@
             jax.ShapeDtypeStruct((3, rows, width), BF16),
         ],
         scratch_shapes=[
-            pltpu.VMEM((rows, width), F32),
+            pltpu.VMEM((rows, width), BF16),
             pltpu.VMEM((rows, width), F32),
             pltpu.VMEM((rows, width), F32),
             pltpu.SemaphoreType.DMA((8,)),
@@ -207,7 +208,7 @@
     return jnp.concatenate([b_ref[0:1, mine], b_ref[1:2, mine]], axis=1)
 
 
-def filter_kernel(x_ref, fwd_ref, inv_ref, spread_ref, w1_ref, b1_ref, w2_ref, b2_ref, out_ref, big1, big2, packed):
+def filter_kernel(x_ref, fwd_ref, inv_ref, spread_ref, w1_ref, b1_ref, w2_ref, b2_ref, out_ref, big1, big2, spec_s, packed):
     groups, owners, two_rows, wide = x_ref.shape
     rows = two_rows // 2
     lanes = wide // 2
@@ -218,47 +219,62 @@
     norm = 1.0 / math.sqrt(height)
     last_cos = jnp.where(turn == 0, norm, jnp.where(turn == 2, -norm, 0.0))
     last_sin = jnp.where(turn == 1, norm, jnp.where(turn == 3, -norm, 0.0))
-    for group in range(groups):
-        fill_weights(w1_ref, group, spread_ref[...], big1, lanes)
-        fill_weights(w2_ref, group, spread_ref[...], big2, lanes)
-        bias1 = bias_row(b1_ref, group, lanes)
-        bias2 = bias_row(b2_ref, group, lanes)
+    real_part = lambda kk: slice(kk * lanes, (kk + 1) * lanes)
+    imag_part = lambda kk: slice(wide + kk * lanes, wide + (kk + 1) * lanes)
+
+    def transform(group):
         real_in = x_ref[group, :, :rows, :].reshape(height, wide)
         imag_in = x_ref[group, :, rows:, :].reshape(height, wide)
         from_real = jnp.dot(fwd_ref[...], real_in, preferred_element_type=F32)
         from_imag = jnp.dot(fwd_ref[...], imag_in, preferred_element_type=F32)
-        extra = []
+        last = slice(2 * quarter, 2 * quarter + 1)
+        last_sine = slice(2 * quarter + 1, 2 * quarter + 2)
         for kk in range(2):
-            part = slice(kk * lanes, (kk + 1) * lanes)
+            part = real_part(kk)
             cos_re, sin_re = from_real[:quarter, part], from_real[quarter : 2 * quarter, part]
             cos_im, sin_im = from_imag[:quarter, part], from_imag[quarter : 2 * quarter, part]
-            last_re = from_real[2 * quarter : 2 * quarter + 1, part] - from_imag[2 * quarter + 1 : 2 * quarter + 2, part]
-            last_im = from_imag[2 * quarter : 2 * quarter + 1, part] + from_real[2 * quarter + 1 : 2 * quarter + 2, part]
-            plus = jnp.concatenate([cos_re + sin_im, cos_im - sin_re], axis=1)
-            minus = jnp.concatenate(
-                [jnp.where(top, last_re, cos_re - sin_im), jnp.where(top, last_im, cos_im + sin_re)], axis=1
-            )
-            spectrum = jnp.concatenate([plus, minus], axis=0).astype(BF16)
-            hidden = jnp.dot(spectrum, big1[...], preferred_element_type=F32) + bias1
+            last_re = from_real[last, part] - from_imag[last_sine, part]
+            last_im = from_imag[last, part] + from_real[last_sine, part]
+            spec_s[group, kk, :quarter, :lanes] = (cos_re + sin_im).astype(BF16)
+            spec_s[group, kk, :quarter, lanes:] = (cos_im - sin_re).astype(BF16)
+            spec_s[group, kk, quarter:, :lanes] = jnp.where(top, last_re, cos_re - sin_im).astype(BF16)
+            spec_s[group, kk, quarter:, lanes:] = jnp.where(top, last_im, cos_im + sin_re).astype(BF16)
+
+    def mix(group):
+        extra_re, extra_im = [], []
+        for kk in range(2):
+            hidden = jnp.dot(spec_s[group, kk], big1[group], preferred_element_type=F32) + bias_row(b1_ref, group, lanes)
             hidden = jnp.maximum(hidden, 0.0).astype(BF16)
-            mixed = jnp.dot(hidden, big2[...], preferred_element_type=F32) + bias2
+            mixed = jnp.dot(hidden, big2[group], preferred_element_type=F32) + bias_row(b2_ref, group, lanes)
             kept = mixed - jnp.clip(mixed, -SHRINK, SHRINK)
             plus_re, plus_im = kept[:quarter, :lanes], kept[:quarter, lanes:]
             minus_re, minus_im = kept[quarter:, :lanes], kept[quarter:, lanes:]
             last_re, last_im = minus_re[0:1], minus_im[0:1]
             minus_re = jnp.where(top, 0.0, minus_re)
             minus_im = jnp.where(top, 0.0, minus_im)
-            packed[:quarter, part] = (plus_re + minus_re).astype(BF16)
-            packed[:quarter, wide + kk * lanes : wide + (kk + 1) * lanes] = (plus_im + minus_im).astype(BF16)
-            packed[quarter:, part] = (minus_im - plus_im).astype(BF16)
-            packed[quarter:, wide + kk * lanes : wide + (kk + 1) * lanes] = (plus_re - minus_re).astype(BF16)
-            extra.append((last_cos * last_re + last_sin * last_im, last_cos * last_im - last_sin * last_re))
-        column = jnp.dot(inv_ref[...], packed[...], preferred_element_type=F32)
-        extra = jnp.concatenate([extra[0][0], extra[1][0], extra[0][1], extra[1][1]], axis=1)
+            packed[group, :quarter, real_part(kk)] = (plus_re + minus_re).astype(BF16)
+            packed[group, :quarter, imag_part(kk)] = (plus_im + minus_im).astype(BF16)
+            packed[group, quarter:, real_part(kk)] = (minus_im - plus_im).astype(BF16)
+            packed[group, quarter:, imag_part(kk)] = (plus_re - minus_re).astype(BF16)
+            extra_re.append(last_cos * last_re + last_sin * last_im)
+            extra_im.append(last_cos * last_im - last_sin * last_re)
+        return jnp.concatenate(extra_re + extra_im, axis=1)
+
+    def invert(group, extra):
+        column = jnp.dot(inv_ref[...], packed[group], preferred_element_type=F32)
         column = (column.reshape(height // 8, 8, 2 * wide) + extra[None]).astype(BF16)
         column = column.reshape(height, 2 * wide)
         out_ref[group, :, :rows, :] = column[:, :wide].reshape(owners, rows, wide)
         out_ref[group, :, rows:, :] = column[:, wide:].reshape(owners, rows, wide)
+
+    for group in range(groups):
+        fill_weights(w1_ref, group, spread_ref[...], big1.at[group], lanes)
+        fill_weights(w2_ref, group, spread_ref[...], big2.at[group], lanes)
+    for group in range(groups):
+        transform(group)
+    extra = [mix(group) for group in range(groups)]
+    for group in range(groups):
+        invert(group, extra[group])
 
 
 def filter_columns(received, fwd, inv, spread, w_first, b_first, w_second, b_second):
@@ -275,9 +291,10 @@
         out_specs=vmem,
         out_shape=jax.ShapeDtypeStruct(received.shape, BF16),
         scratch_shapes=[
-            pltpu.VMEM((wide, wide), BF16),
-            pltpu.VMEM((wide, wide), BF16),
-            pltpu.VMEM((height // 2, 2 * wide), BF16),
+            pltpu.VMEM((groups, wide, wide), BF16),
+            pltpu.VMEM((groups, wide, wide), BF16),
+            pltpu.VMEM((groups, 2, height // 2, wide), BF16),
+            pltpu.VMEM((groups, height // 2, 2 * wide), BF16),
         ],
         compiler_params=pltpu.CompilerParams(vmem_limit_bytes=40 * MIB),
         cost_estimate=pl.CostEstimate(

time: 98.7 us -> 97.2 us (0.985)
  Pallas kernels: 18.4 us -> 16.9 us
where the time goes in v3:
time: 97.2 us; the launch traced here: 97 us
  blocking collectives  76.2 us (78%)
  Pallas kernels  16.9 us (17%)
  starting transfers between devices  2.27 us (2%)
  waiting for transfers between devices  1.28 us (1%)
    all_to_all x2, blocking collectives, exchange(): lax.all_to_all(flat, ('blk', 'row'), split_axis=0, concat_axis=0, tiled=T...  76.2 us
    pallas_call x1, Pallas kernels, inverse_rows(): pl.pallas_call(functools.partial(inverse_kernel, chan_block, pitch), in_s...  4.75 us
    pallas_call x2, Pallas kernels, channel_stats(): pl.pallas_call(functools.partial(stats_kernel, which), in_specs=[pl.Block...  4.73 us
    pallas_call x2, Pallas kernels, forward_slice(): pl.pallas_call(functools.partial(forward_kernel, which, chan_block, pitch...  4.2 us
    pallas_call x1, Pallas kernels, filter_columns(): pl.pallas_call(filter_kernel, in_specs=[vmem] * 8, out_specs=vmem, out_sh...  3.24 us
    ppermute x2, starting transfers between devices, local(): other = [lax.ppermute(s, 'blk', swap) for s in own]  2.27 us
  transfers between devices with their start and end apart: 2, of which 1 were waited for; matrix products, arithmetic and copies ran while one was open for 0% of the time, Pallas kernels for 5%

profile of v3, /device:TPU:1, one launch (start us, length us, event | category | flops | bytes accessed | tf_op | source)
XLA Modules:
  0.0 97.0 jit_solution(15127771759400177004)
XLA Ops:
  0.0 2.4 %channel_stats.3 = (bf16[128,16,1024]{2,1,0:T(8,128)(2,1)S(1)}, bf16[3,16,1024]{2,1,0:T(8,128)(2,1)S(1)}) custom-call(bf16[2,128,16,1024]{3,2,1,0:T(8,128)(2,1)} %x_ref.3), custom_call_target="tpu_custom_call" | custom-call | flops 10485760 | bytes 4194304 | tf_op jit(solution)/shard_map/channel_stats/pallas_call | solution.py:104
  2.4 0.0 copy-start
  2.4 0.0 copy-start.2
  2.4 2.1 %collective-permute-start.1 = (bf16[3,16,1024]{2,1,0:T(8,128)(2,1)S(1)}, bf16[3,16,1024]{2,1,0:T(8,128)(2,1)S(1)}, u32[]{:S(2)}, u32[]{:S(2)}) collective-permute-start(bf16[3,16,1024]{2,1,0:T(8,128)(2,1)S(1)} %get-tuple-element.12.own_ref), channel_id=1, source_target_pairs={{0,1},{1,0},{2,3},{3,2},{4,5},{5,4},{6,7},{7,6},{8,9},{9,8},{10,11... | collective-permute-start | bytes 294920 | tf_op jit(solution)/shard_map/ppermute | solution.py:389
  4.5 2.4 %channel_stats.2 = (bf16[128,16,1024]{2,1,0:T(8,128)(2,1)S(1)}, bf16[3,16,1024]{2,1,0:T(8,128)(2,1)S(1)}) custom-call(bf16[2,128,16,1024]{3,2,1,0:T(8,128)(2,1)} %x_ref.3), custom_call_target="tpu_custom_call" | custom-call | flops 10485760 | bytes 4194304 | tf_op jit(solution)/shard_map/channel_stats/pallas_call | solution.py:104
  6.9 0.2 collective-permute-start
  7.0 0.0 collective-permute-done.1.other_ref
  7.0 0.0 copy-done
  7.1 2.1 %norm_and_row_dft.2.rest_0_ = bf16[2,64,32,256]{3,2,1,0:T(8,128)(2,1)S(1)} custom-call(bf16[128,16,1024]{2,1,0:T(8,128)(2,1)S(1)} %get-tuple-element.11.x_ref, f32[1,128]{1,0:T(1,128)S(1)} %bitcast.11, bf16[3,16,1024]{2,1,0:T(8,128)(2,1)S(1)} %get-tuple-element.12.own_ref, bf16[3,16,1024]{2,1,0:T(8,128)(2,1)S(1)} %collective-permute-done.1.other_ref, ...), custom_call_target="tpu_custom_call" | custom-call | flops 1073741824 | bytes 4194304 | tf_op jit(solution)/shard_map/norm_and_row_dft/pallas_call | solution.py:169
  9.2 1.3 %collective-permute-done.other_ref = bf16[3,16,1024]{2,1,0:T(8,128)(2,1)S(1)} collective-permute-done((bf16[3,16,1024]{2,1,0:T(8,128)(2,1)S(1)}, bf16[3,16,1024]{2,1,0:T(8,128)(2,1)S(1)}, u32[]{:S(2)}, u32[]{:S(2)}) %collective-permute-start) | collective-permute-done | bytes 98336 | tf_op jit(solution)/shard_map/ppermute | solution.py:389
  10.4 2.1 %norm_and_row_dft.3 = bf16[2,64,32,256]{3,2,1,0:T(8,128)(2,1)S(1)} custom-call(bf16[128,16,1024]{2,1,0:T(8,128)(2,1)S(1)} %get-tuple-element.9.x_ref, f32[1,128]{1,0:T(1,128)S(1)} %bitcast.12, bf16[3,16,1024]{2,1,0:T(8,128)(2,1)S(1)} %get-tuple-element.10.own_ref, ...), custom_call_target="tpu_custom_call", output_to_operand_aliasing={{}: (5, {})} | custom-call | flops 1073741824 | bytes 4194304 | tf_op jit(solution)/shard_map/norm_and_row_dft/pallas_call | solution.py:169
  12.5 0.0 copy-start.3
  12.6 0.0 copy-start.4
  12.6 0.0 copy-start.5
  12.6 0.0 copy-start.6
  12.6 0.0 copy-start.7
  12.6 0.0 copy-start.8
  12.6 0.0 copy-start.9
  12.6 41.8 %all_to_all.10 = bf16[128,32,256]{2,1,0:T(8,128)(2,1)S(1)} all-to-all(bf16[128,32,256]{2,1,0:T(8,128)(2,1)S(1)} %bitcast.7), channel_id=1, replica_groups=mesh['row'=64,'blk'=2] {'blk','row'}, dimensions={0} | all-to-all | bytes 4194304 | tf_op jit(solution)/shard_map/all_to_all | solution.py:374
  54.4 0.0 copy-done.6
  54.5 3.2 %column_filter.1 = bf16[2,64,32,256]{3,2,1,0:T(8,128)(2,1)S(1)} custom-call(bf16[2,64,32,256]{3,2,1,0:T(8,128)(2,1)S(1)} %bitcast.9, bf16[528,1024]{1,0:T(8,128)(2,1)S(1)} %copy-done.7, bf16[1024,512]{1,0:T(8,128)(2,1)S(1)} %copy-done.8, bf16[32,128]{1,0:T(8,128)(2,1)S(1)} %copy-done.9, bf16[2,256,32]{2,1,0:T(8,128)(2,1)S(1)} %bitcast.13, ...), custom_call_target="tpu_custom_call" | custom-call | flops 3221225472 | bytes 8388608 | tf_op jit(solution)/shard_map/column_filter/pallas_call | solution.py:288
  57.7 0.0 copy-start.1
  57.7 34.4 %all_to_all.11 = bf16[128,32,256]{2,1,0:T(8,128)(2,1)S(1)} all-to-all(bf16[128,32,256]{2,1,0:T(8,128)(2,1)S(1)} %bitcast.10), channel_id=1, replica_groups=mesh['row'=64,'blk'=2] {'blk','row'}, dimensions={0} | all-to-all | bytes 4194304 | tf_op jit(solution)/shard_map/all_to_all | solution.py:374
  92.1 4.7 %inverse_row_dft.1 = bf16[2,128,16,1024]{3,2,1,0:T(8,128)(2,1)} custom-call(bf16[2,64,32,256]{3,2,1,0:T(8,128)(2,1)S(1)} %bitcast.8, bf16[256,1024]{1,0:T(8,128)(2,1)S(1)} %copy-done.1), custom_call_target="tpu_custom_call" | custom-call | flops 2147483648 | bytes 8388608 | tf_op jit(solution)/shard_map/inverse_row_dft/pallas_call | solution.py:350
  (8 shorter events, 0.0 us)
Async XLA Ops:
  2.4 4.7 %copy-start = (bf16[1024,256]{1,0:T(8,128)(2,1)S(1)}, bf16[1024,256]{1,0:T(8,128)(2,1)}, u32[]{:S(2)}) copy-start(bf16[1024,256]{1,0:T(8,128)(2,1)} %constant.11.clone.table_ref) | copy-start | bytes 1572868
  2.4 4.7 %copy-start.2 = (f32[128]{0:T(128)S(1)}, f32[128]{0:T(128)}, u32[]{:S(2)}) copy-start(f32[128]{0:T(128)} %param.12) | copy-start | bytes 1540
  2.4 4.6 %collective-permute-start.1 = (bf16[3,16,1024]{2,1,0:T(8,128)(2,1)S(1)}, bf16[3,16,1024]{2,1,0:T(8,128)(2,1)S(1)}, u32[]{:S(2)}, u32[]{:S(2)}) collective-permute-start(bf16[3,16,1024]{2,1,0:T(8,128)(2,1)S(1)} %get-tuple-element.12.own_ref), channel_id=1, source_target_pairs={{0,1},{1,0},{2,3},{3,2},{4,5},{5,4},{6,7},{7,6},{8,9},{9,8},{10,11... | collective-permute-start | bytes 294920 | tf_op jit(solution)/shard_map/ppermute | solution.py:389
  6.9 3.5 %collective-permute-start = (bf16[3,16,1024]{2,1,0:T(8,128)(2,1)S(1)}, bf16[3,16,1024]{2,1,0:T(8,128)(2,1)S(1)}, u32[]{:S(2)}, u32[]{:S(2)}) collective-permute-start(bf16[3,16,1024]{2,1,0:T(8,128)(2,1)S(1)} %get-tuple-element.10.own_ref), channel_id=1, source_target_pairs={{0,1},{1,0},{2,3},{3,2},{4,5},{5,4},{6,7},{7,6},{8,9},{9,8},{10,11... | collective-permute-start | bytes 294920 | tf_op jit(solution)/shard_map/ppermute | solution.py:389
  12.5 41.9 %copy-start.3 = (bf16[2,8,32,32]{3,2,1,0:T(8,128)(2,1)S(1)}, bf16[2,8,32,32]{3,2,1,0:T(8,128)(2,1)}, u32[]{:S(2)}) copy-start(bf16[2,8,32,32]{3,2,1,0:T(8,128)(2,1)} %param.13) | copy-start | bytes 98308
  12.6 41.9 %copy-start.4 = (bf16[2,8,32,32]{3,2,1,0:T(8,128)(2,1)S(1)}, bf16[2,8,32,32]{3,2,1,0:T(8,128)(2,1)}, u32[]{:S(2)}) copy-start(bf16[2,8,32,32]{3,2,1,0:T(8,128)(2,1)} %param.15) | copy-start | bytes 98308
  12.6 41.9 %copy-start.5 = (f32[2,256]{1,0:T(2,128)S(1)}, f32[2,256]{1,0:T(2,128)}, u32[]{:S(2)}) copy-start(f32[2,256]{1,0:T(2,128)} %b1_ref.1) | copy-start | bytes 6148
  12.6 41.9 %copy-start.6 = (f32[2,256]{1,0:T(2,128)S(1)}, f32[2,256]{1,0:T(2,128)}, u32[]{:S(2)}) copy-start(f32[2,256]{1,0:T(2,128)} %b2_ref.1) | copy-start | bytes 6148
  12.6 41.9 %copy-start.7 = (bf16[528,1024]{1,0:T(8,128)(2,1)S(1)}, bf16[528,1024]{1,0:T(8,128)(2,1)}, u32[]{:S(2)}) copy-start(bf16[528,1024]{1,0:T(8,128)(2,1)} %constant.12.clone.fwd_ref) | copy-start | bytes 3244036
  12.6 41.9 %copy-start.8 = (bf16[1024,512]{1,0:T(8,128)(2,1)S(1)}, bf16[1024,512]{1,0:T(8,128)(2,1)}, u32[]{:S(2)}) copy-start(bf16[1024,512]{1,0:T(8,128)(2,1)} %constant.13.clone.inv_ref) | copy-start | bytes 3145732
  12.6 41.9 %copy-start.9 = (bf16[32,128]{1,0:T(8,128)(2,1)S(1)}, bf16[32,128]{1,0:T(8,128)(2,1)}, u32[]{:S(2)}) copy-start(bf16[32,128]{1,0:T(8,128)(2,1)} %constant.10.clone.spread_ref) | copy-start | bytes 24580
  57.7 34.4 %copy-start.1 = (bf16[256,1024]{1,0:T(8,128)(2,1)S(1)}, bf16[256,1024]{1,0:T(8,128)(2,1)}, u32[]{:S(2)}) copy-start(bf16[256,1024]{1,0:T(8,128)(2,1)} %constant.14.clone.table_ref) | copy-start | bytes 1572868

commit v4 on v3

v4 whole, which is shorter than its diff:
```python
import functools
import math

import jax
import jax.numpy as jnp
import ml_dtypes
import numpy as np
from jax import lax
from jax.experimental import pallas as pl
from jax.experimental.pallas import tpu as pltpu
from jax.sharding import PartitionSpec as P

BLOCK_CH = 32
EPS = 1e-05
SHRINK = 0.01
LANES = 128
BF16 = jnp.bfloat16
F32 = jnp.float32
MIB = 1 << 20


def _angles(first, second, count):
    phase = np.mod(np.outer(first, second), count)
    return phase.astype(np.float32) * np.float32(2.0 * math.pi / count)


def _bf16(values):
    return np.asarray(values, np.float32).astype(ml_dtypes.bfloat16)


def mode_order(modes):
    return np.arange(modes).reshape(-1, 2).T.reshape(-1)


def forward_table(count, modes):
    t = _angles(np.arange(count), mode_order(modes), count)
    scale = np.float32(1.0 / math.sqrt(count))
    return _bf16(np.concatenate([np.cos(t) * scale, -np.sin(t) * scale], axis=1))


def inverse_table(count, modes):
    order = mode_order(modes)
    t = _angles(order, np.arange(count), count)
    weight = np.where(order == 0, 1.0, 2.0)[:, None].astype(np.float32)
    weight = weight * np.float32(1.0 / math.sqrt(count))
    both = np.stack([np.cos(t) * weight, -np.sin(t) * weight])
    both = both.reshape(2, 2, modes // 2, count).transpose(1, 0, 2, 3)
    return _bf16(both.reshape(2 * modes, count))


def height_tables(height):
    quarter = height // 4
    s = _angles(np.arange(quarter + 1), np.arange(height), height)
    scale = np.float32(1.0 / math.sqrt(height))
    cosine, sine = np.cos(s) * scale, np.sin(s) * scale
    last = np.zeros((16, height), np.float32)
    last[0], last[1] = cosine[quarter], sine[quarter]
    forward = np.concatenate([cosine[:quarter], sine[:quarter], last], axis=0)
    inverse = np.concatenate([cosine[:quarter].T, sine[:quarter].T], axis=1)
    return _bf16(forward), _bf16(inverse)


STEP = 16


def copies_of(segments, x_ref, held_refs, sems):
    found = []
    taken = 0
    for (which, first, lanes), ref in zip(segments, held_refs):
        channels, _, width = x_ref.shape[1], x_ref.shape[2], x_ref.shape[3]
        size = STEP * max(1, width // lanes)
        copies = []
        for c in range(0, channels, size):
            part = pl.ds(c, size)
            source = x_ref.at[which, part, :, pl.ds(first, lanes)]
            copies.append(pltpu.make_async_copy(source, ref.at[part], sems.at[taken]))
            taken += 1
        found.append((copies, size))
    return found


def stats_kernel(segments, x_ref, *refs):
    held_refs = refs[: len(segments)]
    stat_ref, pivot_s, first_s, second_s, sems = refs[len(segments) :]
    channels = x_ref.shape[1]
    rows = x_ref.shape[2]
    segment_copies = copies_of(segments, x_ref, held_refs, sems)
    for copies, _ in segment_copies:
        for copy in copies:
            copy.start()
    base = 0
    for (_, _, lanes), ref, (copies, size) in zip(segments, held_refs, segment_copies):
        wide = 512 if lanes % 512 == 0 else min(256, lanes)
        for at in range(0, channels, STEP):
            if at % size == 0:
                copies[at // size].wait()
            for lane in range(0, lanes, wide):
                there = slice(lane, lane + wide)
                here = slice(base + lane, base + lane + wide)
                if at == 0:
                    pivot = jnp.zeros((rows, wide), F32)
                    for c in range(STEP):
                        pivot = pivot + ref[c, :, there].astype(F32)
                    pivot = (pivot * (1.0 / STEP)).astype(BF16)
                    pivot_s[:, here] = pivot
                    first = jnp.zeros((rows, wide), F32)
                    second = jnp.zeros((rows, wide), F32)
                else:
                    pivot, first, second = pivot_s[:, here], first_s[:, here], second_s[:, here]
                for c in range(at, at + STEP, 2):
                    one = ref[c, :, there] - pivot
                    two = ref[c + 1, :, there] - pivot
                    first = first + (one + two).astype(F32)
                    second = second + (one * one + two * two).astype(F32)
                if at + STEP < channels:
                    first_s[:, here], second_s[:, here] = first, second
                else:
                    offset = first * (1.0 / channels)
                    mean = pivot.astype(F32) + offset
                    high = mean.astype(BF16)
                    stat_ref[0, :, here] = high
                    stat_ref[1, :, here] = (mean - high.astype(F32)).astype(BF16)
                    stat_ref[2, :, here] = jnp.maximum(second - first * offset, 0.0).astype(BF16)
        base += lanes


def channel_stats(field, segments):
    _, channels, rows, width = field.shape
    total = sum(lanes for _, _, lanes in segments)
    count = sum(channels // (STEP * max(1, width // lanes)) for _, _, lanes in segments)
    vmem = pl.BlockSpec(memory_space=pltpu.VMEM)
    *held, stat = pl.pallas_call(
        functools.partial(stats_kernel, segments),
        in_specs=[pl.BlockSpec(memory_space=pltpu.HBM)],
        out_specs=[vmem] * (len(segments) + 1),
        out_shape=[jax.ShapeDtypeStruct((channels, rows, lanes), BF16) for _, _, lanes in segments]
        + [jax.ShapeDtypeStruct((3, rows, total), BF16)],
        scratch_shapes=[
            pltpu.VMEM((rows, total), BF16),
            pltpu.VMEM((rows, total), F32),
            pltpu.VMEM((rows, total), F32),
            pltpu.SemaphoreType.DMA((count,)),
        ],
        compiler_params=pltpu.CompilerParams(vmem_limit_bytes=16 * MIB),
        cost_estimate=pl.CostEstimate(
            flops=5 * channels * rows * total, bytes_accessed=2 * channels * rows * total, transcendentals=0
        ),
        name="channel_stats",
    )(pltpu.with_memory_space_constraint(field, pltpu.HBM))
    return held, stat


def normalizer(own_ref, other_ref, here, channels):
    own_mean = own_ref[0, :, here].astype(F32) + own_ref[1, :, here].astype(F32)
    other_mean = other_ref[0, :, here].astype(F32) + other_ref[1, :, here].astype(F32)
    delta = own_mean - other_mean
    moment = own_ref[2, :, here].astype(F32) + other_ref[2, :, here].astype(F32) + delta * delta * (channels * 0.5)
    return (own_mean + other_mean) * 0.5, lax.rsqrt(moment * (0.5 / channels) + EPS)


def project(x_ref, stats, table_ref, first_row, pitch, add_ref, spec_ref, chan_block=32):
    channels, rows, lanes = x_ref.shape
    parts, _, half = spec_ref.shape
    mean, scale = stats
    table = table_ref[first_row : first_row + lanes, :]
    for first in range(0, channels, chan_block):
        field = x_ref[first : first + chan_block].astype(F32)
        normed = ((field - mean[None]) * scale[None]).astype(BF16)
        spec = jnp.dot(normed.reshape(chan_block * rows, lanes), table, preferred_element_type=F32)
        for c in range(chan_block):
            start = (first + c) * pitch
            for p in range(parts):
                value = spec[c * rows : (c + 1) * rows, p * half : (p + 1) * half]
                if add_ref is not None:
                    value = value + add_ref[p, start : start + rows, :]
                spec_ref[p, start : start + rows, :] = value


def hand_out(which, gain_ref, spec_s, turn_s, send_ref, rows, pitch):
    parts, _, half = spec_s.shape
    channels = turn_s.shape[-1]
    owners = send_ref.shape[1]
    for h in range(rows):
        for p in range(parts):
            turned = spec_s[p, pl.ds(h, channels, stride=pitch), :].T * gain_ref[...]
            turn_s[pl.ds(p * half * pitch + h, half, stride=pitch), :] = turned
    for r in range(2):
        for kk in range(2):
            for d in range(owners):
                start = ((r * 2 + kk) * owners + d) * pitch
                send_ref[which, d, r * rows : (r + 1) * rows, kk * channels : (kk + 1) * channels] = turn_s[
                    start : start + rows, :
                ].astype(BF16)


def forward_first(pitch, x_ref, early_ref, gain_ref, own_ref, other_ref, table_ref, send_ref, part_ref, spec_s, turn_s):
    channels, rows, width = x_ref.shape
    cut = early_ref.shape[2]
    project(x_ref, normalizer(own_ref, other_ref, slice(0, width), channels), table_ref, 0, pitch, None, spec_s)
    hand_out(0, gain_ref, spec_s, turn_s, send_ref, rows, pitch)
    stats = normalizer(own_ref, other_ref, slice(width, width + cut), channels)
    project(early_ref, stats, table_ref, 0, pitch, None, part_ref)


def forward_second(pitch, x_ref, gain_ref, own_ref, other_ref, table_ref, part_ref, _, send_ref, spec_s, turn_s):
    channels, rows, lanes = x_ref.shape
    cut = table_ref.shape[0] - lanes
    stats = normalizer(own_ref, other_ref, slice(0, lanes), channels)
    project(x_ref, stats, table_ref, cut, pitch, part_ref, spec_s)
    hand_out(1, gain_ref, spec_s, turn_s, send_ref, rows, pitch)


def forward_rows(kernel, held, gain, own, other, table, owners, more=()):
    channels, rows, _ = held[0].shape
    width, two_k = table.shape
    pitch = rows + 8
    vmem = pl.BlockSpec(memory_space=pltpu.VMEM)
    send = jax.ShapeDtypeStruct((2, owners, 2 * rows, 2 * channels), BF16)
    part = jax.ShapeDtypeStruct((2, channels * pitch, two_k // 2), F32)
    lanes = sum(x.shape[2] for x in held)
    return pl.pallas_call(
        functools.partial(kernel, pitch),
        in_specs=[vmem] * (len(held) + 4 + len(more)),
        out_specs=vmem if more else [vmem, vmem],
        out_shape=send if more else [send, part],
        scratch_shapes=[
            pltpu.VMEM((2, channels * pitch, two_k // 2), F32),
            pltpu.VMEM((two_k * pitch, channels), F32),
        ],
        input_output_aliases={len(held) + 5: 0} if more else {},
        compiler_params=pltpu.CompilerParams(vmem_limit_bytes=24 * MIB),
        cost_estimate=pl.CostEstimate(
            flops=2 * channels * rows * lanes * two_k, bytes_accessed=2 * channels * rows * lanes, transcendentals=0
        ),
        name="norm_and_row_dft",
    )(*held, gain.reshape(1, channels), own, other, table, *more)


def block_diagonal(weights, spread, lanes):
    tiled = jnp.dot(weights, spread, preferred_element_type=F32)
    row = lax.broadcasted_iota(jnp.int32, (lanes, lanes), 0) // BLOCK_CH
    col = lax.broadcasted_iota(jnp.int32, (lanes, lanes), 1) // BLOCK_CH
    return jnp.where(row == col, tiled, 0.0)


def fill_weights(w_ref, group, spread, big, lanes, turned=None):
    mine = slice(group * lanes, (group + 1) * lanes)
    real = block_diagonal(w_ref[0, mine, :], spread, lanes)
    imag = block_diagonal(w_ref[1, mine, :], spread, lanes)
    for target, shift in ((big, 0), (turned, lanes // 2)):
        if target is not None:
            re = pltpu.roll(real, shift, 1) if shift else real
            im = pltpu.roll(imag, shift, 1) if shift else imag
            target[:lanes, :lanes] = re.astype(BF16)
            target[:lanes, lanes:] = im.astype(BF16)
            target[lanes:, :lanes] = (-im).astype(BF16)
            target[lanes:, lanes:] = re.astype(BF16)


def bias_row(b_ref, group, lanes, shift=0):
    mine = slice(group * lanes, (group + 1) * lanes)
    both = [b_ref[0:1, mine], b_ref[1:2, mine]]
    if shift:
        both = [pltpu.roll(b, shift, 1) for b in both]
    return jnp.concatenate(both, axis=1)


def filter_kernel(x_ref, fwd_ref, inv_ref, spread_ref, w1_ref, b1_ref, w2_ref, b2_ref, out_ref, big1, big2, big2_turned, spec_s, packed):
    groups, owners, two_rows, wide = x_ref.shape
    rows = two_rows // 2
    lanes = wide // 2
    height = owners * rows
    quarter = height // 4
    top = lax.broadcasted_iota(jnp.int32, (quarter, lanes), 0) == 0
    turn = lax.broadcasted_iota(jnp.int32, (8, 1), 0) % 4
    norm = 1.0 / math.sqrt(height)
    last_cos = jnp.where(turn == 0, norm, jnp.where(turn == 2, -norm, 0.0))
    last_sin = jnp.where(turn == 1, norm, jnp.where(turn == 3, -norm, 0.0))
    real_part = lambda kk: slice(kk * lanes, (kk + 1) * lanes)

    def transform(group):
        real_in = x_ref[group, :, :rows, :].reshape(height, wide)
        imag_in = x_ref[group, :, rows:, :].reshape(height, wide)
        from_real = jnp.dot(fwd_ref[...], real_in, preferred_element_type=F32)
        from_imag = jnp.dot(fwd_ref[...], imag_in, preferred_element_type=F32)
        last = slice(2 * quarter, 2 * quarter + 1)
        last_sine = slice(2 * quarter + 1, 2 * quarter + 2)
        for kk in range(2):
            part = real_part(kk)
            cos_re, sin_re = from_real[:quarter, part], from_real[quarter : 2 * quarter, part]
            cos_im, sin_im = from_imag[:quarter, part], from_imag[quarter : 2 * quarter, part]
            last_re = from_real[last, part] - from_imag[last_sine, part]
            last_im = from_imag[last, part] + from_real[last_sine, part]
            spec_s[group, kk, :quarter, :lanes] = (cos_re + sin_im).astype(BF16)
            spec_s[group, kk, :quarter, lanes:] = (cos_im - sin_re).astype(BF16)
            spec_s[group, kk, quarter:, :lanes] = jnp.where(top, last_re, cos_re - sin_im).astype(BF16)
            spec_s[group, kk, quarter:, lanes:] = jnp.where(top, last_im, cos_im + sin_re).astype(BF16)

    def mix(group):
        values, extras = [], []
        for kk in range(2):
            shift = kk * (lanes // 2)
            second = (big2 if kk == 0 else big2_turned)[group]
            hidden = jnp.dot(spec_s[group, kk], big1[group], preferred_element_type=F32) + bias_row(b1_ref, group, lanes)
            hidden = jnp.maximum(hidden, 0.0).astype(BF16)
            mixed = jnp.dot(hidden, second, preferred_element_type=F32) + bias_row(b2_ref, group, lanes, shift)
            kept = mixed - jnp.clip(mixed, -SHRINK, SHRINK)
            plus_re, plus_im = kept[:quarter, :lanes], kept[:quarter, lanes:]
            minus_re, minus_im = kept[quarter:, :lanes], kept[quarter:, lanes:]
            last_re, last_im = minus_re[0:1], minus_im[0:1]
            minus_re = jnp.where(top, 0.0, minus_re)
            minus_im = jnp.where(top, 0.0, minus_im)
            values.append([plus_re + minus_re, plus_im + minus_im, minus_im - plus_im, plus_re - minus_re])
            extras.append([last_cos * last_re + last_sin * last_im, last_cos * last_im - last_sin * last_re])

        def halves(zero, one):
            low = lax.broadcasted_iota(jnp.int32, zero.shape, 1) < lanes // 2
            return jnp.where(low, zero, one), jnp.where(low, one, zero)

        for i, (zero, one) in enumerate(zip(*values)):
            for half, value in enumerate(halves(zero, one)):
                start = (i % 2) * wide + half * lanes
                packed[group, (i // 2) * quarter : (i // 2 + 1) * quarter, start : start + lanes] = value.astype(BF16)
        return jnp.concatenate([part for zero, one in zip(*extras) for part in halves(zero, one)], axis=1)

    def invert(group, extra):
        column = jnp.dot(inv_ref[...], packed[group], preferred_element_type=F32)
        column = (column.reshape(height // 8, 8, 2 * wide) + extra[None]).astype(BF16)
        column = column.reshape(height, 2 * wide)
        out_ref[group, :, :rows, :] = column[:, :wide].reshape(owners, rows, wide)
        out_ref[group, :, rows:, :] = column[:, wide:].reshape(owners, rows, wide)

    for group in range(groups):
        fill_weights(w1_ref, group, spread_ref[...], big1.at[group], lanes)
        fill_weights(w2_ref, group, spread_ref[...], big2.at[group], lanes, big2_turned.at[group])
    for group in range(groups):
        transform(group)
    extra = [mix(group) for group in range(groups)]
    for group in range(groups):
        invert(group, extra[group])


def filter_columns(received, fwd, inv, spread, w_first, b_first, w_second, b_second):
    groups, owners, two_rows, wide = received.shape
    height = owners * two_rows // 2
    vmem = pl.BlockSpec(memory_space=pltpu.VMEM)

    def flat(w):
        return w.reshape(2, -1, BLOCK_CH)

    return pl.pallas_call(
        filter_kernel,
        in_specs=[vmem] * 8,
        out_specs=vmem,
        out_shape=jax.ShapeDtypeStruct(received.shape, BF16),
        scratch_shapes=[
            pltpu.VMEM((groups, wide, wide), BF16),
            pltpu.VMEM((groups, wide, wide), BF16),
            pltpu.VMEM((groups, wide, wide), BF16),
            pltpu.VMEM((groups, 2, height // 2, wide), BF16),
            pltpu.VMEM((groups, height // 2, 2 * wide), BF16),
        ],
        compiler_params=pltpu.CompilerParams(vmem_limit_bytes=40 * MIB),
        cost_estimate=pl.CostEstimate(
            flops=2 * groups * height * wide * 3 * height, bytes_accessed=8 * MIB, transcendentals=0
        ),
        name="column_filter",
    )(received, fwd, inv, spread, flat(w_first), b_first, flat(w_second), b_second)


def inverse_kernel(chan_block, pitch, x_ref, table_ref, out_ref, turn_s, spec_s, done_s, sems):
    slices, owners, two_rows, wide = x_ref.shape
    rows = two_rows // 2
    lanes = wide // 2
    part = lanes // 2
    copies = []
    for which in range(slices):
        for half in range(2):
            for r in range(2):
                for d in range(owners):
                    start = (r * owners + d) * pitch
                    turn_s[half, start : start + rows, :] = x_ref[
                        which, d, r * rows : (r + 1) * rows, half * lanes : (half + 1) * lanes
                    ].astype(F32)
            for h in range(rows):
                turned = turn_s[half, pl.ds(h, 2 * owners, stride=pitch), :].T
                for place in range(2):
                    kk = place if half == 0 else 1 - place
                    spec_s[kk, pl.ds(half * part * pitch + h, part, stride=pitch), :] = turned[
                        place * part : (place + 1) * part
                    ]
            for first in range(half * part, (half + 1) * part, chan_block):
                spec = []
                for c in range(first, first + chan_block):
                    start = c * pitch
                    both = [spec_s[kk, start : start + rows, :].astype(BF16) for kk in range(2)]
                    spec.append(jnp.concatenate(both, axis=1))
                mixed = jnp.dot(jnp.concatenate(spec, axis=0), table_ref[...], preferred_element_type=F32)
                block = pl.ds(first, chan_block)
                done_s[which, block] = mixed.astype(BF16).reshape(chan_block, rows, -1)
                copies.append(
                    pltpu.make_async_copy(done_s.at[which, block], out_ref.at[which, block], sems.at[len(copies)])
                )
                copies[-1].start()
    for copy in copies:
        copy.wait()


def inverse_rows(received, table):
    slices, owners, two_rows, wide = received.shape
    rows = two_rows // 2
    channels = wide // 2
    two_k, width = table.shape
    chan_block = min(16, channels)
    pitch = rows + 8
    vmem = pl.BlockSpec(memory_space=pltpu.VMEM)
    return pl.pallas_call(
        functools.partial(inverse_kernel, chan_block, pitch),
        in_specs=[vmem, vmem],
        out_specs=pl.BlockSpec(memory_space=pltpu.HBM),
        out_shape=jax.ShapeDtypeStruct((slices, channels, rows, width), BF16),
        scratch_shapes=[
            pltpu.VMEM((2, two_k // 2 * pitch, channels), F32),
            pltpu.VMEM((2, channels * pitch, two_k // 2), F32),
            pltpu.VMEM((slices, channels, rows, width), BF16),
            pltpu.SemaphoreType.DMA((slices * channels // chan_block,)),
        ],
        compiler_params=pltpu.CompilerParams(vmem_limit_bytes=40 * MIB),
        cost_estimate=pl.CostEstimate(
            flops=2 * slices * channels * rows * width * two_k,
            bytes_accessed=2 * slices * channels * rows * width,
            transcendentals=0,
        ),
        name="inverse_row_dft",
    )(received, table)


def exchange(blocks):
    shape = blocks.shape
    flat = blocks.reshape((shape[0] * shape[1],) + shape[2:])
    flat = lax.all_to_all(flat, ("blk", "row"), split_axis=0, concat_axis=0, tiled=True)
    return flat.reshape(shape)


def local(field, gain, w_first, b_first, w_second, b_second):
    slices, channels, rows, width = field.shape
    owners = lax.axis_size("row")
    modes_x = 2 * owners
    height = owners * rows
    fwd, inv = height_tables(height)
    spread = jnp.asarray(np.tile(np.eye(BLOCK_CH), (1, channels // BLOCK_CH)), BF16)
    table = jnp.asarray(forward_table(width, modes_x))

    swap = [(0, 1), (1, 0)]
    cut = width // 4
    groups = (((0, 0, width), (1, 0, cut)), ((1, cut, width - cut),))
    (held_first, own_first), (held_second, own_second) = [channel_stats(field, group) for group in groups]
    other_first = lax.ppermute(own_first, "blk", swap)
    other_second = lax.ppermute(own_second, "blk", swap)
    send, part = forward_rows(forward_first, held_first, gain, own_first, other_first, table, owners)
    send = forward_rows(
        forward_second, held_second, gain, own_second, other_second, table, owners, (part, send)
    )
    columns = exchange(send)
    filtered = filter_columns(
        columns, jnp.asarray(fwd), jnp.asarray(inv), spread, w_first, b_first, w_second, b_second
    )
    colfield = exchange(filtered)
    return inverse_rows(colfield, jnp.asarray(inverse_table(width, modes_x)))


def solution(mesh):
    return jax.shard_map(
        local,
        mesh=mesh,
        in_specs=(P(None, "blk", "row", None), P("blk"), P(), P(), P(), P()),
        out_specs=P(None, "blk", "row", None),
        check_vma=False,
    )
```

time: 97.2 us -> 96.5 us (level)
  transfers between devices with their start and end apart: 2 -> 2, of which waited for: 1 -> 2; matrix products, arithmetic and copies ran while one was open for 0% -> 0% of each run, Pallas kernels for 5% -> 5%
where the time goes in v4:
time: 96.5 us; the launch traced here: 96.3 us
  blocking collectives  76.2 us (79%)
  Pallas kernels  16.9 us (18%)
  starting transfers between devices  2.27 us (2%)
    all_to_all x2, blocking collectives, exchange(): lax.all_to_all(flat, ('blk', 'row'), split_axis=0, concat_axis=0, tiled=T...  76.2 us
    pallas_call x2, Pallas kernels, channel_stats(): pl.pallas_call(functools.partial(stats_kernel, segments), in_specs=[pl.Bl...  4.69 us
    pallas_call x2, Pallas kernels, forward_rows(): pl.pallas_call(functools.partial(kernel, pitch), in_specs=[vmem] * (len(h...  4.46 us
    pallas_call x1, Pallas kernels, inverse_rows(): pl.pallas_call(functools.partial(inverse_kernel, chan_block, pitch), in_s...  4.44 us
    pallas_call x1, Pallas kernels, filter_columns(): pl.pallas_call(filter_kernel, in_specs=[vmem] * 8, out_specs=vmem, out_sh...  3.29 us
    ppermute x1, starting transfers between devices, local(): other_first = lax.ppermute(own_first, 'blk', swap)  2.12 us
  transfers between devices with their start and end apart: 2, of which 2 were waited for; matrix products, arithmetic and copies ran while one was open for 0% of the time, Pallas kernels for 5%

profile of v4, /device:TPU:1, one launch (start us, length us, event | category | flops | bytes accessed | tf_op | source)
XLA Modules:
  0.0 96.3 jit_solution(15385042426709876168)
XLA Ops:
  0.0 2.7 %channel_stats.3 = (bf16[128,16,1024]{2,1,0:T(8,128)(2,1)S(1)}, bf16[128,16,256]{2,1,0:T(8,128)(2,1)S(1)}, bf16[3,16,1280]{2,1,0:T(8,128)(2,1)S(1)}) custom-call(bf16[2,128,16,1024]{3,2,1,0:T(8,128)(2,1)} %x_ref.3), custom_call_target="tpu_custom_call" | custom-call | flops 13107200 | bytes 5242880 | tf_op jit(solution)/shard_map/channel_stats/pallas_call | solution.py:132
  2.7 0.0 copy-start
  2.7 0.0 copy-start.2
  2.7 2.1 %collective-permute-start.1 = (bf16[3,16,1280]{2,1,0:T(8,128)(2,1)S(1)}, bf16[3,16,1280]{2,1,0:T(8,128)(2,1)S(1)}, u32[]{:S(2)}, u32[]{:S(2)}) collective-permute-start(bf16[3,16,1280]{2,1,0:T(8,128)(2,1)S(1)} %get-tuple-element.16.own_ref), channel_id=1, source_target_pairs={{0,1},{1,0},{2,3},{3,2},{4,5},{5,4},{6,7},{7,6},{8,9},{9,8},{10,11... | collective-permute-start | bytes 368648 | tf_op jit(solution)/shard_map/ppermute | solution.py:458
  4.8 2.0 %channel_stats.2 = (bf16[128,16,768]{2,1,0:T(8,128)(2,1)S(1)}, bf16[3,16,768]{2,1,0:T(8,128)(2,1)S(1)}) custom-call(bf16[2,128,16,1024]{3,2,1,0:T(8,128)(2,1)} %x_ref.3), custom_call_target="tpu_custom_call" | custom-call | flops 7864320 | bytes 3145728 | tf_op jit(solution)/shard_map/channel_stats/pallas_call | solution.py:132
  6.9 0.2 collective-permute-start
  7.0 0.1 collective-permute-done.1.other_ref
  7.1 0.0 copy-done.2
  7.1 2.5 %norm_and_row_dft.2 = (bf16[2,64,32,256]{3,2,1,0:T(8,128)(2,1)S(1)}, f32[2,3072,128]{2,1,0:T(8,128)S(1)}) custom-call(bf16[128,16,1024]{2,1,0:T(8,128)(2,1)S(1)} %get-tuple-element.14.x_ref, bf16[128,16,256]{2,1,0:T(8,128)(2,1)S(1)} %get-tuple-element.15.early_ref, f32[1,128]{1,0:T(1,128)S(1)} %bitcast.11, ...), custom_call_target="tpu_custom_call" | custom-call | flops 1342177280 | bytes 5242880 | tf_op jit(solution)/shard_map/norm_and_row_dft/pallas_call | solution.py:221
  9.7 0.5 collective-permute-done.other_ref
  10.1 1.9 %norm_and_row_dft.3 = bf16[2,64,32,256]{3,2,1,0:T(8,128)(2,1)S(1)} custom-call(bf16[128,16,768]{2,1,0:T(8,128)(2,1)S(1)} %get-tuple-element.12.x_ref, f32[1,128]{1,0:T(1,128)S(1)} %bitcast.12, bf16[3,16,768]{2,1,0:T(8,128)(2,1)S(1)} %get-tuple-element.13.own_ref, ...), custom_call_target="tpu_custom_call", output_to_operand_aliasing={{}: (6, {})} | custom-call | flops 805306368 | bytes 3145728 | tf_op jit(solution)/shard_map/norm_and_row_dft/pallas_call | solution.py:221
  12.1 0.0 copy-start.3
  12.1 0.0 copy-start.4
  12.1 0.0 copy-start.5
  12.1 0.0 copy-start.6
  12.1 0.0 copy-start.7
  12.1 0.0 copy-start.8
  12.2 0.0 copy-start.9
  12.2 41.8 %all_to_all.10 = bf16[128,32,256]{2,1,0:T(8,128)(2,1)S(1)} all-to-all(bf16[128,32,256]{2,1,0:T(8,128)(2,1)S(1)} %bitcast.7), channel_id=1, replica_groups=mesh['row'=64,'blk'=2] {'blk','row'}, dimensions={0} | all-to-all | bytes 4194304 | tf_op jit(solution)/shard_map/all_to_all | solution.py:441
  54.0 0.0 copy-done.5
  54.0 3.3 %column_filter.1 = bf16[2,64,32,256]{3,2,1,0:T(8,128)(2,1)S(1)} custom-call(bf16[2,64,32,256]{3,2,1,0:T(8,128)(2,1)S(1)} %bitcast.9, bf16[528,1024]{1,0:T(8,128)(2,1)S(1)} %copy-done.7, bf16[1024,512]{1,0:T(8,128)(2,1)S(1)} %copy-done.8, bf16[32,128]{1,0:T(8,128)(2,1)S(1)} %copy-done.9, bf16[2,256,32]{2,1,0:T(8,128)(2,1)S(1)} %bitcast.13, ...), custom_call_target="tpu_custom_call" | custom-call | flops 3221225472 | bytes 8388608 | tf_op jit(solution)/shard_map/column_filter/pallas_call | solution.py:351
  57.3 0.0 copy-start.1
  57.3 34.4 %all_to_all.11 = bf16[128,32,256]{2,1,0:T(8,128)(2,1)S(1)} all-to-all(bf16[128,32,256]{2,1,0:T(8,128)(2,1)S(1)} %bitcast.10), channel_id=1, replica_groups=mesh['row'=64,'blk'=2] {'blk','row'}, dimensions={0} | all-to-all | bytes 4194304 | tf_op jit(solution)/shard_map/all_to_all | solution.py:441
  91.7 4.4 %inverse_row_dft.1 = bf16[2,128,16,1024]{3,2,1,0:T(8,128)(2,1)} custom-call(bf16[2,64,32,256]{3,2,1,0:T(8,128)(2,1)S(1)} %bitcast.8, bf16[256,1024]{1,0:T(8,128)(2,1)S(1)} %copy-done.1), custom_call_target="tpu_custom_call" | custom-call | flops 2147483648 | bytes 8388608 | tf_op jit(solution)/shard_map/inverse_row_dft/pallas_call | solution.py:417
  (8 shorter events, 0.0 us)
Async XLA Ops:
  2.7 4.4 %copy-start = (bf16[1024,256]{1,0:T(8,128)(2,1)S(1)}, bf16[1024,256]{1,0:T(8,128)(2,1)}, u32[]{:S(2)}) copy-start(bf16[1024,256]{1,0:T(8,128)(2,1)} %constant.11.clone.table_ref) | copy-start | bytes 1572868
  2.7 4.4 %copy-start.2 = (f32[128]{0:T(128)S(1)}, f32[128]{0:T(128)}, u32[]{:S(2)}) copy-start(f32[128]{0:T(128)} %param.12) | copy-start | bytes 1540
  2.7 4.4 %collective-permute-start.1 = (bf16[3,16,1280]{2,1,0:T(8,128)(2,1)S(1)}, bf16[3,16,1280]{2,1,0:T(8,128)(2,1)S(1)}, u32[]{:S(2)}, u32[]{:S(2)}) collective-permute-start(bf16[3,16,1280]{2,1,0:T(8,128)(2,1)S(1)} %get-tuple-element.16.own_ref), channel_id=1, source_target_pairs={{0,1},{1,0},{2,3},{3,2},{4,5},{5,4},{6,7},{7,6},{8,9},{9,8},{10,11... | collective-permute-start | bytes 368648 | tf_op jit(solution)/shard_map/ppermute | solution.py:458
  6.9 3.3 %collective-permute-start = (bf16[3,16,768]{2,1,0:T(8,128)(2,1)S(1)}, bf16[3,16,768]{2,1,0:T(8,128)(2,1)S(1)}, u32[]{:S(2)}, u32[]{:S(2)}) collective-permute-start(bf16[3,16,768]{2,1,0:T(8,128)(2,1)S(1)} %get-tuple-element.13.own_ref), channel_id=1, source_target_pairs={{0,1},{1,0},{2,3},{3,2},{4,5},{5,4},{6,7},{7,6},{8,9},{9,8},{10,11... | collective-permute-start | bytes 221192 | tf_op jit(solution)/shard_map/ppermute | solution.py:459
  12.1 41.9 %copy-start.3 = (bf16[2,8,32,32]{3,2,1,0:T(8,128)(2,1)S(1)}, bf16[2,8,32,32]{3,2,1,0:T(8,128)(2,1)}, u32[]{:S(2)}) copy-start(bf16[2,8,32,32]{3,2,1,0:T(8,128)(2,1)} %param.13) | copy-start | bytes 98308
  12.1 41.9 %copy-start.4 = (bf16[2,8,32,32]{3,2,1,0:T(8,128)(2,1)S(1)}, bf16[2,8,32,32]{3,2,1,0:T(8,128)(2,1)}, u32[]{:S(2)}) copy-start(bf16[2,8,32,32]{3,2,1,0:T(8,128)(2,1)} %param.15) | copy-start | bytes 98308
  12.1 41.9 %copy-start.5 = (f32[2,256]{1,0:T(2,128)S(1)}, f32[2,256]{1,0:T(2,128)}, u32[]{:S(2)}) copy-start(f32[2,256]{1,0:T(2,128)} %b1_ref.1) | copy-start | bytes 6148
  12.1 41.9 %copy-start.6 = (f32[2,256]{1,0:T(2,128)S(1)}, f32[2,256]{1,0:T(2,128)}, u32[]{:S(2)}) copy-start(f32[2,256]{1,0:T(2,128)} %b2_ref.1) | copy-start | bytes 6148
  12.1 41.9 %copy-start.7 = (bf16[528,1024]{1,0:T(8,128)(2,1)S(1)}, bf16[528,1024]{1,0:T(8,128)(2,1)}, u32[]{:S(2)}) copy-start(bf16[528,1024]{1,0:T(8,128)(2,1)} %constant.12.clone.fwd_ref) | copy-start | bytes 3244036
  12.1 41.9 %copy-start.8 = (bf16[1024,512]{1,0:T(8,128)(2,1)S(1)}, bf16[1024,512]{1,0:T(8,128)(2,1)}, u32[]{:S(2)}) copy-start(bf16[1024,512]{1,0:T(8,128)(2,1)} %constant.13.clone.inv_ref) | copy-start | bytes 3145732
  12.2 41.9 %copy-start.9 = (bf16[32,128]{1,0:T(8,128)(2,1)S(1)}, bf16[32,128]{1,0:T(8,128)(2,1)}, u32[]{:S(2)}) copy-start(bf16[32,128]{1,0:T(8,128)(2,1)} %constant.10.clone.spread_ref) | copy-start | bytes 24580
  57.3 34.4 %copy-start.1 = (bf16[256,1024]{1,0:T(8,128)(2,1)S(1)}, bf16[256,1024]{1,0:T(8,128)(2,1)}, u32[]{:S(2)}) copy-start(bf16[256,1024]{1,0:T(8,128)(2,1)} %constant.14.clone.table_ref) | copy-start | bytes 1572868

commit v5 on v4

--- a/solution.py
+++ b/solution.py
@@ -13,7 +13,6 @@
 BLOCK_CH = 32
 EPS = 1e-05
 SHRINK = 0.01
-LANES = 128
 BF16 = jnp.bfloat16
 F32 = jnp.float32
 MIB = 1 << 20
@@ -174,16 +173,22 @@
                 if add_ref is not None:
                     value = value + add_ref[p, start : start + rows, :]
                 spec_ref[p, start : start + rows, :] = value
-
-
-def hand_out(which, gain_ref, spec_s, turn_s, send_ref, rows, pitch):
+        yield
+
+
+def hand_out(which, gain_ref, spec_s, turn_s, send_ref, rows, pitch, beside=()):
     parts, _, half = spec_s.shape
     channels = turn_s.shape[-1]
     owners = send_ref.shape[1]
+    beside = iter(beside)
     for h in range(rows):
+        if h % 4 == 0:
+            next(beside, None)
         for p in range(parts):
             turned = spec_s[p, pl.ds(h, channels, stride=pitch), :].T * gain_ref[...]
             turn_s[pl.ds(p * half * pitch + h, half, stride=pitch), :] = turned
+    for _ in beside:
+        pass
     for r in range(2):
         for kk in range(2):
             for d in range(owners):
@@ -196,17 +201,20 @@
 def forward_first(pitch, x_ref, early_ref, gain_ref, own_ref, other_ref, table_ref, send_ref, part_ref, spec_s, turn_s):
     channels, rows, width = x_ref.shape
     cut = early_ref.shape[2]
-    project(x_ref, normalizer(own_ref, other_ref, slice(0, width), channels), table_ref, 0, pitch, None, spec_s)
-    hand_out(0, gain_ref, spec_s, turn_s, send_ref, rows, pitch)
+    stats = normalizer(own_ref, other_ref, slice(0, width), channels)
+    for _ in project(x_ref, stats, table_ref, 0, pitch, None, spec_s):
+        pass
     stats = normalizer(own_ref, other_ref, slice(width, width + cut), channels)
-    project(early_ref, stats, table_ref, 0, pitch, None, part_ref)
+    early = project(early_ref, stats, table_ref, 0, pitch, None, part_ref)
+    hand_out(0, gain_ref, spec_s, turn_s, send_ref, rows, pitch, early)
 
 
 def forward_second(pitch, x_ref, gain_ref, own_ref, other_ref, table_ref, part_ref, _, send_ref, spec_s, turn_s):
     channels, rows, lanes = x_ref.shape
     cut = table_ref.shape[0] - lanes
     stats = normalizer(own_ref, other_ref, slice(0, lanes), channels)
-    project(x_ref, stats, table_ref, cut, pitch, part_ref, spec_s)
+    for _ in project(x_ref, stats, table_ref, cut, pitch, part_ref, spec_s):
+        pass
     hand_out(1, gain_ref, spec_s, turn_s, send_ref, rows, pitch)
 
 
@@ -216,7 +224,7 @@
     pitch = rows + 8
     vmem = pl.BlockSpec(memory_space=pltpu.VMEM)
     send = jax.ShapeDtypeStruct((2, owners, 2 * rows, 2 * channels), BF16)
-    part = jax.ShapeDtypeStruct((2, channels * pitch, two_k // 2), F32)
+    part = jax.ShapeDtypeStruct((2, (channels + 1) * pitch, two_k // 2), F32)
     lanes = sum(x.shape[2] for x in held)
     return pl.pallas_call(
         functools.partial(kernel, pitch),
@@ -224,8 +232,8 @@
         out_specs=vmem if more else [vmem, vmem],
         out_shape=send if more else [send, part],
         scratch_shapes=[
-            pltpu.VMEM((2, channels * pitch, two_k // 2), F32),
-            pltpu.VMEM((two_k * pitch, channels), F32),
+            pltpu.VMEM((2, (channels + 1) * pitch, two_k // 2), F32),
+            pltpu.VMEM(((two_k + 1) * pitch, channels), F32),
         ],
         input_output_aliases={len(held) + 5: 0} if more else {},
         compiler_params=pltpu.CompilerParams(vmem_limit_bytes=24 * MIB),
@@ -420,8 +428,8 @@
         out_specs=pl.BlockSpec(memory_space=pltpu.HBM),
         out_shape=jax.ShapeDtypeStruct((slices, channels, rows, width), BF16),
         scratch_shapes=[
-            pltpu.VMEM((2, two_k // 2 * pitch, channels), F32),
-            pltpu.VMEM((2, channels * pitch, two_k // 2), F32),
+            pltpu.VMEM((2, (two_k // 2 + 1) * pitch, channels), F32),
+            pltpu.VMEM((2, (channels + 1) * pitch, two_k // 2), F32),
             pltpu.VMEM((slices, channels, rows, width), BF16),
             pltpu.SemaphoreType.DMA((slices * channels // chan_block,)),
         ],

time: 96.5 us -> 96.5 us (level)
  no operation moved by 1% of the time
where the time goes in v5:
time: 96.5 us; the launch traced here: 96.4 us
  blocking collectives  76.2 us (79%)
  Pallas kernels  16.9 us (18%)
  starting transfers between devices  2.27 us (2%)
    all_to_all x2, blocking collectives, exchange(): lax.all_to_all(flat, ('blk', 'row'), split_axis=0, concat_axis=0, tiled=T...  76.2 us
    pallas_call x2, Pallas kernels, channel_stats(): pl.pallas_call(functools.partial(stats_kernel, segments), in_specs=[pl.Bl...  4.69 us
    pallas_call x2, Pallas kernels, forward_rows(): pl.pallas_call(functools.partial(kernel, pitch), in_specs=[vmem] * (len(h...  4.46 us
    pallas_call x1, Pallas kernels, inverse_rows(): pl.pallas_call(functools.partial(inverse_kernel, chan_block, pitch), in_s...  4.45 us
    pallas_call x1, Pallas kernels, filter_columns(): pl.pallas_call(filter_kernel, in_specs=[vmem] * 8, out_specs=vmem, out_sh...  3.31 us
    ppermute x1, starting transfers between devices, local(): other_first = lax.ppermute(own_first, 'blk', swap)  2.12 us
  transfers between devices with their start and end apart: 2, of which 2 were waited for; matrix products, arithmetic and copies ran while one was open for 0% of the time, Pallas kernels for 5%

profile of v5, /device:TPU:1, one launch (start us, length us, event | category | flops | bytes accessed | tf_op | source)
XLA Modules:
  0.0 96.4 jit_solution(13186182420907506732)
XLA Ops:
  0.0 2.7 %channel_stats.3 = (bf16[128,16,1024]{2,1,0:T(8,128)(2,1)S(1)}, bf16[128,16,256]{2,1,0:T(8,128)(2,1)S(1)}, bf16[3,16,1280]{2,1,0:T(8,128)(2,1)S(1)}) custom-call(bf16[2,128,16,1024]{3,2,1,0:T(8,128)(2,1)} %x_ref.3), custom_call_target="tpu_custom_call" | custom-call | flops 13107200 | bytes 5242880 | tf_op jit(solution)/shard_map/channel_stats/pallas_call | solution.py:131
  2.7 0.0 copy-start
  2.7 0.0 copy-start.2
  2.7 2.1 %collective-permute-start.1 = (bf16[3,16,1280]{2,1,0:T(8,128)(2,1)S(1)}, bf16[3,16,1280]{2,1,0:T(8,128)(2,1)S(1)}, u32[]{:S(2)}, u32[]{:S(2)}) collective-permute-start(bf16[3,16,1280]{2,1,0:T(8,128)(2,1)S(1)} %get-tuple-element.16.own_ref), channel_id=1, source_target_pairs={{0,1},{1,0},{2,3},{3,2},{4,5},{5,4},{6,7},{7,6},{8,9},{9,8},{10,11... | collective-permute-start | bytes 368648 | tf_op jit(solution)/shard_map/ppermute | solution.py:466
  4.8 2.0 %channel_stats.2 = (bf16[128,16,768]{2,1,0:T(8,128)(2,1)S(1)}, bf16[3,16,768]{2,1,0:T(8,128)(2,1)S(1)}) custom-call(bf16[2,128,16,1024]{3,2,1,0:T(8,128)(2,1)} %x_ref.3), custom_call_target="tpu_custom_call" | custom-call | flops 7864320 | bytes 3145728 | tf_op jit(solution)/shard_map/channel_stats/pallas_call | solution.py:131
  6.9 0.2 collective-permute-start
  7.0 0.1 collective-permute-done.1.other_ref
  7.1 0.0 copy-done
  7.1 0.0 copy-done.2
  7.1 2.5 %norm_and_row_dft.2 = (bf16[2,64,32,256]{3,2,1,0:T(8,128)(2,1)S(1)}, f32[2,3096,128]{2,1,0:T(8,128)S(1)}) custom-call(bf16[128,16,1024]{2,1,0:T(8,128)(2,1)S(1)} %get-tuple-element.14.x_ref, bf16[128,16,256]{2,1,0:T(8,128)(2,1)S(1)} %get-tuple-element.15.early_ref, f32[1,128]{1,0:T(1,128)S(1)} %bitcast.11, ...), custom_call_target="tpu_custom_call" | custom-call | flops 1342177280 | bytes 5242880 | tf_op jit(solution)/shard_map/norm_and_row_dft/pallas_call | solution.py:229
  9.6 0.5 collective-permute-done.other_ref
  10.1 2.0 %norm_and_row_dft.3 = bf16[2,64,32,256]{3,2,1,0:T(8,128)(2,1)S(1)} custom-call(bf16[128,16,768]{2,1,0:T(8,128)(2,1)S(1)} %get-tuple-element.12.x_ref, f32[1,128]{1,0:T(1,128)S(1)} %bitcast.12, bf16[3,16,768]{2,1,0:T(8,128)(2,1)S(1)} %get-tuple-element.13.own_ref, ...), custom_call_target="tpu_custom_call", output_to_operand_aliasing={{}: (6, {})} | custom-call | flops 805306368 | bytes 3145728 | tf_op jit(solution)/shard_map/norm_and_row_dft/pallas_call | solution.py:229
  12.1 0.0 copy-start.3
  12.1 0.0 copy-start.4
  12.1 0.0 copy-start.5
  12.1 0.0 copy-start.6
  12.2 0.0 copy-start.7
  12.2 0.0 copy-start.8
  12.2 0.0 copy-start.9
  12.2 41.8 %all_to_all.10 = bf16[128,32,256]{2,1,0:T(8,128)(2,1)S(1)} all-to-all(bf16[128,32,256]{2,1,0:T(8,128)(2,1)S(1)} %bitcast.7), channel_id=1, replica_groups=mesh['row'=64,'blk'=2] {'blk','row'}, dimensions={0} | all-to-all | bytes 4194304 | tf_op jit(solution)/shard_map/all_to_all | solution.py:449
  54.0 3.3 %column_filter.1 = bf16[2,64,32,256]{3,2,1,0:T(8,128)(2,1)S(1)} custom-call(bf16[2,64,32,256]{3,2,1,0:T(8,128)(2,1)S(1)} %bitcast.9, bf16[528,1024]{1,0:T(8,128)(2,1)S(1)} %copy-done.7, bf16[1024,512]{1,0:T(8,128)(2,1)S(1)} %copy-done.8, bf16[32,128]{1,0:T(8,128)(2,1)S(1)} %copy-done.9, bf16[2,256,32]{2,1,0:T(8,128)(2,1)S(1)} %bitcast.13, ...), custom_call_target="tpu_custom_call" | custom-call | flops 3221225472 | bytes 8388608 | tf_op jit(solution)/shard_map/column_filter/pallas_call | solution.py:359
  57.3 0.0 copy-start.1
  57.4 34.4 %all_to_all.11 = bf16[128,32,256]{2,1,0:T(8,128)(2,1)S(1)} all-to-all(bf16[128,32,256]{2,1,0:T(8,128)(2,1)S(1)} %bitcast.10), channel_id=1, replica_groups=mesh['row'=64,'blk'=2] {'blk','row'}, dimensions={0} | all-to-all | bytes 4194304 | tf_op jit(solution)/shard_map/all_to_all | solution.py:449
  91.8 4.4 %inverse_row_dft.1 = bf16[2,128,16,1024]{3,2,1,0:T(8,128)(2,1)} custom-call(bf16[2,64,32,256]{3,2,1,0:T(8,128)(2,1)S(1)} %bitcast.8, bf16[256,1024]{1,0:T(8,128)(2,1)S(1)} %copy-done.1), custom_call_target="tpu_custom_call" | custom-call | flops 2147483648 | bytes 8388608 | tf_op jit(solution)/shard_map/inverse_row_dft/pallas_call | solution.py:425
  (8 shorter events, 0.0 us)
Async XLA Ops:
  2.7 4.4 %copy-start = (bf16[1024,256]{1,0:T(8,128)(2,1)S(1)}, bf16[1024,256]{1,0:T(8,128)(2,1)}, u32[]{:S(2)}) copy-start(bf16[1024,256]{1,0:T(8,128)(2,1)} %constant.11.clone.table_ref) | copy-start | bytes 1572868
  2.7 4.4 %copy-start.2 = (f32[128]{0:T(128)S(1)}, f32[128]{0:T(128)}, u32[]{:S(2)}) copy-start(f32[128]{0:T(128)} %param.12) | copy-start | bytes 1540
  2.7 4.4 %collective-permute-start.1 = (bf16[3,16,1280]{2,1,0:T(8,128)(2,1)S(1)}, bf16[3,16,1280]{2,1,0:T(8,128)(2,1)S(1)}, u32[]{:S(2)}, u32[]{:S(2)}) collective-permute-start(bf16[3,16,1280]{2,1,0:T(8,128)(2,1)S(1)} %get-tuple-element.16.own_ref), channel_id=1, source_target_pairs={{0,1},{1,0},{2,3},{3,2},{4,5},{5,4},{6,7},{7,6},{8,9},{9,8},{10,11... | collective-permute-start | bytes 368648 | tf_op jit(solution)/shard_map/ppermute | solution.py:466
  6.9 3.3 %collective-permute-start = (bf16[3,16,768]{2,1,0:T(8,128)(2,1)S(1)}, bf16[3,16,768]{2,1,0:T(8,128)(2,1)S(1)}, u32[]{:S(2)}, u32[]{:S(2)}) collective-permute-start(bf16[3,16,768]{2,1,0:T(8,128)(2,1)S(1)} %get-tuple-element.13.own_ref), channel_id=1, source_target_pairs={{0,1},{1,0},{2,3},{3,2},{4,5},{5,4},{6,7},{7,6},{8,9},{9,8},{10,11... | collective-permute-start | bytes 221192 | tf_op jit(solution)/shard_map/ppermute | solution.py:467
  12.1 41.9 %copy-start.3 = (bf16[2,8,32,32]{3,2,1,0:T(8,128)(2,1)S(1)}, bf16[2,8,32,32]{3,2,1,0:T(8,128)(2,1)}, u32[]{:S(2)}) copy-start(bf16[2,8,32,32]{3,2,1,0:T(8,128)(2,1)} %param.13) | copy-start | bytes 98308
  12.1 41.9 %copy-start.4 = (bf16[2,8,32,32]{3,2,1,0:T(8,128)(2,1)S(1)}, bf16[2,8,32,32]{3,2,1,0:T(8,128)(2,1)}, u32[]{:S(2)}) copy-start(bf16[2,8,32,32]{3,2,1,0:T(8,128)(2,1)} %param.15) | copy-start | bytes 98308
  12.1 41.8 %copy-start.5 = (f32[2,256]{1,0:T(2,128)S(1)}, f32[2,256]{1,0:T(2,128)}, u32[]{:S(2)}) copy-start(f32[2,256]{1,0:T(2,128)} %b1_ref.1) | copy-start | bytes 6148
  12.1 41.8 %copy-start.6 = (f32[2,256]{1,0:T(2,128)S(1)}, f32[2,256]{1,0:T(2,128)}, u32[]{:S(2)}) copy-start(f32[2,256]{1,0:T(2,128)} %b2_ref.1) | copy-start | bytes 6148
  12.2 41.8 %copy-start.7 = (bf16[528,1024]{1,0:T(8,128)(2,1)S(1)}, bf16[528,1024]{1,0:T(8,128)(2,1)}, u32[]{:S(2)}) copy-start(bf16[528,1024]{1,0:T(8,128)(2,1)} %constant.12.clone.fwd_ref) | copy-start | bytes 3244036
  12.2 41.8 %copy-start.8 = (bf16[1024,512]{1,0:T(8,128)(2,1)S(1)}, bf16[1024,512]{1,0:T(8,128)(2,1)}, u32[]{:S(2)}) copy-start(bf16[1024,512]{1,0:T(8,128)(2,1)} %constant.13.clone.inv_ref) | copy-start | bytes 3145732
  12.2 41.8 %copy-start.9 = (bf16[32,128]{1,0:T(8,128)(2,1)S(1)}, bf16[32,128]{1,0:T(8,128)(2,1)}, u32[]{:S(2)}) copy-start(bf16[32,128]{1,0:T(8,128)(2,1)} %constant.10.clone.spread_ref) | copy-start | bytes 24580
  57.3 34.4 %copy-start.1 = (bf16[256,1024]{1,0:T(8,128)(2,1)S(1)}, bf16[256,1024]{1,0:T(8,128)(2,1)}, u32[]{:S(2)}) copy-start(bf16[256,1024]{1,0:T(8,128)(2,1)} %constant.14.clone.table_ref) | copy-start | bytes 1572868

commit v6 on v5

--- a/solution.py
+++ b/solution.py
@@ -109,8 +109,9 @@
                 for c in range(at, at + STEP, 2):
                     one = ref[c, :, there] - pivot
                     two = ref[c + 1, :, there] - pivot
-                    first = first + (one + two).astype(F32)
-                    second = second + (one * one + two * two).astype(F32)
+                    one, two = one.astype(F32), two.astype(F32)
+                    first = first + (one + two)
+                    second = second + (one * one + two * two)
                 if at + STEP < channels:
                     first_s[:, here], second_s[:, here] = first, second
                 else:

time: 96.5 us -> 96.7 us (level)
  transfers between devices with their start and end apart: 2 -> 2, of which waited for: 2 -> 1; matrix products, arithmetic and copies ran while one was open for 0% -> 0% of each run, Pallas kernels for 5% -> 5%
where the time goes in v6:
time: 96.7 us; the launch traced here: 96.6 us
  blocking collectives  76.2 us (79%)
  Pallas kernels  17.1 us (18%)
  starting transfers between devices  2.27 us (2%)
    all_to_all x2, blocking collectives, exchange(): lax.all_to_all(flat, ('blk', 'row'), split_axis=0, concat_axis=0, tiled=T...  76.2 us
    pallas_call x2, Pallas kernels, channel_stats(): pl.pallas_call(functools.partial(stats_kernel, segments), in_specs=[pl.Bl...  4.89 us
    pallas_call x1, Pallas kernels, inverse_rows(): pl.pallas_call(functools.partial(inverse_kernel, chan_block, pitch), in_s...  4.45 us
    pallas_call x2, Pallas kernels, forward_rows(): pl.pallas_call(functools.partial(kernel, pitch), in_specs=[vmem] * (len(h...  4.44 us
    pallas_call x1, Pallas kernels, filter_columns(): pl.pallas_call(filter_kernel, in_specs=[vmem] * 8, out_specs=vmem, out_sh...  3.31 us
    ppermute x1, starting transfers between devices, local(): other_first = lax.ppermute(own_first, 'blk', swap)  2.12 us
  transfers between devices with their start and end apart: 2, of which 1 were waited for; matrix products, arithmetic and copies ran while one was open for 0% of the time, Pallas kernels for 5%

profile of v6, /device:TPU:1, one launch (start us, length us, event | category | flops | bytes accessed | tf_op | source)
XLA Modules:
  0.0 96.6 jit_solution(4123723268030867735)
XLA Ops:
  0.0 2.8 %channel_stats.3 = (bf16[128,16,1024]{2,1,0:T(8,128)(2,1)S(1)}, bf16[128,16,256]{2,1,0:T(8,128)(2,1)S(1)}, bf16[3,16,1280]{2,1,0:T(8,128)(2,1)S(1)}) custom-call(bf16[2,128,16,1024]{3,2,1,0:T(8,128)(2,1)} %x_ref.3), custom_call_target="tpu_custom_call" | custom-call | flops 13107200 | bytes 5242880 | tf_op jit(solution)/shard_map/channel_stats/pallas_call | solution.py:132
  2.8 0.0 copy-start
  2.8 0.0 copy-start.2
  2.8 2.1 %collective-permute-start.1 = (bf16[3,16,1280]{2,1,0:T(8,128)(2,1)S(1)}, bf16[3,16,1280]{2,1,0:T(8,128)(2,1)S(1)}, u32[]{:S(2)}, u32[]{:S(2)}) collective-permute-start(bf16[3,16,1280]{2,1,0:T(8,128)(2,1)S(1)} %get-tuple-element.16.own_ref), channel_id=1, source_target_pairs={{0,1},{1,0},{2,3},{3,2},{4,5},{5,4},{6,7},{7,6},{8,9},{9,8},{10,11... | collective-permute-start | bytes 368648 | tf_op jit(solution)/shard_map/ppermute | solution.py:467
  5.0 2.1 %channel_stats.2 = (bf16[128,16,768]{2,1,0:T(8,128)(2,1)S(1)}, bf16[3,16,768]{2,1,0:T(8,128)(2,1)S(1)}) custom-call(bf16[2,128,16,1024]{3,2,1,0:T(8,128)(2,1)} %x_ref.3), custom_call_target="tpu_custom_call" | custom-call | flops 7864320 | bytes 3145728 | tf_op jit(solution)/shard_map/channel_stats/pallas_call | solution.py:132
  7.1 0.2 collective-permute-start
  7.2 0.0 collective-permute-done.1.other_ref
  7.2 0.0 copy-done.2
  7.2 2.5 %norm_and_row_dft.2 = (bf16[2,64,32,256]{3,2,1,0:T(8,128)(2,1)S(1)}, f32[2,3096,128]{2,1,0:T(8,128)S(1)}) custom-call(bf16[128,16,1024]{2,1,0:T(8,128)(2,1)S(1)} %get-tuple-element.14.x_ref, bf16[128,16,256]{2,1,0:T(8,128)(2,1)S(1)} %get-tuple-element.15.early_ref, f32[1,128]{1,0:T(1,128)S(1)} %bitcast.11, ...), custom_call_target="tpu_custom_call" | custom-call | flops 1342177280 | bytes 5242880 | tf_op jit(solution)/shard_map/norm_and_row_dft/pallas_call | solution.py:230
  9.7 0.6 collective-permute-done.other_ref
  10.3 2.0 %norm_and_row_dft.3 = bf16[2,64,32,256]{3,2,1,0:T(8,128)(2,1)S(1)} custom-call(bf16[128,16,768]{2,1,0:T(8,128)(2,1)S(1)} %get-tuple-element.12.x_ref, f32[1,128]{1,0:T(1,128)S(1)} %bitcast.12, bf16[3,16,768]{2,1,0:T(8,128)(2,1)S(1)} %get-tuple-element.13.own_ref, ...), custom_call_target="tpu_custom_call", output_to_operand_aliasing={{}: (6, {})} | custom-call | flops 805306368 | bytes 3145728 | tf_op jit(solution)/shard_map/norm_and_row_dft/pallas_call | solution.py:230
  12.3 0.0 copy-start.3
  12.3 0.0 copy-start.4
  12.3 0.0 copy-start.5
  12.3 0.0 copy-start.6
  12.4 0.0 copy-start.7
  12.4 0.0 copy-start.8
  12.4 0.0 copy-start.9
  12.4 41.8 %all_to_all.10 = bf16[128,32,256]{2,1,0:T(8,128)(2,1)S(1)} all-to-all(bf16[128,32,256]{2,1,0:T(8,128)(2,1)S(1)} %bitcast.7), channel_id=1, replica_groups=mesh['row'=64,'blk'=2] {'blk','row'}, dimensions={0} | all-to-all | bytes 4194304 | tf_op jit(solution)/shard_map/all_to_all | solution.py:450
  54.2 0.0 copy-done.5
  54.2 3.3 %column_filter.1 = bf16[2,64,32,256]{3,2,1,0:T(8,128)(2,1)S(1)} custom-call(bf16[2,64,32,256]{3,2,1,0:T(8,128)(2,1)S(1)} %bitcast.9, bf16[528,1024]{1,0:T(8,128)(2,1)S(1)} %copy-done.7, bf16[1024,512]{1,0:T(8,128)(2,1)S(1)} %copy-done.8, bf16[32,128]{1,0:T(8,128)(2,1)S(1)} %copy-done.9, bf16[2,256,32]{2,1,0:T(8,128)(2,1)S(1)} %bitcast.13, ...), custom_call_target="tpu_custom_call" | custom-call | flops 3221225472 | bytes 8388608 | tf_op jit(solution)/shard_map/column_filter/pallas_call | solution.py:360
  57.5 0.0 copy-start.1
  57.5 34.4 %all_to_all.11 = bf16[128,32,256]{2,1,0:T(8,128)(2,1)S(1)} all-to-all(bf16[128,32,256]{2,1,0:T(8,128)(2,1)S(1)} %bitcast.10), channel_id=1, replica_groups=mesh['row'=64,'blk'=2] {'blk','row'}, dimensions={0} | all-to-all | bytes 4194304 | tf_op jit(solution)/shard_map/all_to_all | solution.py:450
  91.9 4.4 %inverse_row_dft.1 = bf16[2,128,16,1024]{3,2,1,0:T(8,128)(2,1)} custom-call(bf16[2,64,32,256]{3,2,1,0:T(8,128)(2,1)S(1)} %bitcast.8, bf16[256,1024]{1,0:T(8,128)(2,1)S(1)} %copy-done.1), custom_call_target="tpu_custom_call" | custom-call | flops 2147483648 | bytes 8388608 | tf_op jit(solution)/shard_map/inverse_row_dft/pallas_call | solution.py:426
  (8 shorter events, 0.0 us)
Async XLA Ops:
  2.8 4.4 %copy-start = (bf16[1024,256]{1,0:T(8,128)(2,1)S(1)}, bf16[1024,256]{1,0:T(8,128)(2,1)}, u32[]{:S(2)}) copy-start(bf16[1024,256]{1,0:T(8,128)(2,1)} %constant.11.clone.table_ref) | copy-start | bytes 1572868
  2.8 4.4 %copy-start.2 = (f32[128]{0:T(128)S(1)}, f32[128]{0:T(128)}, u32[]{:S(2)}) copy-start(f32[128]{0:T(128)} %param.12) | copy-start | bytes 1540
  2.8 4.4 %collective-permute-start.1 = (bf16[3,16,1280]{2,1,0:T(8,128)(2,1)S(1)}, bf16[3,16,1280]{2,1,0:T(8,128)(2,1)S(1)}, u32[]{:S(2)}, u32[]{:S(2)}) collective-permute-start(bf16[3,16,1280]{2,1,0:T(8,128)(2,1)S(1)} %get-tuple-element.16.own_ref), channel_id=1, source_target_pairs={{0,1},{1,0},{2,3},{3,2},{4,5},{5,4},{6,7},{7,6},{8,9},{9,8},{10,11... | collective-permute-start | bytes 368648 | tf_op jit(solution)/shard_map/ppermute | solution.py:467
  7.1 3.3 %collective-permute-start = (bf16[3,16,768]{2,1,0:T(8,128)(2,1)S(1)}, bf16[3,16,768]{2,1,0:T(8,128)(2,1)S(1)}, u32[]{:S(2)}, u32[]{:S(2)}) collective-permute-start(bf16[3,16,768]{2,1,0:T(8,128)(2,1)S(1)} %get-tuple-element.13.own_ref), channel_id=1, source_target_pairs={{0,1},{1,0},{2,3},{3,2},{4,5},{5,4},{6,7},{7,6},{8,9},{9,8},{10,11... | collective-permute-start | bytes 221192 | tf_op jit(solution)/shard_map/ppermute | solution.py:468
  12.3 41.9 %copy-start.3 = (bf16[2,8,32,32]{3,2,1,0:T(8,128)(2,1)S(1)}, bf16[2,8,32,32]{3,2,1,0:T(8,128)(2,1)}, u32[]{:S(2)}) copy-start(bf16[2,8,32,32]{3,2,1,0:T(8,128)(2,1)} %param.13) | copy-start | bytes 98308
  12.3 41.9 %copy-start.4 = (bf16[2,8,32,32]{3,2,1,0:T(8,128)(2,1)S(1)}, bf16[2,8,32,32]{3,2,1,0:T(8,128)(2,1)}, u32[]{:S(2)}) copy-start(bf16[2,8,32,32]{3,2,1,0:T(8,128)(2,1)} %param.15) | copy-start | bytes 98308
  12.3 41.9 %copy-start.5 = (f32[2,256]{1,0:T(2,128)S(1)}, f32[2,256]{1,0:T(2,128)}, u32[]{:S(2)}) copy-start(f32[2,256]{1,0:T(2,128)} %b1_ref.1) | copy-start | bytes 6148
  12.3 41.8 %copy-start.6 = (f32[2,256]{1,0:T(2,128)S(1)}, f32[2,256]{1,0:T(2,128)}, u32[]{:S(2)}) copy-start(f32[2,256]{1,0:T(2,128)} %b2_ref.1) | copy-start | bytes 6148
  12.4 41.8 %copy-start.7 = (bf16[528,1024]{1,0:T(8,128)(2,1)S(1)}, bf16[528,1024]{1,0:T(8,128)(2,1)}, u32[]{:S(2)}) copy-start(bf16[528,1024]{1,0:T(8,128)(2,1)} %constant.12.clone.fwd_ref) | copy-start | bytes 3244036
  12.4 41.8 %copy-start.8 = (bf16[1024,512]{1,0:T(8,128)(2,1)S(1)}, bf16[1024,512]{1,0:T(8,128)(2,1)}, u32[]{:S(2)}) copy-start(bf16[1024,512]{1,0:T(8,128)(2,1)} %constant.13.clone.inv_ref) | copy-start | bytes 3145732
  12.4 41.8 %copy-start.9 = (bf16[32,128]{1,0:T(8,128)(2,1)S(1)}, bf16[32,128]{1,0:T(8,128)(2,1)}, u32[]{:S(2)}) copy-start(bf16[32,128]{1,0:T(8,128)(2,1)} %constant.10.clone.spread_ref) | copy-start | bytes 24580
  57.5 34.4 %copy-start.1 = (bf16[256,1024]{1,0:T(8,128)(2,1)S(1)}, bf16[256,1024]{1,0:T(8,128)(2,1)}, u32[]{:S(2)}) copy-start(bf16[256,1024]{1,0:T(8,128)(2,1)} %constant.14.clone.table_ref) | copy-start | bytes 1572868

commit v7 on v6

--- a/solution.py
+++ b/solution.py
@@ -177,10 +177,10 @@
         yield
 
 
-def hand_out(which, gain_ref, spec_s, turn_s, send_ref, rows, pitch, beside=()):
+def hand_out(gain_ref, spec_s, turn_s, slice_ref, rows, pitch, beside=()):
     parts, _, half = spec_s.shape
     channels = turn_s.shape[-1]
-    owners = send_ref.shape[1]
+    owners = slice_ref.shape[0]
     beside = iter(beside)
     for h in range(rows):
         if h % 4 == 0:
@@ -194,12 +194,12 @@
         for kk in range(2):
             for d in range(owners):
                 start = ((r * 2 + kk) * owners + d) * pitch
-                send_ref[which, d, r * rows : (r + 1) * rows, kk * channels : (kk + 1) * channels] = turn_s[
+                slice_ref[d, r * rows : (r + 1) * rows, kk * channels : (kk + 1) * channels] = turn_s[
                     start : start + rows, :
                 ].astype(BF16)
 
 
-def forward_first(pitch, x_ref, early_ref, gain_ref, own_ref, other_ref, table_ref, send_ref, part_ref, spec_s, turn_s):
+def forward_first(pitch, x_ref, early_ref, gain_ref, own_ref, other_ref, table_ref, first_ref, part_ref, spec_s, turn_s):
     channels, rows, width = x_ref.shape
     cut = early_ref.shape[2]
     stats = normalizer(own_ref, other_ref, slice(0, width), channels)
@@ -207,16 +207,21 @@
         pass
     stats = normalizer(own_ref, other_ref, slice(width, width + cut), channels)
     early = project(early_ref, stats, table_ref, 0, pitch, None, part_ref)
-    hand_out(0, gain_ref, spec_s, turn_s, send_ref, rows, pitch, early)
-
-
-def forward_second(pitch, x_ref, gain_ref, own_ref, other_ref, table_ref, part_ref, _, send_ref, spec_s, turn_s):
+    hand_out(gain_ref, spec_s, turn_s, first_ref, rows, pitch, early)
+
+
+def forward_second(
+    pitch, x_ref, gain_ref, own_ref, other_ref, table_ref, first_ref, part_ref, send_ref, spec_s, turn_s, sem
+):
+    copy = pltpu.make_async_copy(first_ref, send_ref.at[0], sem)
+    copy.start()
     channels, rows, lanes = x_ref.shape
     cut = table_ref.shape[0] - lanes
     stats = normalizer(own_ref, other_ref, slice(0, lanes), channels)
     for _ in project(x_ref, stats, table_ref, cut, pitch, part_ref, spec_s):
         pass
-    hand_out(1, gain_ref, spec_s, turn_s, send_ref, rows, pitch)
+    hand_out(gain_ref, spec_s, turn_s, send_ref.at[1], rows, pitch)
+    copy.wait()
 
 
 def forward_rows(kernel, held, gain, own, other, table, owners, more=()):
@@ -224,19 +229,19 @@
     width, two_k = table.shape
     pitch = rows + 8
     vmem = pl.BlockSpec(memory_space=pltpu.VMEM)
-    send = jax.ShapeDtypeStruct((2, owners, 2 * rows, 2 * channels), BF16)
+    one = (owners, 2 * rows, 2 * channels)
     part = jax.ShapeDtypeStruct((2, (channels + 1) * pitch, two_k // 2), F32)
     lanes = sum(x.shape[2] for x in held)
     return pl.pallas_call(
         functools.partial(kernel, pitch),
         in_specs=[vmem] * (len(held) + 4 + len(more)),
         out_specs=vmem if more else [vmem, vmem],
-        out_shape=send if more else [send, part],
+        out_shape=jax.ShapeDtypeStruct((2,) + one, BF16) if more else [jax.ShapeDtypeStruct(one, BF16), part],
         scratch_shapes=[
             pltpu.VMEM((2, (channels + 1) * pitch, two_k // 2), F32),
             pltpu.VMEM(((two_k + 1) * pitch, channels), F32),
-        ],
-        input_output_aliases={len(held) + 5: 0} if more else {},
+        ]
+        + [pltpu.SemaphoreType.DMA] * (1 if more else 0),
         compiler_params=pltpu.CompilerParams(vmem_limit_bytes=24 * MIB),
         cost_estimate=pl.CostEstimate(
             flops=2 * channels * rows * lanes * two_k, bytes_accessed=2 * channels * rows * lanes, transcendentals=0
@@ -466,9 +471,9 @@
     (held_first, own_first), (held_second, own_second) = [channel_stats(field, group) for group in groups]
     other_first = lax.ppermute(own_first, "blk", swap)
     other_second = lax.ppermute(own_second, "blk", swap)
-    send, part = forward_rows(forward_first, held_first, gain, own_first, other_first, table, owners)
+    first, part = forward_rows(forward_first, held_first, gain, own_first, other_first, table, owners)
     send = forward_rows(
-        forward_second, held_second, gain, own_second, other_second, table, owners, (part, send)
+        forward_second, held_second, gain, own_second, other_second, table, owners, (first, part)
     )
     columns = exchange(send)
     filtered = filter_columns(

time: 96.7 us -> 96.8 us (level)
  no operation moved by 1% of the time
where the time goes in v7:
time: 96.8 us; the launch traced here: 96.6 us
  blocking collectives  76.2 us (79%)
  Pallas kernels  17.2 us (18%)
  starting transfers between devices  2.27 us (2%)
    all_to_all x2, blocking collectives, exchange(): lax.all_to_all(flat, ('blk', 'row'), split_axis=0, concat_axis=0, tiled=T...  76.2 us
    pallas_call x2, Pallas kernels, channel_stats(): pl.pallas_call(functools.partial(stats_kernel, segments), in_specs=[pl.Bl...  4.89 us
    pallas_call x2, Pallas kernels, forward_rows(): pl.pallas_call(functools.partial(kernel, pitch), in_specs=[vmem] * (len(h...  4.54 us
    pallas_call x1, Pallas kernels, inverse_rows(): pl.pallas_call(functools.partial(inverse_kernel, chan_block, pitch), in_s...  4.44 us
    pallas_call x1, Pallas kernels, filter_columns(): pl.pallas_call(filter_kernel, in_specs=[vmem] * 8, out_specs=vmem, out_sh...  3.29 us
    ppermute x1, starting transfers between devices, local(): other_first = lax.ppermute(own_first, 'blk', swap)  2.12 us
  transfers between devices with their start and end apart: 2, of which 1 were waited for; matrix products, arithmetic and copies ran while one was open for 0% of the time, Pallas kernels for 5%

profile of v7, /device:TPU:1, one launch (start us, length us, event | category | flops | bytes accessed | tf_op | source)
XLA Modules:
  0.0 96.6 jit_solution(11990815922901311060)
XLA Ops:
  0.0 2.8 %channel_stats.3 = (bf16[128,16,1024]{2,1,0:T(8,128)(2,1)S(1)}, bf16[128,16,256]{2,1,0:T(8,128)(2,1)S(1)}, bf16[3,16,1280]{2,1,0:T(8,128)(2,1)S(1)}) custom-call(bf16[2,128,16,1024]{3,2,1,0:T(8,128)(2,1)} %x_ref.3), custom_call_target="tpu_custom_call" | custom-call | flops 13107200 | bytes 5242880 | tf_op jit(solution)/shard_map/channel_stats/pallas_call | solution.py:132
  2.8 0.0 copy-start
  2.8 0.0 copy-start.2
  2.8 2.1 %collective-permute-start.1 = (bf16[3,16,1280]{2,1,0:T(8,128)(2,1)S(1)}, bf16[3,16,1280]{2,1,0:T(8,128)(2,1)S(1)}, u32[]{:S(2)}, u32[]{:S(2)}) collective-permute-start(bf16[3,16,1280]{2,1,0:T(8,128)(2,1)S(1)} %get-tuple-element.16.own_ref), channel_id=1, source_target_pairs={{0,1},{1,0},{2,3},{3,2},{4,5},{5,4},{6,7},{7,6},{8,9},{9,8},{10,11... | collective-permute-start | bytes 368648 | tf_op jit(solution)/shard_map/ppermute | solution.py:472
  5.0 2.1 %channel_stats.2 = (bf16[128,16,768]{2,1,0:T(8,128)(2,1)S(1)}, bf16[3,16,768]{2,1,0:T(8,128)(2,1)S(1)}) custom-call(bf16[2,128,16,1024]{3,2,1,0:T(8,128)(2,1)} %x_ref.3), custom_call_target="tpu_custom_call" | custom-call | flops 7864320 | bytes 3145728 | tf_op jit(solution)/shard_map/channel_stats/pallas_call | solution.py:132
  7.1 0.2 collective-permute-start
  7.2 0.0 collective-permute-done.1.other_ref
  7.2 0.0 copy-done.2
  7.2 2.5 %norm_and_row_dft.2 = (bf16[64,32,256]{2,1,0:T(8,128)(2,1)S(1)}, f32[2,3096,128]{2,1,0:T(8,128)S(1)}) custom-call(bf16[128,16,1024]{2,1,0:T(8,128)(2,1)S(1)} %get-tuple-element.14.x_ref, bf16[128,16,256]{2,1,0:T(8,128)(2,1)S(1)} %get-tuple-element.15.early_ref, f32[1,128]{1,0:T(1,128)S(1)} %bitcast.11, bf16[3,16,1280]{2,1,0:T(8,128)(2,1)S(1)} %get-tuple-element.16.own_ref, ...), custom_call_target="tpu_custom_call" | custom-call | flops 1342177280 | bytes 5242880 | tf_op jit(solution)/shard_map/norm_and_row_dft/pallas_call | solution.py:235
  9.8 0.6 collective-permute-done.other_ref
  10.3 2.0 %norm_and_row_dft.3 = bf16[2,64,32,256]{3,2,1,0:T(8,128)(2,1)S(1)} custom-call(bf16[128,16,768]{2,1,0:T(8,128)(2,1)S(1)} %get-tuple-element.12.x_ref, f32[1,128]{1,0:T(1,128)S(1)} %bitcast.12, bf16[3,16,768]{2,1,0:T(8,128)(2,1)S(1)} %get-tuple-element.13.own_ref, bf16[3,16,768]{2,1,0:T(8,128)(2,1)S(1)} %collective-permute-done.other_ref, ...), custom_call_target="tpu_custom_call" | custom-call | flops 805306368 | bytes 3145728 | tf_op jit(solution)/shard_map/norm_and_row_dft/pallas_call | solution.py:235
  12.4 0.0 copy-start.3
  12.4 0.0 copy-start.4
  12.4 0.0 copy-start.5
  12.4 0.0 copy-start.6
  12.4 0.0 copy-start.7
  12.4 0.0 copy-start.8
  12.5 0.0 copy-start.9
  12.5 41.8 %all_to_all.10 = bf16[128,32,256]{2,1,0:T(8,128)(2,1)S(1)} all-to-all(bf16[128,32,256]{2,1,0:T(8,128)(2,1)S(1)} %bitcast.7), channel_id=1, replica_groups=mesh['row'=64,'blk'=2] {'blk','row'}, dimensions={0} | all-to-all | bytes 4194304 | tf_op jit(solution)/shard_map/all_to_all | solution.py:455
  54.3 0.0 copy-done.4
  54.3 3.3 %column_filter.1 = bf16[2,64,32,256]{3,2,1,0:T(8,128)(2,1)S(1)} custom-call(bf16[2,64,32,256]{3,2,1,0:T(8,128)(2,1)S(1)} %bitcast.9, bf16[528,1024]{1,0:T(8,128)(2,1)S(1)} %copy-done.7, bf16[1024,512]{1,0:T(8,128)(2,1)S(1)} %copy-done.8, bf16[32,128]{1,0:T(8,128)(2,1)S(1)} %copy-done.9, bf16[2,256,32]{2,1,0:T(8,128)(2,1)S(1)} %bitcast.13, ...), custom_call_target="tpu_custom_call" | custom-call | flops 3221225472 | bytes 8388608 | tf_op jit(solution)/shard_map/column_filter/pallas_call | solution.py:365
  57.6 0.0 copy-start.1
  57.6 34.4 %all_to_all.11 = bf16[128,32,256]{2,1,0:T(8,128)(2,1)S(1)} all-to-all(bf16[128,32,256]{2,1,0:T(8,128)(2,1)S(1)} %bitcast.10), channel_id=1, replica_groups=mesh['row'=64,'blk'=2] {'blk','row'}, dimensions={0} | all-to-all | bytes 4194304 | tf_op jit(solution)/shard_map/all_to_all | solution.py:455
  92.0 4.4 %inverse_row_dft.1 = bf16[2,128,16,1024]{3,2,1,0:T(8,128)(2,1)} custom-call(bf16[2,64,32,256]{3,2,1,0:T(8,128)(2,1)S(1)} %bitcast.8, bf16[256,1024]{1,0:T(8,128)(2,1)S(1)} %copy-done.1), custom_call_target="tpu_custom_call" | custom-call | flops 2147483648 | bytes 8388608 | tf_op jit(solution)/shard_map/inverse_row_dft/pallas_call | solution.py:431
  (8 shorter events, 0.0 us)
Async XLA Ops:
  2.8 4.4 %copy-start = (bf16[1024,256]{1,0:T(8,128)(2,1)S(1)}, bf16[1024,256]{1,0:T(8,128)(2,1)}, u32[]{:S(2)}) copy-start(bf16[1024,256]{1,0:T(8,128)(2,1)} %constant.11.clone.table_ref) | copy-start | bytes 1572868
  2.8 4.4 %copy-start.2 = (f32[128]{0:T(128)S(1)}, f32[128]{0:T(128)}, u32[]{:S(2)}) copy-start(f32[128]{0:T(128)} %param.12) | copy-start | bytes 1540
  2.8 4.4 %collective-permute-start.1 = (bf16[3,16,1280]{2,1,0:T(8,128)(2,1)S(1)}, bf16[3,16,1280]{2,1,0:T(8,128)(2,1)S(1)}, u32[]{:S(2)}, u32[]{:S(2)}) collective-permute-start(bf16[3,16,1280]{2,1,0:T(8,128)(2,1)S(1)} %get-tuple-element.16.own_ref), channel_id=1, source_target_pairs={{0,1},{1,0},{2,3},{3,2},{4,5},{5,4},{6,7},{7,6},{8,9},{9,8},{10,11... | collective-permute-start | bytes 368648 | tf_op jit(solution)/shard_map/ppermute | solution.py:472
  7.1 3.3 %collective-permute-start = (bf16[3,16,768]{2,1,0:T(8,128)(2,1)S(1)}, bf16[3,16,768]{2,1,0:T(8,128)(2,1)S(1)}, u32[]{:S(2)}, u32[]{:S(2)}) collective-permute-start(bf16[3,16,768]{2,1,0:T(8,128)(2,1)S(1)} %get-tuple-element.13.own_ref), channel_id=1, source_target_pairs={{0,1},{1,0},{2,3},{3,2},{4,5},{5,4},{6,7},{7,6},{8,9},{9,8},{10,11... | collective-permute-start | bytes 221192 | tf_op jit(solution)/shard_map/ppermute | solution.py:473
  12.4 41.9 %copy-start.3 = (bf16[2,8,32,32]{3,2,1,0:T(8,128)(2,1)S(1)}, bf16[2,8,32,32]{3,2,1,0:T(8,128)(2,1)}, u32[]{:S(2)}) copy-start(bf16[2,8,32,32]{3,2,1,0:T(8,128)(2,1)} %param.13) | copy-start | bytes 98308
  12.4 41.9 %copy-start.4 = (bf16[2,8,32,32]{3,2,1,0:T(8,128)(2,1)S(1)}, bf16[2,8,32,32]{3,2,1,0:T(8,128)(2,1)}, u32[]{:S(2)}) copy-start(bf16[2,8,32,32]{3,2,1,0:T(8,128)(2,1)} %param.15) | copy-start | bytes 98308
  12.4 41.9 %copy-start.5 = (f32[2,256]{1,0:T(2,128)S(1)}, f32[2,256]{1,0:T(2,128)}, u32[]{:S(2)}) copy-start(f32[2,256]{1,0:T(2,128)} %b1_ref.1) | copy-start | bytes 6148
  12.4 41.9 %copy-start.6 = (f32[2,256]{1,0:T(2,128)S(1)}, f32[2,256]{1,0:T(2,128)}, u32[]{:S(2)}) copy-start(f32[2,256]{1,0:T(2,128)} %b2_ref.1) | copy-start | bytes 6148
  12.4 41.9 %copy-start.7 = (bf16[528,1024]{1,0:T(8,128)(2,1)S(1)}, bf16[528,1024]{1,0:T(8,128)(2,1)}, u32[]{:S(2)}) copy-start(bf16[528,1024]{1,0:T(8,128)(2,1)} %constant.12.clone.fwd_ref) | copy-start | bytes 3244036
  12.4 41.9 %copy-start.8 = (bf16[1024,512]{1,0:T(8,128)(2,1)S(1)}, bf16[1024,512]{1,0:T(8,128)(2,1)}, u32[]{:S(2)}) copy-start(bf16[1024,512]{1,0:T(8,128)(2,1)} %constant.13.clone.inv_ref) | copy-start | bytes 3145732
  12.5 41.9 %copy-start.9 = (bf16[32,128]{1,0:T(8,128)(2,1)S(1)}, bf16[32,128]{1,0:T(8,128)(2,1)}, u32[]{:S(2)}) copy-start(bf16[32,128]{1,0:T(8,128)(2,1)} %constant.10.clone.spread_ref) | copy-start | bytes 24580
  57.6 34.4 %copy-start.1 = (bf16[256,1024]{1,0:T(8,128)(2,1)S(1)}, bf16[256,1024]{1,0:T(8,128)(2,1)}, u32[]{:S(2)}) copy-start(bf16[256,1024]{1,0:T(8,128)(2,1)} %constant.14.clone.table_ref) | copy-start | bytes 1572868

commit v8 on v7

--- a/solution.py
+++ b/solution.py
@@ -415,7 +415,7 @@
                 copies.append(
                     pltpu.make_async_copy(done_s.at[which, block], out_ref.at[which, block], sems.at[len(copies)])
                 )
-                copies[-1].start()
+                copies[-1].start(priority=len(copies) % 2)
     for copy in copies:
         copy.wait()
 

time: 96.8 us -> 96.8 us (level)
  no operation moved by 1% of the time
where the time goes in v8:
time: 96.8 us; the launch traced here: 96.6 us
  blocking collectives  76.2 us (79%)
  Pallas kernels  17.2 us (18%)
  starting transfers between devices  2.27 us (2%)
    all_to_all x2, blocking collectives, exchange(): lax.all_to_all(flat, ('blk', 'row'), split_axis=0, concat_axis=0, tiled=T...  76.2 us
    pallas_call x2, Pallas kernels, channel_stats(): pl.pallas_call(functools.partial(stats_kernel, segments), in_specs=[pl.Bl...  4.89 us
    pallas_call x2, Pallas kernels, forward_rows(): pl.pallas_call(functools.partial(kernel, pitch), in_specs=[vmem] * (len(h...  4.54 us
    pallas_call x1, Pallas kernels, inverse_rows(): pl.pallas_call(functools.partial(inverse_kernel, chan_block, pitch), in_s...  4.44 us
    pallas_call x1, Pallas kernels, filter_columns(): pl.pallas_call(filter_kernel, in_specs=[vmem] * 8, out_specs=vmem, out_sh...  3.29 us
    ppermute x1, starting transfers between devices, local(): other_first = lax.ppermute(own_first, 'blk', swap)  2.12 us
  transfers between devices with their start and end apart: 2, of which 1 were waited for; matrix products, arithmetic and copies ran while one was open for 0% of the time, Pallas kernels for 5%

profile of v8, /device:TPU:1, one launch (start us, length us, event | category | flops | bytes accessed | tf_op | source)
XLA Modules:
  0.0 96.6 jit_solution(16410631979809325274)
XLA Ops:
  0.0 2.8 %channel_stats.3 = (bf16[128,16,1024]{2,1,0:T(8,128)(2,1)S(1)}, bf16[128,16,256]{2,1,0:T(8,128)(2,1)S(1)}, bf16[3,16,1280]{2,1,0:T(8,128)(2,1)S(1)}) custom-call(bf16[2,128,16,1024]{3,2,1,0:T(8,128)(2,1)} %x_ref.3), custom_call_target="tpu_custom_call" | custom-call | flops 13107200 | bytes 5242880 | tf_op jit(solution)/shard_map/channel_stats/pallas_call | solution.py:132
  2.8 0.0 copy-start
  2.8 0.0 copy-start.2
  2.8 2.1 %collective-permute-start.1 = (bf16[3,16,1280]{2,1,0:T(8,128)(2,1)S(1)}, bf16[3,16,1280]{2,1,0:T(8,128)(2,1)S(1)}, u32[]{:S(2)}, u32[]{:S(2)}) collective-permute-start(bf16[3,16,1280]{2,1,0:T(8,128)(2,1)S(1)} %get-tuple-element.16.own_ref), channel_id=1, source_target_pairs={{0,1},{1,0},{2,3},{3,2},{4,5},{5,4},{6,7},{7,6},{8,9},{9,8},{10,11... | collective-permute-start | bytes 368648 | tf_op jit(solution)/shard_map/ppermute | solution.py:472
  5.0 2.1 %channel_stats.2 = (bf16[128,16,768]{2,1,0:T(8,128)(2,1)S(1)}, bf16[3,16,768]{2,1,0:T(8,128)(2,1)S(1)}) custom-call(bf16[2,128,16,1024]{3,2,1,0:T(8,128)(2,1)} %x_ref.3), custom_call_target="tpu_custom_call" | custom-call | flops 7864320 | bytes 3145728 | tf_op jit(solution)/shard_map/channel_stats/pallas_call | solution.py:132
  7.1 0.2 collective-permute-start
  7.2 0.0 collective-permute-done.1.other_ref
  7.2 0.0 copy-done.2
  7.2 2.5 %norm_and_row_dft.2 = (bf16[64,32,256]{2,1,0:T(8,128)(2,1)S(1)}, f32[2,3096,128]{2,1,0:T(8,128)S(1)}) custom-call(bf16[128,16,1024]{2,1,0:T(8,128)(2,1)S(1)} %get-tuple-element.14.x_ref, bf16[128,16,256]{2,1,0:T(8,128)(2,1)S(1)} %get-tuple-element.15.early_ref, f32[1,128]{1,0:T(1,128)S(1)} %bitcast.11, bf16[3,16,1280]{2,1,0:T(8,128)(2,1)S(1)} %get-tuple-element.16.own_ref, ...), custom_call_target="tpu_custom_call" | custom-call | flops 1342177280 | bytes 5242880 | tf_op jit(solution)/shard_map/norm_and_row_dft/pallas_call | solution.py:235
  9.8 0.6 collective-permute-done.other_ref
  10.3 2.0 %norm_and_row_dft.3 = bf16[2,64,32,256]{3,2,1,0:T(8,128)(2,1)S(1)} custom-call(bf16[128,16,768]{2,1,0:T(8,128)(2,1)S(1)} %get-tuple-element.12.x_ref, f32[1,128]{1,0:T(1,128)S(1)} %bitcast.12, bf16[3,16,768]{2,1,0:T(8,128)(2,1)S(1)} %get-tuple-element.13.own_ref, bf16[3,16,768]{2,1,0:T(8,128)(2,1)S(1)} %collective-permute-done.other_ref, ...), custom_call_target="tpu_custom_call" | custom-call | flops 805306368 | bytes 3145728 | tf_op jit(solution)/shard_map/norm_and_row_dft/pallas_call | solution.py:235
  12.4 0.0 copy-start.3
  12.4 0.0 copy-start.4
  12.4 0.0 copy-start.5
  12.4 0.0 copy-start.6
  12.4 0.0 copy-start.7
  12.4 0.0 copy-start.8
  12.5 0.0 copy-start.9
  12.5 41.8 %all_to_all.10 = bf16[128,32,256]{2,1,0:T(8,128)(2,1)S(1)} all-to-all(bf16[128,32,256]{2,1,0:T(8,128)(2,1)S(1)} %bitcast.7), channel_id=1, replica_groups=mesh['row'=64,'blk'=2] {'blk','row'}, dimensions={0} | all-to-all | bytes 4194304 | tf_op jit(solution)/shard_map/all_to_all | solution.py:455
  54.3 0.0 copy-done.4
  54.3 3.3 %column_filter.1 = bf16[2,64,32,256]{3,2,1,0:T(8,128)(2,1)S(1)} custom-call(bf16[2,64,32,256]{3,2,1,0:T(8,128)(2,1)S(1)} %bitcast.9, bf16[528,1024]{1,0:T(8,128)(2,1)S(1)} %copy-done.7, bf16[1024,512]{1,0:T(8,128)(2,1)S(1)} %copy-done.8, bf16[32,128]{1,0:T(8,128)(2,1)S(1)} %copy-done.9, bf16[2,256,32]{2,1,0:T(8,128)(2,1)S(1)} %bitcast.13, ...), custom_call_target="tpu_custom_call" | custom-call | flops 3221225472 | bytes 8388608 | tf_op jit(solution)/shard_map/column_filter/pallas_call | solution.py:365
  57.6 0.0 copy-start.1
  57.6 34.4 %all_to_all.11 = bf16[128,32,256]{2,1,0:T(8,128)(2,1)S(1)} all-to-all(bf16[128,32,256]{2,1,0:T(8,128)(2,1)S(1)} %bitcast.10), channel_id=1, replica_groups=mesh['row'=64,'blk'=2] {'blk','row'}, dimensions={0} | all-to-all | bytes 4194304 | tf_op jit(solution)/shard_map/all_to_all | solution.py:455
  92.0 4.4 %inverse_row_dft.1 = bf16[2,128,16,1024]{3,2,1,0:T(8,128)(2,1)} custom-call(bf16[2,64,32,256]{3,2,1,0:T(8,128)(2,1)S(1)} %bitcast.8, bf16[256,1024]{1,0:T(8,128)(2,1)S(1)} %copy-done.1), custom_call_target="tpu_custom_call" | custom-call | flops 2147483648 | bytes 8388608 | tf_op jit(solution)/shard_map/inverse_row_dft/pallas_call | solution.py:431
  (8 shorter events, 0.0 us)
Async XLA Ops:
  2.8 4.4 %copy-start = (bf16[1024,256]{1,0:T(8,128)(2,1)S(1)}, bf16[1024,256]{1,0:T(8,128)(2,1)}, u32[]{:S(2)}) copy-start(bf16[1024,256]{1,0:T(8,128)(2,1)} %constant.11.clone.table_ref) | copy-start | bytes 1572868
  2.8 4.4 %copy-start.2 = (f32[128]{0:T(128)S(1)}, f32[128]{0:T(128)}, u32[]{:S(2)}) copy-start(f32[128]{0:T(128)} %param.12) | copy-start | bytes 1540
  2.8 4.4 %collective-permute-start.1 = (bf16[3,16,1280]{2,1,0:T(8,128)(2,1)S(1)}, bf16[3,16,1280]{2,1,0:T(8,128)(2,1)S(1)}, u32[]{:S(2)}, u32[]{:S(2)}) collective-permute-start(bf16[3,16,1280]{2,1,0:T(8,128)(2,1)S(1)} %get-tuple-element.16.own_ref), channel_id=1, source_target_pairs={{0,1},{1,0},{2,3},{3,2},{4,5},{5,4},{6,7},{7,6},{8,9},{9,8},{10,11... | collective-permute-start | bytes 368648 | tf_op jit(solution)/shard_map/ppermute | solution.py:472
  7.1 3.3 %collective-permute-start = (bf16[3,16,768]{2,1,0:T(8,128)(2,1)S(1)}, bf16[3,16,768]{2,1,0:T(8,128)(2,1)S(1)}, u32[]{:S(2)}, u32[]{:S(2)}) collective-permute-start(bf16[3,16,768]{2,1,0:T(8,128)(2,1)S(1)} %get-tuple-element.13.own_ref), channel_id=1, source_target_pairs={{0,1},{1,0},{2,3},{3,2},{4,5},{5,4},{6,7},{7,6},{8,9},{9,8},{10,11... | collective-permute-start | bytes 221192 | tf_op jit(solution)/shard_map/ppermute | solution.py:473
  12.4 41.9 %copy-start.3 = (bf16[2,8,32,32]{3,2,1,0:T(8,128)(2,1)S(1)}, bf16[2,8,32,32]{3,2,1,0:T(8,128)(2,1)}, u32[]{:S(2)}) copy-start(bf16[2,8,32,32]{3,2,1,0:T(8,128)(2,1)} %param.13) | copy-start | bytes 98308
  12.4 41.9 %copy-start.4 = (bf16[2,8,32,32]{3,2,1,0:T(8,128)(2,1)S(1)}, bf16[2,8,32,32]{3,2,1,0:T(8,128)(2,1)}, u32[]{:S(2)}) copy-start(bf16[2,8,32,32]{3,2,1,0:T(8,128)(2,1)} %param.15) | copy-start | bytes 98308
  12.4 41.9 %copy-start.5 = (f32[2,256]{1,0:T(2,128)S(1)}, f32[2,256]{1,0:T(2,128)}, u32[]{:S(2)}) copy-start(f32[2,256]{1,0:T(2,128)} %b1_ref.1) | copy-start | bytes 6148
  12.4 41.9 %copy-start.6 = (f32[2,256]{1,0:T(2,128)S(1)}, f32[2,256]{1,0:T(2,128)}, u32[]{:S(2)}) copy-start(f32[2,256]{1,0:T(2,128)} %b2_ref.1) | copy-start | bytes 6148
  12.4 41.9 %copy-start.7 = (bf16[528,1024]{1,0:T(8,128)(2,1)S(1)}, bf16[528,1024]{1,0:T(8,128)(2,1)}, u32[]{:S(2)}) copy-start(bf16[528,1024]{1,0:T(8,128)(2,1)} %constant.12.clone.fwd_ref) | copy-start | bytes 3244036
  12.4 41.9 %copy-start.8 = (bf16[1024,512]{1,0:T(8,128)(2,1)S(1)}, bf16[1024,512]{1,0:T(8,128)(2,1)}, u32[]{:S(2)}) copy-start(bf16[1024,512]{1,0:T(8,128)(2,1)} %constant.13.clone.inv_ref) | copy-start | bytes 3145732
  12.5 41.9 %copy-start.9 = (bf16[32,128]{1,0:T(8,128)(2,1)S(1)}, bf16[32,128]{1,0:T(8,128)(2,1)}, u32[]{:S(2)}) copy-start(bf16[32,128]{1,0:T(8,128)(2,1)} %constant.10.clone.spread_ref) | copy-start | bytes 24580
  57.6 34.4 %copy-start.1 = (bf16[256,1024]{1,0:T(8,128)(2,1)S(1)}, bf16[256,1024]{1,0:T(8,128)(2,1)}, u32[]{:S(2)}) copy-start(bf16[256,1024]{1,0:T(8,128)(2,1)} %constant.14.clone.table_ref) | copy-start | bytes 1572868
